TPU v7x, 256 devices: a whole 4x4x8 slice. The times are simulated.
256 devices in a mesh: pb: 8 (over z_lo, core), pa: 32 (over y, x, z_hi).
Axes of the slice: x: 4, y: 4, z: 8 (z_hi: 2, z_lo: 4; z = z_hi * 4 + z_lo), core: 2. Of those that a mesh axis runs over, the one named last changes fastest.
Arguments:
- queries: bfloat16 [20480, 768], P(('pb', 'pa')), may hold values from -8 to 8
- passages: bfloat16 [20480, 768], P(('pb', 'pa')), may hold values from -8 to 8
- positives: int32 [20480], P('pb'), may hold values from 0 to 20479, each once
- inv_temp: float32 [], replicated, may hold values from 80 to 320
Outputs:
- query_loss: float32 [20480], P(('pb', 'pa'))
- query_grads: bfloat16 [20480, 768], P(('pb', 'pa'))
- passage_grads: bfloat16 [20480, 768], P(('pb', 'pa'))
Inputs may be any that keep to these rules, and one draw needn't show every extreme that they name: `positives`: each passage is the positive of exactly one query.
All inputs are finite; a program needn't handle non-finite values.
Results may differ from a plain program's by a relative error of at most 0.02.
Values may be sent and summed in bfloat16 or wider, within the bound.
No kernel may reach another device: no remote copies, remote signals or barrier semaphores. Data moves between devices by JAX's collectives and lax.ppermute only.
A program may use at most 64 MiB of HBM per device.

v0:
```python
import math

import jax
import jax.numpy as jnp
from jax import lax
from jax.sharding import PartitionSpec as P


def unit_rows(values):
    wide = values.astype(jnp.float32)
    length = jnp.sqrt(jnp.sum(wide * wide, axis=1, keepdims=True))
    return (wide / length, length)


def unit_back(unit, length, grad):
    along = jnp.sum(unit * grad, axis=1, keepdims=True)
    return ((grad - unit * along) / length).astype(jnp.bfloat16)


def similar(rows, column_rows, inv_temp):
    product = lax.dot_general(
        rows, column_rows, (((1,), (1,)), ((), ())), preferred_element_type=jnp.float32
    )
    return product * inv_temp


def make_delta(rows, totals, targets, column_rows, inv_temp):
    logits = similar(rows, column_rows, inv_temp)
    cols = lax.broadcasted_iota(jnp.int32, logits.shape, 1)
    hit = cols == targets[:, None]
    return (jnp.exp(logits - totals[:, None]) - jnp.where(hit, 1.0, 0.0)).astype(jnp.bfloat16)


def local(queries, passages, positives, inv_temp):
    tok_rows = queries.shape[0]
    width = queries.shape[1]
    query_unit, query_len = unit_rows(queries)
    passage_unit, passage_len = unit_rows(passages)
    query_low = query_unit.astype(jnp.bfloat16)
    passage_low = passage_unit.astype(jnp.bfloat16)
    query_block = lax.all_gather(query_low, "pa", axis=0, tiled=True)
    passage_block = lax.all_gather(passage_low, "pb", axis=0, tiled=True)
    row_count = query_block.shape[0]
    here = lax.axis_index("pa")
    span = lax.axis_size("pa")
    shard = positives // tok_rows
    owner = shard % span
    target = jnp.where(owner == here, shard // span * tok_rows + positives % tok_rows, -1)
    block = math.gcd(row_count, 1024)
    count_blocks = row_count // block
    query_tiles = query_block.reshape(count_blocks, block, width)
    target_tiles = target.reshape(count_blocks, block)

    def block_stats(inputs):
        rows, targets = inputs
        logits = similar(rows, passage_block, inv_temp)
        biggest = jnp.max(logits, axis=1)
        expsum = jnp.sum(jnp.exp(logits - biggest[:, None]), axis=1)
        cols = lax.broadcasted_iota(jnp.int32, logits.shape, 1)
        positive = jnp.sum(jnp.where(cols == targets[:, None], logits, 0.0), axis=1)
        return (biggest, expsum, positive)

    biggest, expsum, positive = lax.map(block_stats, (query_tiles, target_tiles))
    biggest = biggest.reshape(row_count)
    expsum = expsum.reshape(row_count)
    positive = positive.reshape(row_count)
    top = lax.pmax(biggest, "pa")
    summed, positive_all = lax.psum((expsum * jnp.exp(biggest - top), positive), "pa")
    totals = top + jnp.log(summed)
    losses = totals - positive_all
    query_loss = lax.dynamic_slice_in_dim(losses, here * tok_rows, tok_rows, 0)
    col_count = passage_block.shape[0]

    def tile_delta(inputs):
        rows, part_totals, part_targets = inputs
        return make_delta(rows, part_totals, part_targets, passage_block, inv_temp)

    stored = lax.map(tile_delta, (query_tiles, totals.reshape(count_blocks, block), target_tiles))
    stored = stored.reshape(row_count, col_count)
    delta = stored
    unit_qgrad = lax.psum_scatter(
        (inv_temp * jnp.dot(delta, passage_block, preferred_element_type=jnp.float32)).astype(
            jnp.bfloat16
        ),
        "pa",
        scatter_dimension=0,
        tiled=True,
    ).astype(jnp.float32)
    delta = stored
    update = lax.dot_general(
        delta, query_block, (((0,), (0,)), ((), ())), preferred_element_type=jnp.float32
    )
    unit_pgrad = lax.psum_scatter(
        (inv_temp * update).astype(jnp.bfloat16), "pb", scatter_dimension=0, tiled=True
    ).astype(jnp.float32)
    query_grads = unit_back(query_unit, query_len, unit_qgrad)
    passage_grads = unit_back(passage_unit, passage_len, unit_pgrad)
    return (query_loss, query_grads, passage_grads)


def solution(mesh):
    return jax.shard_map(
        local,
        mesh=mesh,
        in_specs=(P(("pb", "pa"), None), P(("pb", "pa"), None), P("pb"), P()),
        out_specs=(P(("pb", "pa")), P(("pb", "pa"), None), P(("pb", "pa"), None)),
        check_vma=False,
    )
```

profile of v0, /device:TPU:1, one launch (start us, length us, event | category | flops | bytes accessed | tf_op | source)
XLA Modules:
  0.0 905.3 jit_solution(8094734569449493520)
XLA Ops:
  7.2 1.0 fusion.12
  8.3 1.7 fusion.27
  10.7 1.0 fusion.13
  11.7 0.7 fusion.23
  12.5 1.0 fusion.28
  13.5 18.8 %all_gather.7 = bf16[640,768]{1,0:T(8,128)(2,1)S(1)} all-gather(bf16[80,768]{1,0:T(8,128)(2,1)S(1)} %fusion.28), channel_id=1, replica_groups=mesh['pb'=8,'pa'=32] {'pb'}, dimensions={0}, use_global_device_ids=true | all-gather | bytes 1105920 | tf_op jit(solution)/shard_map/all_gather | solution.py:42
  32.3 91.3 %all-gather.2.cloned.1.call-done = bf16[2560,768]{1,0:T(8,128)(2,1)} async-done(((bf16[80,768]{1,0:T(8,128)(2,1)}), bf16[2560,768]{1,0:T(8,128)(2,1)}) %all-gather.2.cloned.1.call-update) | async-done | bytes 3932176 | tf_op jit(solution)/shard_map/all_gather | solution.py:41
  123.6 17.4 %while.24 = (s32[]{:T(128)}, f32[5,512]{1,0:T(8,128)S(1)}, f32[5,512]{1,0:T(8,128)S(1)}, f32[5,512]{1,0:T(8,128)S(1)}, bf16[5,512,768]{2,1,0:T(8,128)(2,1)}, /*i...) while((s32[]{:T(128)}, f32[5,512]{1,0:T(8,128)S(1)}, ...), condition=%wide.region_6.7_spmd, body=%wide.region_2.6_spmd.sunk | while | flops 505608704 | bytes 4418177 | solution.py:63
  123.6 2.7 fusion.42
  126.2 0.6 select_reduce_fusion.2
  126.8 0.1 dynamic_update_slice.19
  126.9 0.1 dynamic_update_slice.21
  126.9 0.1 dynamic_update_slice.20
  127.0 2.7 fusion.42
  129.7 0.6 select_reduce_fusion.2
  130.3 0.1 dynamic_update_slice.19
  130.4 0.1 dynamic_update_slice.21
  130.4 0.1 dynamic_update_slice.20
  130.5 2.7 fusion.42
  133.2 0.6 select_reduce_fusion.2
  133.8 0.1 dynamic_update_slice.19
  133.8 0.1 dynamic_update_slice.21
  133.9 0.1 dynamic_update_slice.20
  134.0 2.7 fusion.42
  136.7 0.6 select_reduce_fusion.2
  137.3 0.1 dynamic_update_slice.19
  137.3 0.1 dynamic_update_slice.21
  137.4 0.1 dynamic_update_slice.20
  137.5 2.7 fusion.42
  140.2 0.6 select_reduce_fusion.2
  140.7 0.1 dynamic_update_slice.19
  141.0 187.6 %pmax.7 = f32[2560]{0:T(1024)S(1)} all-reduce(f32[2560]{0:T(1024)S(1)} %reshape.46), channel_id=1, replica_groups=mesh['pb'=8,'pa'=32] {'pa'}, use_global_device_ids=true, to_apply=%region_7.8 | all-reduce | flops 2560 | bytes 20480 | tf_op jit(solution)/shard_map/pmax | solution.py:67
  328.6 189.7 %all-reduce = (f32[2560]{0:T(1024)S(1)}, f32[2560]{0:T(1024)S(1)}) all-reduce(f32[2560]{0:T(1024)S(1)} %reshape.48, f32[2560]{0:T(1024)S(1)} %exponential_multiply_fusion), channel_id=1, replica_groups=mesh['pb'=8,'pa'=32] {'pa'}, use_global_device_ids=true, to_apply=%region_9.10 | all-reduce | flops 5120 | bytes 40960 | tf_op jit(solution)/shard_map/psum | solution.py:68
  518.3 17.6 %while.25 = (s32[]{:T(128)}, bf16[5,512,640]{2,1,0:T(8,128)(2,1)}, bf16[5,512,768]{2,1,0:T(8,128)(2,1)}, bf16[640,768]{1,0:T(8,128)(2,1)S(1)}, f32[]{:T(128)}, /...) while((s32[]{:T(128)}, bf16[5,512,640]{2,1,0:T(8,128)(2,1)}, bf16[5,512,768]{2,1,0:T(8,128)(2,1)}, ...), condition=%wide.region_11.12_spmd, body=%wide.region_10.11_spmd.sunk | while | flops 505282560 | bytes 2438757 | solution.py:78
  518.4 3.5 fusion.45
  521.9 3.5 fusion.45
  525.4 3.5 fusion.45
  528.9 3.5 fusion.45
  532.4 3.5 fusion.45
  535.9 6.8 multiply_convert_fusion.1
  542.8 7.1 multiply_convert_fusion
  549.9 0.6 dynamic-slice_subtract_fusion
  550.5 77.1 %reduce-scatter.5.cloned.1.call-done = bf16[80,768]{1,0:T(8,128)(2,1)} async-done(((bf16[640,768]{1,0:T(8,128)(2,1)}), bf16[80,768]{1,0:T(8,128)(2,1)}) %reduce-scatter.5.cloned.1.call-update) | async-done | bytes 122896 | tf_op jit(solution)/shard_map/reduce_scatter | solution.py:93
  627.6 1.1 fusion.17
  628.7 1.7 fusion.19
  630.4 265.5 %reduce-scatter.3.cloned.1.call-done = bf16[80,768]{1,0:T(8,128)(2,1)} async-done(((bf16[2560,768]{1,0:T(8,128)(2,1)}), bf16[80,768]{1,0:T(8,128)(2,1)}) %reduce-scatter.3.cloned.1.call-update) | async-done | bytes 122896 | tf_op jit(solution)/shard_map/reduce_scatter | solution.py:81
  895.9 1.1 fusion.14
  897.1 1.7 fusion.16
  (40 shorter events, 0.5 us)
Async XLA Ops:
  7.2 116.4 %all-gather.2.cloned.1.call-start = ((), (), s32[]{:S(2)}) async-start(), calls=%async_computation.2 | async-start | bytes 4055040 | tf_op jit(solution)/shard_map/all_gather | solution.py:41
  9.9 617.7 %reduce-scatter.5.cloned.1.call-start = ((), (), s32[]{:S(2)}) async-start(), calls=%async_computation.4 | async-start | bytes 1105920 | tf_op jit(solution)/shard_map/reduce_scatter | solution.py:93
  542.8 353.1 %reduce-scatter.3.cloned.1.call-start = ((), (), s32[]{:S(2)}) async-start(), calls=%async_computation.3 | async-start | bytes 4055040 | tf_op jit(solution)/shard_map/reduce_scatter | solution.py:81
  549.9 77.7 %copy-start = (bf16[80,768]{1,0:T(8,128)(2,1)S(1)}, bf16[80,768]{1,0:T(8,128)(2,1)}, u32[]{:S(2)}) copy-start(bf16[80,768]{1,0:T(8,128)(2,1)} %param.9) | copy-start | bytes 368644
  549.9 346.0 %copy-start.1 = (bf16[80,768]{1,0:T(8,128)(2,1)S(1)}, bf16[80,768]{1,0:T(8,128)(2,1)}, u32[]{:S(2)}) copy-start(bf16[80,768]{1,0:T(8,128)(2,1)} %param.8) | copy-start | bytes 368644
Sparse Core Ops, SparseCore 0:
  12.1 111.4 all-gather.1
  542.9 84.6 reduce-scatter.4
  634.0 261.8 reduce-scatter.2
where the time goes:
time: 907 us; the launch traced here: 905 us
  waiting for transfers between devices  434 us (48%)
  blocking collectives  396 us (44%)
  matrix products  44.8 us (5%)
  other arithmetic  14.5 us (2%)
  between operations  14.5 us (2%)
    reduce_scatter x1, waiting for transfers between devices, local(): lax.psum_scatter((inv_temp * jnp.dot(delta, passage_block, preferred_elem...  266 us
    psum x1, blocking collectives, local(): lax.psum((expsum * jnp.exp(biggest - top), positive), 'pa')  190 us
    pmax x1, blocking collectives, local(): top = lax.pmax(biggest, 'pa')  188 us
    all_gather x1, waiting for transfers between devices, local(): query_block = lax.all_gather(query_low, 'pa', axis=0, tiled=True)  91.3 us
    reduce_scatter x1, waiting for transfers between devices, local(): lax.psum_scatter((inv_temp * update).astype(jnp.bfloat16), 'pb', scatter_...  77.1 us
    dot_general x10, matrix products, similar(): lax.dot_general(rows, column_rows, (((1,), (1,)), ((), ())), preferred_el...  30.9 us
    all_gather x1, blocking collectives, local(): passage_block = lax.all_gather(passage_low, 'pb', axis=0, tiled=True)  18.8 us
  transfers between devices with their start and end apart: 3, of which 3 were waited for; matrix products, arithmetic and copies ran while one was open for 1% of the time, Pallas kernels for 0%

commit v1 on v0

v1 whole, which is shorter than its diff:
```python
import functools

import jax
import jax.numpy as jnp
from jax import lax
from jax.experimental import pallas as pl
from jax.experimental.pallas import tpu as pltpu
from jax.sharding import Mesh
from jax.sharding import PartitionSpec as P

AXES = ("zl", "core", "y", "x", "zh")
SIZES = (4, 2, 4, 4, 2)
VMEM_LIMIT = 50 * 2**20
F32 = jnp.float32
BF16 = jnp.bfloat16


def device_at(z, core, y, x):
    z, y, x = z % 8, y % 4, x % 4
    return ((((z % 4) * 2 + core) * 4 + y) * 4 + x) * 2 + z // 4


def fetch(array, source):
    pairs = []
    for z in range(8):
        for core in range(2):
            for y in range(4):
                for x in range(4):
                    pairs.append((device_at(*source(z, core, y, x)), device_at(z, core, y, x)))
    return lax.ppermute(array, AXES, pairs)


def swap(array):
    return fetch(array, lambda z, c, y, x: (z, 1 - c, y, x))


def along_z(array, k):
    return fetch(array, lambda z, c, y, x: (z + (k if c == 0 else -k), c, y, x))


def inner(array, k):
    return fetch(array, lambda z, c, y, x: (z, c, y, x + k) if c == 0 else (z, c, y + k, x))


def outer(array, k):
    return fetch(array, lambda z, c, y, x: (z, c, y + k, x) if c == 0 else (z, c, y, x + k))


def norm_kernel(q_ref, p_ref, q_low, p_low):
    for src, dst in ((q_ref, q_low), (p_ref, p_low)):
        wide = src[...].astype(F32)
        length = jnp.sqrt(jnp.sum(wide * wide, axis=1, keepdims=True))
        dst[...] = (wide / length).astype(BF16)


def stats_kernel(rows, tile, offs, temp, target, *refs):
    q_parts, p_parts = refs[:4], refs[4:13]
    e_out, stat, pos_out, q_all, p_all, logits, sems = refs[13:]
    count = rows * 16
    copies = []
    for k, part in enumerate(q_parts):
        for b in range(4):
            copies.append(
                pltpu.make_async_copy(
                    part.at[pl.ds(b * rows, rows)],
                    q_all.at[pl.ds(pl.multiple_of(offs[4 * k + b], 16), rows)],
                    sems.at[len(copies)],
                )
            )
    at = 0
    for part in p_parts:
        size = part.shape[0]
        copies.append(
            pltpu.make_async_copy(part, p_all.at[pl.ds(at, size)], sems.at[len(copies)])
        )
        at += size
    for copy in copies:
        copy.start()
    for copy in copies:
        copy.wait()
    scale = temp[0]
    for t in range(count // tile):
        cols = slice(t * tile, (t + 1) * tile)
        logits[...] = scale * lax.dot_general(
            p_all[...], q_all[cols, :], (((1,), (1,)), ((), ())), preferred_element_type=F32
        )
        values = logits[...]
        top = jnp.max(values, axis=0, keepdims=True)
        hit = lax.broadcasted_iota(jnp.int32, values.shape, 0) == target[:, cols]
        positive = jnp.sum(jnp.where(hit, values, 0.0), axis=0, keepdims=True)
        e = jnp.exp(values - top)
        e_out[:, cols] = e.astype(BF16)
        total = jnp.sum(e, axis=0, keepdims=True)
        stat[:, cols] = jnp.broadcast_to(top, (16, tile))
        stat[:, t * tile + count : (t + 1) * tile + count] = jnp.broadcast_to(total, (16, tile))
        pos_out[:, cols] = positive
    for j in range(16):
        stat[j : j + 1, 2 * count : 2 * count + rows] = pos_out[:, j * rows : (j + 1) * rows]


def grads_kernel(rows, tile, offs, temp, target, own, pos, stat, e_in, q_all, p_all, *refs):
    q_outs, p_outs = refs[:4], refs[4:13]
    total_out, pos_sum, delta, q_grad, p_grad = refs[13:]
    count = rows * 16
    scale = temp[0]
    tops = stat[:, :count]
    top = jnp.max(tops, axis=0, keepdims=True)
    total = top + jnp.log(
        jnp.sum(stat[:, count : 2 * count] * jnp.exp(tops - top), axis=0, keepdims=True)
    )
    total_out[...] = total
    pos_sum[...] = jnp.sum(stat[:, 2 * count :], axis=0, keepdims=True)
    factor = jnp.exp(own[0:1, :count] - total)
    at_hit = jnp.exp(pos[...] - total) - 1.0
    for t in range(count // tile):
        cols = slice(t * tile, (t + 1) * tile)
        hit = lax.broadcasted_iota(jnp.int32, (count, tile), 0) == target[:, cols]
        prob = e_in[:, cols].astype(F32) * factor[:, cols]
        delta[:, cols] = jnp.where(hit, at_hit[:, cols], prob).astype(BF16)
    for t in range(count // tile):
        part = slice(t * tile, (t + 1) * tile)
        p_grad[part, :] = (
            scale * jnp.dot(delta[part, :], q_all[...], preferred_element_type=F32)
        ).astype(BF16)
    at = 0
    for out in p_outs:
        size = out.shape[0]
        out[...] = p_grad[at : at + size, :]
        at += size
    for t in range(count // tile):
        part = slice(t * tile, (t + 1) * tile)
        q_grad[part, :] = (
            scale
            * lax.dot_general(
                delta[:, part], p_all[...], (((0,), (0,)), ((), ())), preferred_element_type=F32
            )
        ).astype(BF16)
    for k, out in enumerate(q_outs):
        for b in range(4):
            out[b * rows : (b + 1) * rows, :] = q_grad[
                pl.ds(pl.multiple_of(offs[4 * k + b], 16), rows), :
            ]


def add_kernel(*refs):
    out = refs[-1]
    total = refs[0][...].astype(F32)
    for ref in refs[1:-1]:
        total = total + ref[...].astype(F32)
    out[...] = total.astype(out.dtype)


def final_kernel(q_ref, p_ref, q0, q1, q2, q3, p0, p1, q_out, p_out):
    def back(src, grad, dst):
        wide = src[...].astype(F32)
        length = jnp.sqrt(jnp.sum(wide * wide, axis=1, keepdims=True))
        unit = wide / length
        along = jnp.sum(unit * grad, axis=1, keepdims=True)
        dst[...] = ((grad - unit * along) / length).astype(BF16)

    q_sum = q0[...].astype(F32) + q1[...].astype(F32) + q2[...].astype(F32) + q3[...].astype(F32)
    back(q_ref, q_sum, q_out)
    back(p_ref, p0[...].astype(F32) + p1[...].astype(F32), p_out)


def vmem(n):
    return [pl.BlockSpec(memory_space=pltpu.VMEM)] * n


def smem(n):
    return [pl.BlockSpec(memory_space=pltpu.SMEM)] * n


def call(kernel, shapes, in_specs, args, scratch=()):
    multi = isinstance(shapes, (list, tuple))
    return pl.pallas_call(
        kernel,
        out_shape=shapes,
        in_specs=in_specs,
        out_specs=vmem(len(shapes)) if multi else vmem(1)[0],
        scratch_shapes=list(scratch),
        compiler_params=pltpu.CompilerParams(vmem_limit_bytes=VMEM_LIMIT),
    )(*args)


def gather_queries(low):
    near = jnp.concatenate([low] + [inner(low, k) for k in (1, 2, 3)], axis=0)
    return [near] + [outer(near, k) for k in (1, 2, 3)]


def gather_passages(low):
    pair = jnp.concatenate([low, swap(low)], axis=0)
    one = along_z(pair, 1)
    two = along_z(pair, 2)
    three = along_z(two, 1)
    four = along_z(two[: low.shape[0]], 2)
    return [pair, one, two, three, four, swap(four), swap(one), swap(two), swap(three)]


def add(shape, dtype, *terms):
    return call(
        add_kernel, jax.ShapeDtypeStruct(shape, dtype), vmem(len(terms)), terms
    )


def scatter_queries(parts, rows):
    terms = [parts[0]] + [outer(parts[k], -k) for k in (1, 2, 3)]
    near = add(parts[0].shape, BF16, *terms)
    return [near[:rows]] + [inner(near[k * rows : (k + 1) * rows], -k) for k in (1, 2, 3)]


def scatter_passages(parts, rows):
    pair, one, two, three, four = parts[:5]
    four_b, one_b, two_b, three_b = (swap(part) for part in parts[5:])
    shape = pair.shape
    three = add(shape, BF16, three, three_b)
    four = add(four.shape, BF16, four, four_b)
    from_three = along_z(three, -1)
    from_four = along_z(four, -2)
    one = add(shape, BF16, one, one_b)
    from_one = along_z(one, -1)
    zero = jnp.zeros_like(from_four)
    two = add(shape, BF16, two, two_b, from_three, jnp.concatenate([from_four, zero], axis=0))
    from_two = along_z(two, -2)
    here = add(shape, BF16, pair, from_one, from_two)
    return here[:rows], swap(here[rows:])


def local(queries, passages, positives, inv_temp):
    rows, width = queries.shape
    count = rows * 16
    tile = 256
    zl, core, y, x, zh = (lax.axis_index(name) for name in AXES)
    z = zh * 4 + zl
    shape = jax.ShapeDtypeStruct
    q_low, p_low = call(
        norm_kernel, [shape((rows, width), BF16)] * 2, vmem(2), (queries, passages)
    )
    q_parts = gather_queries(q_low)
    p_parts = gather_passages(p_low)

    near, far = jnp.arange(16) % 4, jnp.arange(16) // 4
    from_y = (y + jnp.where(core == 0, far, near)) % 4
    from_x = (x + jnp.where(core == 0, near, far)) % 4
    offs = ((from_y * 4 + from_x) * rows).astype(jnp.int32)

    wanted = lax.dynamic_index_in_dim(positives.reshape(16, 2, rows), zh, 1, keepdims=False)
    block = wanted // rows
    owner_z = (block % 2) * 4 + block // 64
    owner_core = (block // 32) % 2
    other = (owner_core != core).astype(jnp.int32)
    away = jnp.where(core == 0, owner_z - z, z - owner_z) % 8
    slot = jnp.where(
        away < 4,
        2 * away + other,
        jnp.where(away == 4, 8 + other, 10 + 2 * (7 - away) + 1 - other),
    )
    present = (block // 8) % 4 * 4 + (block // 2) % 4 == y * 4 + x
    target = jnp.where(present, slot * rows + wanted % rows, -1).reshape(1, count)
    temp = inv_temp.reshape(1)

    stat_width = 2 * count + -(-rows // 128) * 128
    e, stat, pos, q_all, p_all = call(
        functools.partial(stats_kernel, rows, tile),
        [
            shape((count, count), BF16),
            shape((16, stat_width), F32),
            shape((1, count), F32),
            shape((count, width), BF16),
            shape((count, width), BF16),
        ],
        smem(2) + vmem(1) + [pl.BlockSpec(memory_space=pl.ANY)] * 13,
        (offs, temp, target, *q_parts, *p_parts),
        [pltpu.VMEM((count, tile), F32), pltpu.SemaphoreType.DMA((25,))],
    )
    stats = lax.all_to_all(stat, ("y", "x"), 0, 0, tiled=True)

    grads = call(
        functools.partial(grads_kernel, rows, tile),
        [shape(part.shape, BF16) for part in (*q_parts, *p_parts)]
        + [shape((1, count), F32), shape((1, stat_width - 2 * count), F32)],
        smem(2) + vmem(7),
        (offs, temp, target, stat, pos, stats, e, q_all, p_all),
        [
            pltpu.VMEM((count, count), BF16),
            pltpu.VMEM((count, width), BF16),
            pltpu.VMEM((count, width), BF16),
        ],
    )
    q_terms = scatter_queries(grads[:4], rows)
    p_terms = scatter_passages(grads[4:13], rows)
    total, pos_sum = grads[13:]
    mine = lax.dynamic_slice_in_dim(total[0], (y * 4 + x) * rows, rows, 0)
    query_loss = mine - pos_sum[0, :rows]
    query_grads, passage_grads = call(
        final_kernel,
        [shape((rows, width), BF16)] * 2,
        vmem(8),
        (queries, passages, *q_terms, *p_terms),
    )
    return (query_loss, query_grads, passage_grads)


def solution(mesh):
    fine = Mesh(mesh.devices.reshape(SIZES), AXES)
    return jax.shard_map(
        local,
        mesh=fine,
        in_specs=(P(AXES, None), P(AXES, None), P(("zl", "core")), P()),
        out_specs=(P(AXES), P(AXES, None), P(AXES, None)),
        check_vma=False,
    )
```

time: 907 us -> 119 us (0.13)
  waiting for transfers between devices: 434 us -> 19 us
  blocking collectives: 396 us -> 13.3 us
  starting transfers between devices: 0.12 us -> 52.6 us
  matrix products: 44.8 us -> 0 us
  Pallas kernels: 0 us -> 25.7 us
  other arithmetic: 14.5 us -> 0.93 us
  between operations: 14.5 us -> 1.53 us
    reduce_scatter x2 -> x0, waiting for transfers between devices: 343 us -> none  [the longest x1 266 us: local(): lax.psum_scatter((inv_temp * jnp.dot(delta, passage_block, preferred_elem...]
    psum x1 -> x0, blocking collectives: 190 us -> none  [local(): lax.psum((expsum * jnp.exp(biggest - top), positive), 'pa')]
    pmax x1 -> x0, blocking collectives: 188 us -> none  [local(): top = lax.pmax(biggest, 'pa')]
    all_gather x1 -> x0, waiting for transfers between devices: 91.3 us -> none  [local(): query_block = lax.all_gather(query_low, 'pa', axis=0, tiled=True)]
    ppermute x0 -> x30, starting transfers between devices: none -> 52.6 us  [fetch(): return lax.ppermute(array, AXES, pairs)]
    dot_general x12 -> x0, matrix products: 44.8 us -> none  [the longest x10 30.9 us: similar(): lax.dot_general(rows, column_rows, (((1,), (1,)), ((), ())), preferred_el...]
    pallas_call x0 -> x10, Pallas kernels: none -> 25.7 us  [call(): pl.pallas_call(kernel, out_shape=shapes, in_specs=in_specs, out_specs=vme...]
    ppermute x0 -> x30, waiting for transfers between devices: none -> 19 us  [fetch(): return lax.ppermute(array, AXES, pairs)]
  transfers between devices with their start and end apart: 3 -> 30, of which waited for: 3 -> 7; matrix products, arithmetic and copies ran while one was open for 1% -> 2% of each run, Pallas kernels for 0% -> 1%
where the time goes in v1:
time: 119 us
  starting transfers between devices  52.6 us (44%)
  Pallas kernels  25.7 us (22%)
  waiting for transfers between devices  19 us (16%)
  blocking collectives  13.3 us (11%)
  local copies, waits for them, and re-layouts  5.64 us (5%)
  between operations  1.53 us (1%)
    ppermute x30, starting transfers between devices, fetch(): return lax.ppermute(array, AXES, pairs)  52.6 us
    pallas_call x10, Pallas kernels, call(): pl.pallas_call(kernel, out_shape=shapes, in_specs=in_specs, out_specs=vme...  25.7 us
    ppermute x30, waiting for transfers between devices, fetch(): return lax.ppermute(array, AXES, pairs)  19 us
    all_to_all x1, blocking collectives, local(): stats = lax.all_to_all(stat, ('y', 'x'), 0, 0, tiled=True)  13.3 us
    unnamed x21, local copies, waits for them, and re-layouts  4.32 us
  transfers between devices with their start and end apart: 30, of which 7 were waited for; matrix products, arithmetic and copies ran while one was open for 2% of the time, Pallas kernels for 1%

profile of v1, /device:TPU:1, one launch (start us, length us, event | category | flops | bytes accessed | tf_op | source)
XLA Modules:
  0.0 118.7 jit_solution(8280654426410473921)
XLA Ops:
  0.6 0.9 copy-done
  1.5 0.9 copy-done.2
  2.6 3.3 %collective-permute-start.6 = (bf16[80,768]{1,0:T(8,128)(2,1)S(1)}, bf16[80,768]{1,0:T(8,128)(2,1)S(1)}, u32[]{:S(2)}, u32[]{:S(2)}) collective-permute-start(bf16[80,768]{1,0:T(8,128)(2,1)S(1)} %get-tuple-element.28), channel_id=1, source_target_pairs={{32,0},{34,2},{36,4},{38,6},{40,8},{42,10},{44,12},{46,14},{48,16}... | collective-permute-start | bytes 368648 | tf_op jit(solution)/shard_map/ppermute | solution.py:30
  5.9 1.0 collective-permute-done.6
  6.9 1.3 %collective-permute-start.8 = (bf16[160,768]{1,0:T(8,128)(2,1)S(1)}, bf16[160,768]{1,0:T(8,128)(2,1)S(1)}, u32[]{:S(2)}, u32[]{:S(2)}) collective-permute-start(bf16[160,768]{1,0:T(8,128)(2,1)S(1)} %constant_dynamic-update-slice_fusion.4.refs_4_), channel_id=1, source_target_pairs={{128,0},{130,2},{132,4},{134,6},{136,8},{138,10},{140,12},{142,14}... | collective-permute-start | bytes 737288 | tf_op jit(solution)/shard_map/ppermute | solution.py:30
  8.2 1.3 %collective-permute-start.2 = (bf16[80,768]{1,0:T(8,128)(2,1)S(1)}, bf16[80,768]{1,0:T(8,128)(2,1)S(1)}, u32[]{:S(2)}, u32[]{:S(2)}) collective-permute-start(bf16[80,768]{1,0:T(8,128)(2,1)S(1)} %get-tuple-element.27), channel_id=1, source_target_pairs={{6,0},{0,2},{2,4},{4,6},{14,8},{8,10},{10,12},{12,14},{22,16},{16,... | collective-permute-start | bytes 368648 | tf_op jit(solution)/shard_map/ppermute | solution.py:30
  9.5 2.6 %collective-permute-start.1 = (bf16[80,768]{1,0:T(8,128)(2,1)S(1)}, bf16[80,768]{1,0:T(8,128)(2,1)S(1)}, u32[]{:S(2)}, u32[]{:S(2)}) collective-permute-start(bf16[80,768]{1,0:T(8,128)(2,1)S(1)} %get-tuple-element.27), channel_id=1, source_target_pairs={{4,0},{6,2},{0,4},{2,6},{12,8},{14,10},{8,12},{10,14},{20,16},{22,... | collective-permute-start | bytes 368648 | tf_op jit(solution)/shard_map/ppermute | solution.py:30
  12.2 1.1 collective-permute-start
  13.2 0.8 reshape.438
  14.0 1.4 %collective-permute-done.8.refs_6_ = bf16[160,768]{1,0:T(8,128)(2,1)S(1)} collective-permute-done((bf16[160,768]{1,0:T(8,128)(2,1)S(1)}, bf16[160,768]{1,0:T(8,128)(2,1)S(1)}, u32[]{:S(2)}, u32[]{:S(2)}) %collective-permute-start.8) | collective-permute-done | bytes 245792 | tf_op jit(solution)/shard_map/ppermute | solution.py:30
  15.5 2.9 %collective-permute-start.10 = (bf16[80,768]{1,0:T(8,128)(2,1)S(1)}, bf16[80,768]{1,0:T(8,128)(2,1)S(1)}, u32[]{:S(2)}, u32[]{:S(2)}) collective-permute-start(bf16[80,768]{1,0:T(8,128)(2,1)S(1)} %slice.32), channel_id=1, source_target_pairs={{128,0},{130,2},{132,4},{134,6},{136,8},{138,10},{140,12},{142,14}... | collective-permute-start | bytes 368648 | tf_op jit(solution)/shard_map/ppermute | solution.py:30
  18.8 0.8 collective-permute-start.7
  19.6 3.7 %collective-permute-start.13 = (bf16[160,768]{1,0:T(8,128)(2,1)S(1)}, bf16[160,768]{1,0:T(8,128)(2,1)S(1)}, u32[]{:S(2)}, u32[]{:S(2)}) collective-permute-start(bf16[160,768]{1,0:T(8,128)(2,1)S(1)} %collective-permute-done.8.refs_6_), channel_id=1, source_target_pairs={{32,0},{34,2},{36,4},{38,6},{40,8},{42,10},{44,12},{46,14},{48,16}... | collective-permute-start | bytes 737288 | tf_op jit(solution)/shard_map/ppermute | solution.py:30
  23.3 0.9 collective-permute-start.9
  24.2 1.4 %collective-permute-start.11 = (bf16[80,768]{1,0:T(8,128)(2,1)S(1)}, bf16[80,768]{1,0:T(8,128)(2,1)S(1)}, u32[]{:S(2)}, u32[]{:S(2)}) collective-permute-start(bf16[80,768]{1,0:T(8,128)(2,1)S(1)} %collective-permute-done.10.refs_8_), channel_id=1, source_target_pairs={{32,0},{34,2},{36,4},{38,6},{40,8},{42,10},{44,12},{46,14},{48,16}... | collective-permute-start | bytes 368648 | tf_op jit(solution)/shard_map/ppermute | solution.py:30
  25.6 2.3 %collective-permute-start.5 = (bf16[320,768]{1,0:T(8,128)(2,1)S(1)}, bf16[320,768]{1,0:T(8,128)(2,1)S(1)}, u32[]{:S(2)}, u32[]{:S(2)}) collective-permute-start(bf16[320,768]{1,0:T(8,128)(2,1)S(1)} %constant_dynamic-update-slice_fusion.refs_0_), channel_id=1, source_target_pairs={{24,0},{26,2},{28,4},{30,6},{0,8},{2,10},{4,12},{6,14},{8,16},{10,... | collective-permute-start | bytes 1474568 | tf_op jit(solution)/shard_map/ppermute | solution.py:30
  27.9 2.0 %collective-permute-start.4 = (bf16[320,768]{1,0:T(8,128)(2,1)S(1)}, bf16[320,768]{1,0:T(8,128)(2,1)S(1)}, u32[]{:S(2)}, u32[]{:S(2)}) collective-permute-start(bf16[320,768]{1,0:T(8,128)(2,1)S(1)} %constant_dynamic-update-slice_fusion.refs_0_), channel_id=1, source_target_pairs={{16,0},{18,2},{20,4},{22,6},{24,8},{26,10},{28,12},{30,14},{0,16},... | collective-permute-start | bytes 1474568 | tf_op jit(solution)/shard_map/ppermute | solution.py:30
  29.9 0.6 copy-done.6
  30.5 1.2 collective-permute-start.3
  31.7 2.8 %collective-permute-start.12 = (bf16[160,768]{1,0:T(8,128)(2,1)S(1)}, bf16[160,768]{1,0:T(8,128)(2,1)S(1)}, u32[]{:S(2)}, u32[]{:S(2)}) collective-permute-start(bf16[160,768]{1,0:T(8,128)(2,1)S(1)} %collective-permute-done.7.refs_5_), channel_id=1, source_target_pairs={{32,0},{34,2},{36,4},{38,6},{40,8},{42,10},{44,12},{46,14},{48,16}... | collective-permute-start | bytes 737288 | tf_op jit(solution)/shard_map/ppermute | solution.py:30
  34.5 0.3 collective-permute-start.14
  35.7 6.0 %collective-permute-done.4.refs_2_ = bf16[320,768]{1,0:T(8,128)(2,1)S(1)} collective-permute-done((bf16[320,768]{1,0:T(8,128)(2,1)S(1)}, bf16[320,768]{1,0:T(8,128)(2,1)S(1)}, u32[]{:S(2)}, u32[]{:S(2)}) %collective-permute-start.4) | collective-permute-done | bytes 491552 | tf_op jit(solution)/shard_map/ppermute | solution.py:30
  41.7 0.9 copy-done.5
  42.6 0.9 copy-done.7
  43.5 14.3 %shard_map.68 = (bf16[1280,1280]{1,0:T(8,128)(2,1)}, f32[16,2688]{1,0:T(8,128)S(1)}, f32[1,1280]{1,0:T(1,128)S(1)}, bf16[1280,768]{1,0:T(8,128)(2,1)}, bf16[1280,768]{1,0:T(8,128)(2,1)}) custom-call(s32[16]{0:T(128)S(1)} %fusion.16.offs, f32[1]{0:T(128)} %bitcast.7.temp, s32[1,1280]{1,0:T(1,128)S(1)} %compare_select_fusion.10.target, ...), custom_call_target="tpu_custom_call" | custom-call | tf_op jit(solution)/shard_map/pallas_call | solution.py:176
  58.0 13.3 %all_to_all.11 = f32[16,1,2688]{2,1,0:T(1,128)S(1)} all-to-all(f32[16,1,2688]{2,1,0:T(1,128)S(1)} %copy.7), channel_id=1, replica_groups=mesh['zl'=4,'core'=2,'y'=4,'x'=4,'zh'=2] {'y','x'}, dimensions={0} | all-to-all | bytes 344064 | tf_op jit(solution)/shard_map/all_to_all | solution.py:276
  71.3 9.7 %shard_map.69 = (bf16[320,768]{1,0:T(8,128)(2,1)S(1)}, bf16[320,768]{1,0:T(8,128)(2,1)}, bf16[320,768]{1,0:T(8,128)(2,1)}, bf16[320,768]{1,0:T(8,128)(2,1)}, bf1...) custom-call(s32[16]{0:T(128)S(1)} %fusion.16.offs, ...), custom_call_target="tpu_custom_call" | custom-call | tf_op jit(solution)/shard_map/pallas_call | solution.py:176
  80.9 5.2 %collective-permute-start.24 = (bf16[160,768]{1,0:T(8,128)(2,1)S(1)}, bf16[160,768]{1,0:T(8,128)(2,1)S(1)}, u32[]{:S(2)}, u32[]{:S(2)}) collective-permute-start(bf16[160,768]{1,0:T(8,128)(2,1)S(1)} %get-tuple-element.46), channel_id=1, source_target_pairs={{32,0},{34,2},{36,4},{38,6},{40,8},{42,10},{44,12},{46,14},{48,16}... | collective-permute-start | bytes 737288 | tf_op jit(solution)/shard_map/ppermute | solution.py:30
  86.1 0.5 collective-permute-start.21
  86.6 0.3 collective-permute-start.15
  86.9 1.5 %collective-permute-start.16 = (bf16[320,768]{1,0:T(8,128)(2,1)}, bf16[320,768]{1,0:T(8,128)(2,1)S(1)}, u32[]{:S(2)}, u32[]{:S(2)}) collective-permute-start(bf16[320,768]{1,0:T(8,128)(2,1)} %get-tuple-element.38), channel_id=1, source_target_pairs={{16,0},{18,2},{20,4},{22,6},{24,8},{26,10},{28,12},{30,14},{0,16},... | collective-permute-start | bytes 1474568 | tf_op jit(solution)/shard_map/ppermute | solution.py:30
  88.4 1.1 collective-permute-start.17
  89.6 1.9 %collective-permute-start.27 = (bf16[80,768]{1,0:T(8,128)(2,1)S(1)}, bf16[80,768]{1,0:T(8,128)(2,1)S(1)}, u32[]{:S(2)}, u32[]{:S(2)}) collective-permute-start(bf16[80,768]{1,0:T(8,128)(2,1)S(1)} %shard_map.73), channel_id=1, source_target_pairs={{129,0},{131,2},{133,4},{135,6},{137,8},{139,10},{141,12},{143,14}... | collective-permute-start | bytes 368648 | tf_op jit(solution)/shard_map/ppermute | solution.py:30
  91.5 3.5 %collective-permute-done.27 = bf16[80,768]{1,0:T(8,128)(2,1)S(1)} collective-permute-done((bf16[80,768]{1,0:T(8,128)(2,1)S(1)}, bf16[80,768]{1,0:T(8,128)(2,1)S(1)}, u32[]{:S(2)}, u32[]{:S(2)}) %collective-permute-start.27) | collective-permute-done | bytes 122912 | tf_op jit(solution)/shard_map/ppermute | solution.py:30
  95.0 3.1 %collective-permute-start.23 = (bf16[160,768]{1,0:T(8,128)(2,1)S(1)}, bf16[160,768]{1,0:T(8,128)(2,1)S(1)}, u32[]{:S(2)}, u32[]{:S(2)}) collective-permute-start(bf16[160,768]{1,0:T(8,128)(2,1)S(1)} %get-tuple-element.44), channel_id=1, source_target_pairs={{32,0},{34,2},{36,4},{38,6},{40,8},{42,10},{44,12},{46,14},{48,16}... | collective-permute-start | bytes 737288 | tf_op jit(solution)/shard_map/ppermute | solution.py:30
  98.1 1.2 collective-permute-start.25
  99.3 1.0 collective-permute-start.22
  100.4 3.0 %collective-permute-done.25.refs_2_ = bf16[160,768]{1,0:T(8,128)(2,1)S(1)} collective-permute-done((bf16[160,768]{1,0:T(8,128)(2,1)S(1)}, bf16[160,768]{1,0:T(8,128)(2,1)S(1)}, u32[]{:S(2)}, u32[]{:S(2)}) %collective-permute-start.25) | collective-permute-done | bytes 245792 | tf_op jit(solution)/shard_map/ppermute | solution.py:30
  103.5 1.0 collective-permute-start.28
  104.5 0.2 shard_map.70
  104.8 0.4 collective-permute-start.20
  105.3 2.1 %collective-permute-start.19 = (bf16[80,768]{1,0:T(8,128)(2,1)S(1)}, bf16[80,768]{1,0:T(8,128)(2,1)S(1)}, u32[]{:S(2)}, u32[]{:S(2)}) collective-permute-start(bf16[80,768]{1,0:T(8,128)(2,1)S(1)} %get-tuple-element.54), channel_id=1, source_target_pairs={{4,0},{6,2},{0,4},{2,6},{12,8},{14,10},{8,12},{10,14},{20,16},{22,... | collective-permute-start | bytes 368648 | tf_op jit(solution)/shard_map/ppermute | solution.py:30
  107.3 0.8 collective-permute-start.18
  108.1 3.7 %collective-permute-done.28.refs_2_ = bf16[160,768]{1,0:T(8,128)(2,1)S(1)} collective-permute-done((bf16[160,768]{1,0:T(8,128)(2,1)S(1)}, bf16[160,768]{1,0:T(8,128)(2,1)S(1)}, u32[]{:S(2)}, u32[]{:S(2)}) %collective-permute-start.28) | collective-permute-done | bytes 245792 | tf_op jit(solution)/shard_map/ppermute | solution.py:30
  111.9 4.8 %collective-permute-start.29 = (bf16[80,768]{1,0:T(8,128)(2,1)S(1)}, bf16[80,768]{1,0:T(8,128)(2,1)S(1)}, u32[]{:S(2)}, u32[]{:S(2)}) collective-permute-start(bf16[80,768]{1,0:T(8,128)(2,1)S(1)} %get-tuple-element.57), channel_id=1, source_target_pairs={{32,0},{34,2},{36,4},{38,6},{40,8},{42,10},{44,12},{46,14},{48,16}... | collective-permute-start | bytes 368648 | tf_op jit(solution)/shard_map/ppermute | solution.py:30
  116.7 0.6 subtract_bitcast_fusion
  117.3 0.4 collective-permute-done.29.p1
  117.7 0.9 shard_map.76
  (60 shorter events, 1.5 us)
Async XLA Ops:
  0.6 0.9 copy-start
  1.5 0.9 copy-start.2
  2.6 4.3 %collective-permute-start.6 = (bf16[80,768]{1,0:T(8,128)(2,1)S(1)}, bf16[80,768]{1,0:T(8,128)(2,1)S(1)}, u32[]{:S(2)}, u32[]{:S(2)}) collective-permute-start(bf16[80,768]{1,0:T(8,128)(2,1)S(1)} %get-tuple-element.28), channel_id=1, source_target_pairs={{32,0},{34,2},{36,4},{38,6},{40,8},{42,10},{44,12},{46,14},{48,16}... | collective-permute-start | bytes 368648 | tf_op jit(solution)/shard_map/ppermute | solution.py:30
  6.9 8.5 %collective-permute-start.8 = (bf16[160,768]{1,0:T(8,128)(2,1)S(1)}, bf16[160,768]{1,0:T(8,128)(2,1)S(1)}, u32[]{:S(2)}, u32[]{:S(2)}) collective-permute-start(bf16[160,768]{1,0:T(8,128)(2,1)S(1)} %constant_dynamic-update-slice_fusion.4.refs_4_), channel_id=1, source_target_pairs={{128,0},{130,2},{132,4},{134,6},{136,8},{138,10},{140,12},{142,14}... | collective-permute-start | bytes 737288 | tf_op jit(solution)/shard_map/ppermute | solution.py:30
  8.2 17.4 %collective-permute-start.2 = (bf16[80,768]{1,0:T(8,128)(2,1)S(1)}, bf16[80,768]{1,0:T(8,128)(2,1)S(1)}, u32[]{:S(2)}, u32[]{:S(2)}) collective-permute-start(bf16[80,768]{1,0:T(8,128)(2,1)S(1)} %get-tuple-element.27), channel_id=1, source_target_pairs={{6,0},{0,2},{2,4},{4,6},{14,8},{8,10},{10,12},{12,14},{22,16},{16,... | collective-permute-start | bytes 368648 | tf_op jit(solution)/shard_map/ppermute | solution.py:30
  9.5 10.0 %collective-permute-start.1 = (bf16[80,768]{1,0:T(8,128)(2,1)S(1)}, bf16[80,768]{1,0:T(8,128)(2,1)S(1)}, u32[]{:S(2)}, u32[]{:S(2)}) collective-permute-start(bf16[80,768]{1,0:T(8,128)(2,1)S(1)} %get-tuple-element.27), channel_id=1, source_target_pairs={{4,0},{6,2},{0,4},{2,6},{12,8},{14,10},{8,12},{10,14},{20,16},{22,... | collective-permute-start | bytes 368648 | tf_op jit(solution)/shard_map/ppermute | solution.py:30
  12.2 11.1 %collective-permute-start = (bf16[80,768]{1,0:T(8,128)(2,1)S(1)}, bf16[80,768]{1,0:T(8,128)(2,1)S(1)}, u32[]{:S(2)}, u32[]{:S(2)}) collective-permute-start(bf16[80,768]{1,0:T(8,128)(2,1)S(1)} %get-tuple-element.27), channel_id=1, source_target_pairs={{2,0},{4,2},{6,4},{0,6},{10,8},{12,10},{14,12},{8,14},{18,16},{20,... | collective-permute-start | bytes 368648 | tf_op jit(solution)/shard_map/ppermute | solution.py:30
  15.5 8.7 %collective-permute-start.10 = (bf16[80,768]{1,0:T(8,128)(2,1)S(1)}, bf16[80,768]{1,0:T(8,128)(2,1)S(1)}, u32[]{:S(2)}, u32[]{:S(2)}) collective-permute-start(bf16[80,768]{1,0:T(8,128)(2,1)S(1)} %slice.32), channel_id=1, source_target_pairs={{128,0},{130,2},{132,4},{134,6},{136,8},{138,10},{140,12},{142,14}... | collective-permute-start | bytes 368648 | tf_op jit(solution)/shard_map/ppermute | solution.py:30
  18.8 9.2 %collective-permute-start.7 = (bf16[160,768]{1,0:T(8,128)(2,1)S(1)}, bf16[160,768]{1,0:T(8,128)(2,1)S(1)}, u32[]{:S(2)}, u32[]{:S(2)}) collective-permute-start(bf16[160,768]{1,0:T(8,128)(2,1)S(1)} %constant_dynamic-update-slice_fusion.4.refs_4_), channel_id=1, source_target_pairs={{64,0},{66,2},{68,4},{70,6},{72,8},{74,10},{76,12},{78,14},{80,16}... | collective-permute-start | bytes 737288 | tf_op jit(solution)/shard_map/ppermute | solution.py:30
  19.6 12.1 %collective-permute-start.13 = (bf16[160,768]{1,0:T(8,128)(2,1)S(1)}, bf16[160,768]{1,0:T(8,128)(2,1)S(1)}, u32[]{:S(2)}, u32[]{:S(2)}) collective-permute-start(bf16[160,768]{1,0:T(8,128)(2,1)S(1)} %collective-permute-done.8.refs_6_), channel_id=1, source_target_pairs={{32,0},{34,2},{36,4},{38,6},{40,8},{42,10},{44,12},{46,14},{48,16}... | collective-permute-start | bytes 737288 | tf_op jit(solution)/shard_map/ppermute | solution.py:30
  23.3 11.3 %collective-permute-start.9 = (bf16[160,768]{1,0:T(8,128)(2,1)S(1)}, bf16[160,768]{1,0:T(8,128)(2,1)S(1)}, u32[]{:S(2)}, u32[]{:S(2)}) collective-permute-start(bf16[160,768]{1,0:T(8,128)(2,1)S(1)} %collective-permute-done.8.refs_6_), channel_id=1, source_target_pairs={{64,0},{66,2},{68,4},{70,6},{72,8},{74,10},{76,12},{78,14},{80,16}... | collective-permute-start | bytes 737288 | tf_op jit(solution)/shard_map/ppermute | solution.py:30
  24.2 5.7 %copy-start.4 = (bf16[80,768]{1,0:T(8,128)(2,1)}, bf16[80,768]{1,0:T(8,128)(2,1)S(1)}, u32[]{:S(2)}) copy-start(bf16[80,768]{1,0:T(8,128)(2,1)S(1)} %collective-permute-done.10.refs_8_) | copy-start | bytes 368644
  24.2 5.7 %collective-permute-start.11 = (bf16[80,768]{1,0:T(8,128)(2,1)S(1)}, bf16[80,768]{1,0:T(8,128)(2,1)S(1)}, u32[]{:S(2)}, u32[]{:S(2)}) collective-permute-start(bf16[80,768]{1,0:T(8,128)(2,1)S(1)} %collective-permute-done.10.refs_8_), channel_id=1, source_target_pairs={{32,0},{34,2},{36,4},{38,6},{40,8},{42,10},{44,12},{46,14},{48,16}... | collective-permute-start | bytes 368648 | tf_op jit(solution)/shard_map/ppermute | solution.py:30
  25.6 10.1 %collective-permute-start.5 = (bf16[320,768]{1,0:T(8,128)(2,1)S(1)}, bf16[320,768]{1,0:T(8,128)(2,1)S(1)}, u32[]{:S(2)}, u32[]{:S(2)}) collective-permute-start(bf16[320,768]{1,0:T(8,128)(2,1)S(1)} %constant_dynamic-update-slice_fusion.refs_0_), channel_id=1, source_target_pairs={{24,0},{26,2},{28,4},{30,6},{0,8},{2,10},{4,12},{6,14},{8,16},{10,... | collective-permute-start | bytes 1474568 | tf_op jit(solution)/shard_map/ppermute | solution.py:30
  27.9 13.7 %collective-permute-start.4 = (bf16[320,768]{1,0:T(8,128)(2,1)S(1)}, bf16[320,768]{1,0:T(8,128)(2,1)S(1)}, u32[]{:S(2)}, u32[]{:S(2)}) collective-permute-start(bf16[320,768]{1,0:T(8,128)(2,1)S(1)} %constant_dynamic-update-slice_fusion.refs_0_), channel_id=1, source_target_pairs={{16,0},{18,2},{20,4},{22,6},{24,8},{26,10},{28,12},{30,14},{0,16},... | collective-permute-start | bytes 1474568 | tf_op jit(solution)/shard_map/ppermute | solution.py:30
  29.9 0.6 copy-start.6
  30.5 11.1 %collective-permute-start.3 = (bf16[320,768]{1,0:T(8,128)(2,1)S(1)}, bf16[320,768]{1,0:T(8,128)(2,1)S(1)}, u32[]{:S(2)}, u32[]{:S(2)}) collective-permute-start(bf16[320,768]{1,0:T(8,128)(2,1)S(1)} %constant_dynamic-update-slice_fusion.refs_0_), channel_id=1, source_target_pairs={{8,0},{10,2},{12,4},{14,6},{16,8},{18,10},{20,12},{22,14},{24,16},... | collective-permute-start | bytes 1474568 | tf_op jit(solution)/shard_map/ppermute | solution.py:30
  31.7 4.0 %collective-permute-start.12 = (bf16[160,768]{1,0:T(8,128)(2,1)S(1)}, bf16[160,768]{1,0:T(8,128)(2,1)S(1)}, u32[]{:S(2)}, u32[]{:S(2)}) collective-permute-start(bf16[160,768]{1,0:T(8,128)(2,1)S(1)} %collective-permute-done.7.refs_5_), channel_id=1, source_target_pairs={{32,0},{34,2},{36,4},{38,6},{40,8},{42,10},{44,12},{46,14},{48,16}... | collective-permute-start | bytes 737288 | tf_op jit(solution)/shard_map/ppermute | solution.py:30
  34.5 7.1 %collective-permute-start.14 = (bf16[160,768]{1,0:T(8,128)(2,1)S(1)}, bf16[160,768]{1,0:T(8,128)(2,1)}, u32[]{:S(2)}, u32[]{:S(2)}) collective-permute-start(bf16[160,768]{1,0:T(8,128)(2,1)S(1)} %collective-permute-done.9.refs_7_), channel_id=1, source_target_pairs={{32,0},{34,2},{36,4},{38,6},{40,8},{42,10},{44,12},{46,14},{48,16}... | collective-permute-start | bytes 737288 | tf_op jit(solution)/shard_map/ppermute | solution.py:30
  41.7 0.9 copy-start.5
  42.6 0.9 copy-start.7
  80.9 8.6 %collective-permute-start.24 = (bf16[160,768]{1,0:T(8,128)(2,1)S(1)}, bf16[160,768]{1,0:T(8,128)(2,1)S(1)}, u32[]{:S(2)}, u32[]{:S(2)}) collective-permute-start(bf16[160,768]{1,0:T(8,128)(2,1)S(1)} %get-tuple-element.46), channel_id=1, source_target_pairs={{32,0},{34,2},{36,4},{38,6},{40,8},{42,10},{44,12},{46,14},{48,16}... | collective-permute-start | bytes 737288 | tf_op jit(solution)/shard_map/ppermute | solution.py:30
  86.1 2.3 %collective-permute-start.26 = (bf16[80,768]{1,0:T(8,128)(2,1)S(1)}, bf16[80,768]{1,0:T(8,128)(2,1)S(1)}, u32[]{:S(2)}, u32[]{:S(2)}) collective-permute-start(bf16[80,768]{1,0:T(8,128)(2,1)S(1)} %get-tuple-element.48), channel_id=1, source_target_pairs={{32,0},{34,2},{36,4},{38,6},{40,8},{42,10},{44,12},{46,14},{48,16}... | collective-permute-start | bytes 368648 | tf_op jit(solution)/shard_map/ppermute | solution.py:30
  86.1 12.0 %collective-permute-start.21 = (bf16[160,768]{1,0:T(8,128)(2,1)S(1)}, bf16[160,768]{1,0:T(8,128)(2,1)S(1)}, u32[]{:S(2)}, u32[]{:S(2)}) collective-permute-start(bf16[160,768]{1,0:T(8,128)(2,1)S(1)} %get-tuple-element.42), channel_id=1, source_target_pairs={{32,0},{34,2},{36,4},{38,6},{40,8},{42,10},{44,12},{46,14},{48,16}... | collective-permute-start | bytes 737288 | tf_op jit(solution)/shard_map/ppermute | solution.py:30
  86.6 17.9 %collective-permute-start.15 = (bf16[320,768]{1,0:T(8,128)(2,1)}, bf16[320,768]{1,0:T(8,128)(2,1)S(1)}, u32[]{:S(2)}, u32[]{:S(2)}) collective-permute-start(bf16[320,768]{1,0:T(8,128)(2,1)} %get-tuple-element.37), channel_id=1, source_target_pairs={{24,0},{26,2},{28,4},{30,6},{0,8},{2,10},{4,12},{6,14},{8,16},{10,... | collective-permute-start | bytes 1474568 | tf_op jit(solution)/shard_map/ppermute | solution.py:30
  86.9 17.6 %collective-permute-start.16 = (bf16[320,768]{1,0:T(8,128)(2,1)}, bf16[320,768]{1,0:T(8,128)(2,1)S(1)}, u32[]{:S(2)}, u32[]{:S(2)}) collective-permute-start(bf16[320,768]{1,0:T(8,128)(2,1)} %get-tuple-element.38), channel_id=1, source_target_pairs={{16,0},{18,2},{20,4},{22,6},{24,8},{26,10},{28,12},{30,14},{0,16},... | collective-permute-start | bytes 1474568 | tf_op jit(solution)/shard_map/ppermute | solution.py:30
  88.4 16.1 %collective-permute-start.17 = (bf16[320,768]{1,0:T(8,128)(2,1)}, bf16[320,768]{1,0:T(8,128)(2,1)S(1)}, u32[]{:S(2)}, u32[]{:S(2)}) collective-permute-start(bf16[320,768]{1,0:T(8,128)(2,1)} %get-tuple-element.39), channel_id=1, source_target_pairs={{8,0},{10,2},{12,4},{14,6},{16,8},{18,10},{20,12},{22,14},{24,16},... | collective-permute-start | bytes 1474568 | tf_op jit(solution)/shard_map/ppermute | solution.py:30
  89.6 5.4 %collective-permute-start.27 = (bf16[80,768]{1,0:T(8,128)(2,1)S(1)}, bf16[80,768]{1,0:T(8,128)(2,1)S(1)}, u32[]{:S(2)}, u32[]{:S(2)}) collective-permute-start(bf16[80,768]{1,0:T(8,128)(2,1)S(1)} %shard_map.73), channel_id=1, source_target_pairs={{129,0},{131,2},{133,4},{135,6},{137,8},{139,10},{141,12},{143,14}... | collective-permute-start | bytes 368648 | tf_op jit(solution)/shard_map/ppermute | solution.py:30
  95.0 4.3 %collective-permute-start.23 = (bf16[160,768]{1,0:T(8,128)(2,1)S(1)}, bf16[160,768]{1,0:T(8,128)(2,1)S(1)}, u32[]{:S(2)}, u32[]{:S(2)}) collective-permute-start(bf16[160,768]{1,0:T(8,128)(2,1)S(1)} %get-tuple-element.44), channel_id=1, source_target_pairs={{32,0},{34,2},{36,4},{38,6},{40,8},{42,10},{44,12},{46,14},{48,16}... | collective-permute-start | bytes 737288 | tf_op jit(solution)/shard_map/ppermute | solution.py:30
  98.1 5.3 %collective-permute-start.25 = (bf16[160,768]{1,0:T(8,128)(2,1)S(1)}, bf16[160,768]{1,0:T(8,128)(2,1)S(1)}, u32[]{:S(2)}, u32[]{:S(2)}) collective-permute-start(bf16[160,768]{1,0:T(8,128)(2,1)S(1)} %shard_map.72), channel_id=1, source_target_pairs={{193,0},{195,2},{197,4},{199,6},{201,8},{203,10},{205,12},{207,14}... | collective-permute-start | bytes 737288 | tf_op jit(solution)/shard_map/ppermute | solution.py:30
  99.3 8.8 %collective-permute-start.22 = (bf16[160,768]{1,0:T(8,128)(2,1)S(1)}, bf16[160,768]{1,0:T(8,128)(2,1)S(1)}, u32[]{:S(2)}, u32[]{:S(2)}) collective-permute-start(bf16[160,768]{1,0:T(8,128)(2,1)S(1)} %shard_map.71), channel_id=1, source_target_pairs={{193,0},{195,2},{197,4},{199,6},{201,8},{203,10},{205,12},{207,14}... | collective-permute-start | bytes 737288 | tf_op jit(solution)/shard_map/ppermute | solution.py:30
  103.5 8.3 %collective-permute-start.28 = (bf16[160,768]{1,0:T(8,128)(2,1)S(1)}, bf16[160,768]{1,0:T(8,128)(2,1)S(1)}, u32[]{:S(2)}, u32[]{:S(2)}) collective-permute-start(bf16[160,768]{1,0:T(8,128)(2,1)S(1)} %shard_map.74), channel_id=1, source_target_pairs={{129,0},{131,2},{133,4},{135,6},{137,8},{139,10},{141,12},{143,14}... | collective-permute-start | bytes 737288 | tf_op jit(solution)/shard_map/ppermute | solution.py:30
  104.5 13.2 %copy-start.1 = (bf16[80,768]{1,0:T(8,128)(2,1)S(1)}, bf16[80,768]{1,0:T(8,128)(2,1)}, u32[]{:S(2)}) copy-start(bf16[80,768]{1,0:T(8,128)(2,1)} %q_ref.3) | copy-start | bytes 368644
  104.5 13.2 %copy-start.3 = (bf16[80,768]{1,0:T(8,128)(2,1)S(1)}, bf16[80,768]{1,0:T(8,128)(2,1)}, u32[]{:S(2)}) copy-start(bf16[80,768]{1,0:T(8,128)(2,1)} %p_ref.3) | copy-start | bytes 368644
  104.8 12.5 %collective-permute-start.20 = (bf16[80,768]{1,0:T(8,128)(2,1)S(1)}, bf16[80,768]{1,0:T(8,128)(2,1)S(1)}, u32[]{:S(2)}, u32[]{:S(2)}) collective-permute-start(bf16[80,768]{1,0:T(8,128)(2,1)S(1)} %get-tuple-element.53), channel_id=1, source_target_pairs={{2,0},{4,2},{6,4},{0,6},{10,8},{12,10},{14,12},{8,14},{18,16},{20,... | collective-permute-start | bytes 368648 | tf_op jit(solution)/shard_map/ppermute | solution.py:30
  105.3 12.1 %collective-permute-start.19 = (bf16[80,768]{1,0:T(8,128)(2,1)S(1)}, bf16[80,768]{1,0:T(8,128)(2,1)S(1)}, u32[]{:S(2)}, u32[]{:S(2)}) collective-permute-start(bf16[80,768]{1,0:T(8,128)(2,1)S(1)} %get-tuple-element.54), channel_id=1, source_target_pairs={{4,0},{6,2},{0,4},{2,6},{12,8},{14,10},{8,12},{10,14},{20,16},{22,... | collective-permute-start | bytes 368648 | tf_op jit(solution)/shard_map/ppermute | solution.py:30
  107.3 10.0 %collective-permute-start.18 = (bf16[80,768]{1,0:T(8,128)(2,1)S(1)}, bf16[80,768]{1,0:T(8,128)(2,1)S(1)}, u32[]{:S(2)}, u32[]{:S(2)}) collective-permute-start(bf16[80,768]{1,0:T(8,128)(2,1)S(1)} %get-tuple-element.55), channel_id=1, source_target_pairs={{6,0},{0,2},{2,4},{4,6},{14,8},{8,10},{10,12},{12,14},{22,16},{16,... | collective-permute-start | bytes 368648 | tf_op jit(solution)/shard_map/ppermute | solution.py:30
  111.9 5.8 %collective-permute-start.29 = (bf16[80,768]{1,0:T(8,128)(2,1)S(1)}, bf16[80,768]{1,0:T(8,128)(2,1)S(1)}, u32[]{:S(2)}, u32[]{:S(2)}) collective-permute-start(bf16[80,768]{1,0:T(8,128)(2,1)S(1)} %get-tuple-element.57), channel_id=1, source_target_pairs={{32,0},{34,2},{36,4},{38,6},{40,8},{42,10},{44,12},{46,14},{48,16}... | collective-permute-start | bytes 368648 | tf_op jit(solution)/shard_map/ppermute | solution.py:30

commit v2 on v1

v2 whole, which is shorter than its diff:
```python
import functools

import jax
import jax.numpy as jnp
from jax import lax
from jax.experimental import pallas as pl
from jax.experimental.pallas import tpu as pltpu
from jax.sharding import Mesh
from jax.sharding import PartitionSpec as P

AXES = ("zl", "core", "y", "x", "zh")
SIZES = (4, 2, 4, 4, 2)
VMEM_LIMIT = 24 * 2**20
F32 = jnp.float32
BF16 = jnp.bfloat16


def device_at(z, core, y, x):
    z, y, x = z % 8, y % 4, x % 4
    return ((((z % 4) * 2 + core) * 4 + y) * 4 + x) * 2 + z // 4


def fetch(array, source):
    pairs = []
    for z in range(8):
        for core in range(2):
            for y in range(4):
                for x in range(4):
                    pairs.append((device_at(*source(z, core, y, x)), device_at(z, core, y, x)))
    return lax.ppermute(array, AXES, pairs)


def swap(array):
    return fetch(array, lambda z, c, y, x: (z, 1 - c, y, x))


def along_z(array, k):
    return fetch(array, lambda z, c, y, x: (z + (k if c == 0 else -k), c, y, x))


def inner(array, k):
    return fetch(array, lambda z, c, y, x: (z, c, y, x + k) if c == 0 else (z, c, y + k, x))


def outer(array, k):
    return fetch(array, lambda z, c, y, x: (z, c, y + k, x) if c == 0 else (z, c, y, x + k))


def norm_kernel(q_ref, p_ref, q_low, p_low):
    for src, dst in ((q_ref, q_low), (p_ref, p_low)):
        wide = src[...].astype(F32)
        length = jnp.sqrt(jnp.sum(wide * wide, axis=1, keepdims=True))
        dst[...] = (wide / length).astype(BF16)


def logits_kernel(chunk, temp, *refs):
    parts = (len(refs) - 2) // 4
    q_parts, targets, p_all = refs[:parts], refs[parts : 2 * parts], refs[2 * parts]
    e_outs, row_outs = refs[2 * parts + 1 : 3 * parts + 1], refs[3 * parts + 1 : 4 * parts + 1]
    logits = refs[-1]
    count = p_all.shape[0]
    scale = temp[0]
    for q, target, e_out, row_out in zip(q_parts, targets, e_outs, row_outs):
        tops = []
        for at in range(0, count, chunk):
            part = slice(at, at + chunk)
            values = scale * lax.dot_general(
                p_all[part, :], q[...], (((1,), (1,)), ((), ())), preferred_element_type=F32
            )
            logits[part, :] = values
            tops.append(jnp.max(values, axis=0, keepdims=True))
        top = functools.reduce(jnp.maximum, tops)
        total = jnp.zeros_like(top)
        positive = jnp.zeros_like(top)
        for at in range(0, count, chunk):
            part = slice(at, at + chunk)
            values = logits[part, :]
            hit = lax.broadcasted_iota(jnp.int32, values.shape, 0) + at == target[...]
            positive = positive + jnp.sum(jnp.where(hit, values, 0.0), axis=0, keepdims=True)
            e = jnp.exp(values - top)
            total = total + jnp.sum(e, axis=0, keepdims=True)
            e_out[part, :] = e.astype(BF16)
        row_out[0:1, :] = top
        row_out[1:2, :] = top + jnp.log(total)
        row_out[2:3, :] = positive


def join_kernel(*refs):
    out = refs[-1]
    at = 0
    for part in refs[:-1]:
        out[at : at + part.shape[0], :] = part[...]
        at += part.shape[0]


def stat_kernel(rows, slots, *refs):
    stat = refs[-1]
    stat[...] = jnp.zeros_like(stat)
    positive = jnp.zeros((16, rows), F32)
    dest = lax.broadcasted_iota(jnp.int32, (16, rows), 0)
    for k, part in enumerate(refs[:-1]):
        for b in range(4):
            slot = slots[4 * k + b]
            lanes = slice(b * rows, (b + 1) * rows)
            stat[:, pl.ds(pl.multiple_of(slot * 128, 128), rows)] = jnp.broadcast_to(
                part[1:2, lanes], (16, rows)
            )
            positive = jnp.where(dest == slot, part[2:3, lanes], positive)
    stat[:, 2048 : 2048 + rows] = positive


def p_grads_kernel(rows, chunk, first, slots, temp, stat, *refs):
    e_parts, row_parts, targets, q_parts = refs[:4], refs[4:8], refs[8:12], refs[12:16]
    delta, q_all, total_out, pos_sum, grad, lane = refs[16:]
    count = delta.shape[0]
    width = e_parts[0].shape[1]
    scale = temp[0]
    sums = stat[:, :2048]
    top = jnp.max(sums, axis=0, keepdims=True)
    total_out[...] = top + jnp.log(jnp.sum(jnp.exp(sums - top), axis=0, keepdims=True))
    pos_sum[...] = jnp.sum(stat[:, 2048:], axis=0, keepdims=True)
    for k in range(4):
        q_all[k * width : (k + 1) * width, :] = q_parts[k][...]
        for b in range(4):
            lane[0:1, b * rows : (b + 1) * rows] = total_out[
                :, pl.ds(pl.multiple_of(slots[4 * k + b] * 128, 128), rows)
            ]
        total = lane[0:1, :]
        factor = jnp.exp(row_parts[k][0:1, :] - total)
        at_hit = jnp.exp(row_parts[k][2:3, :] - total) - 1.0
        for at in range(0, count, chunk):
            part = slice(at, at + chunk)
            prob = e_parts[k][part, :].astype(F32) * factor
            hit = lax.broadcasted_iota(jnp.int32, prob.shape, 0) + at == targets[k][...]
            delta[part, k * width : (k + 1) * width] = jnp.where(hit, at_hit, prob).astype(BF16)
    for at in range(first, count, chunk):
        size = min(chunk, count - at)
        grad[at - first : at - first + size, :] = (
            scale * jnp.dot(delta[at : at + size, :], q_all[...], preferred_element_type=F32)
        ).astype(BF16)


def p_rest_kernel(chunk, temp, delta, q_all, grad):
    scale = temp[0]
    count = grad.shape[0]
    for at in range(0, count, chunk):
        size = min(chunk, count - at)
        grad[at : at + size, :] = (
            scale * jnp.dot(delta[at : at + size, :], q_all[...], preferred_element_type=F32)
        ).astype(BF16)


def q_grads_kernel(temp, delta, p_all, *outs):
    scale = temp[0]
    width = outs[0].shape[0]
    for k, out in enumerate(outs):
        out[...] = (
            scale
            * lax.dot_general(
                delta[:, k * width : (k + 1) * width],
                p_all[...],
                (((0,), (0,)), ((), ())),
                preferred_element_type=F32,
            )
        ).astype(BF16)


def add_kernel(*refs):
    out = refs[-1]
    total = refs[0][...].astype(F32)
    for ref in refs[1:-1]:
        total = total + ref[...].astype(F32)
    out[...] = total.astype(out.dtype)


def final_kernel(q_ref, p_ref, q0, q1, q2, q3, p0, p1, q_out, p_out):
    def back(src, grad, dst):
        wide = src[...].astype(F32)
        length = jnp.sqrt(jnp.sum(wide * wide, axis=1, keepdims=True))
        unit = wide / length
        along = jnp.sum(unit * grad, axis=1, keepdims=True)
        dst[...] = ((grad - unit * along) / length).astype(BF16)

    q_sum = q0[...].astype(F32) + q1[...].astype(F32) + q2[...].astype(F32) + q3[...].astype(F32)
    back(q_ref, q_sum, q_out)
    back(p_ref, p0[...].astype(F32) + p1[...].astype(F32), p_out)


def vmem(n):
    return [pl.BlockSpec(memory_space=pltpu.VMEM)] * n


def smem(n):
    return [pl.BlockSpec(memory_space=pltpu.SMEM)] * n


def call(kernel, shapes, in_specs, args, scratch=()):
    multi = isinstance(shapes, (list, tuple))
    return pl.pallas_call(
        kernel,
        out_shape=shapes,
        in_specs=in_specs,
        out_specs=vmem(len(shapes)) if multi else vmem(1)[0],
        scratch_shapes=list(scratch),
        compiler_params=pltpu.CompilerParams(vmem_limit_bytes=VMEM_LIMIT),
    )(*args)


def gather_queries(low):
    near = jnp.concatenate([low] + [inner(low, k) for k in (1, 2, 3)], axis=0)
    return [near] + [outer(near, k) for k in (1, 2, 3)]


def gather_passages(low, after):
    pair = jnp.concatenate([low, swap(low)], axis=0)
    one = along_z(pair, 1)
    two = along_z(pair, 2)
    two, one, _ = lax.optimization_barrier((two, one, after))
    three = along_z(two, 1)
    four = along_z(two[: low.shape[0]], 2)
    return [pair, one, two, three, four, swap(four), swap(one), swap(two), swap(three)]


def add(shape, dtype, *terms):
    return call(
        add_kernel, jax.ShapeDtypeStruct(shape, dtype), vmem(len(terms)), terms
    )


def scatter_queries(parts, rows):
    terms = [parts[0]] + [outer(parts[k], -k) for k in (1, 2, 3)]
    near = add(parts[0].shape, BF16, *terms)
    return [near[:rows]] + [inner(near[k * rows : (k + 1) * rows], -k) for k in (1, 2, 3)]


def scatter_passages(first, last, rows):
    pair, one, two = (first[2 * k * rows : 2 * (k + 1) * rows] for k in range(3))
    three, four, rest = last[: 2 * rows], last[2 * rows : 3 * rows], last[3 * rows :]
    crossed = swap(rest)
    four_b = crossed[:rows]
    one_b, two_b, three_b = (crossed[(2 * k + 1) * rows : (2 * k + 3) * rows] for k in range(3))
    shape = pair.shape
    three = add(shape, BF16, three, three_b)
    four = add(four.shape, BF16, four, four_b)
    from_three = along_z(three, -1)
    from_four = along_z(four, -2)
    one = add(shape, BF16, one, one_b)
    from_one = along_z(one, -1)
    zero = jnp.zeros_like(from_four)
    two = add(shape, BF16, two, two_b, from_three, jnp.concatenate([from_four, zero], axis=0))
    from_two = along_z(two, -2)
    here = add(shape, BF16, pair, from_one, from_two)
    return here[:rows], swap(here[rows:])


def local(queries, passages, positives, inv_temp):
    rows, width = queries.shape
    count = rows * 16
    zl, core, y, x, zh = (lax.axis_index(name) for name in AXES)
    z = zh * 4 + zl
    shape = jax.ShapeDtypeStruct
    q_low, p_low = call(
        norm_kernel, [shape((rows, width), BF16)] * 2, vmem(2), (queries, passages)
    )
    q_parts = gather_queries(q_low)
    p_parts = gather_passages(p_low, q_parts[0])

    near, far = jnp.arange(16) % 4, jnp.arange(16) // 4
    from_y = (y + jnp.where(core == 0, far, near)) % 4
    from_x = (x + jnp.where(core == 0, near, far)) % 4
    slots = (from_y * 4 + from_x).astype(jnp.int32)

    wanted = lax.dynamic_index_in_dim(positives.reshape(16, 2, rows), zh, 1, keepdims=False)
    wanted = wanted[slots]
    block = wanted // rows
    owner_z = (block % 2) * 4 + block // 64
    owner_core = (block // 32) % 2
    other = (owner_core != core).astype(jnp.int32)
    away = jnp.where(core == 0, owner_z - z, z - owner_z) % 8
    slot = jnp.where(
        away < 4,
        2 * away + other,
        jnp.where(away == 4, 8 + other, 10 + 2 * (7 - away) + 1 - other),
    )
    present = (block // 8) % 4 * 4 + (block // 2) % 4 == y * 4 + x
    target = jnp.where(present, slot * rows + wanted % rows, -1).reshape(4, 1, 4 * rows)
    targets = [target[k] for k in range(4)]
    temp = inv_temp.reshape(1)
    chunk = 256
    part_rows = 4 * rows

    p_all = call(join_kernel, shape((count, width), BF16), vmem(9), p_parts)

    def logits(*ks):
        out = call(
            functools.partial(logits_kernel, chunk),
            [shape((count, part_rows), BF16)] * len(ks) + [shape((8, part_rows), F32)] * len(ks),
            smem(1) + vmem(2 * len(ks) + 1),
            (temp, *(q_parts[k] for k in ks), *(targets[k] for k in ks), p_all),
            [pltpu.VMEM((count, part_rows), F32)],
        )
        return dict(zip(ks, zip(out[: len(ks)], out[len(ks) :])))

    found = {**logits(0), **logits(1, 3), **logits(2)}
    e_parts = [found[k][0] for k in range(4)]
    row_parts = [found[k][1] for k in range(4)]
    stat = call(
        functools.partial(stat_kernel, rows),
        shape((16, 17 * 128), F32),
        smem(1) + vmem(4),
        (slots, *row_parts),
    )
    stats = lax.all_to_all(stat, ("y", "x"), 0, 0, tiled=True)

    first = 6 * rows
    delta, q_all, total, pos_sum, p_last = call(
        functools.partial(p_grads_kernel, rows, chunk, first),
        [
            shape((count, count), BF16),
            shape((count, width), BF16),
            shape((1, 16 * 128), F32),
            shape((1, 128), F32),
            shape((count - first, width), BF16),
        ],
        smem(2) + vmem(17),
        (slots, temp, stats, *e_parts, *row_parts, *targets, *q_parts),
        [pltpu.VMEM((8, part_rows), F32)],
    )
    p_first = call(
        functools.partial(p_rest_kernel, chunk),
        shape((first, width), BF16),
        smem(1) + vmem(2),
        (temp, delta, q_all),
    )
    q_grads = call(
        q_grads_kernel,
        [shape((part_rows, width), BF16)] * 4,
        smem(1) + vmem(2),
        (temp, delta, p_all),
    )
    q_terms = scatter_queries(q_grads, rows)
    p_terms = scatter_passages(p_first, p_last, rows)
    mine = lax.dynamic_slice_in_dim(total[0], (y * 4 + x) * 128, rows, 0)
    query_loss = mine - pos_sum[0, :rows]
    query_grads, passage_grads = call(
        final_kernel,
        [shape((rows, width), BF16)] * 2,
        vmem(8),
        (queries, passages, *q_terms, *p_terms),
    )
    return (query_loss, query_grads, passage_grads)


def solution(mesh):
    fine = Mesh(mesh.devices.reshape(SIZES), AXES)
    return jax.shard_map(
        local,
        mesh=fine,
        in_specs=(P(AXES, None), P(AXES, None), P(("zl", "core")), P()),
        out_specs=(P(AXES), P(AXES, None), P(AXES, None)),
        check_vma=False,
    )
```

time: 119 us -> 107 us (0.90)
  starting transfers between devices: 52.6 us -> 45.9 us
  Pallas kernels: 25.7 us -> 19 us
  waiting for transfers between devices: 19 us -> 22.4 us
  blocking collectives: 13.3 us -> 11.1 us
    ppermute x30 -> x27, starting transfers between devices: 52.6 us -> 45.9 us  [fetch(): return lax.ppermute(array, AXES, pairs)]
    pallas_call x10 -> x16, Pallas kernels: 25.7 us -> 19 us  [call(): pl.pallas_call(kernel, out_shape=shapes, in_specs=in_specs, out_specs=vme...]
    ppermute x30 -> x27, waiting for transfers between devices: 19 us -> 22.4 us  [fetch(): return lax.ppermute(array, AXES, pairs)]
    all_to_all x1, blocking collectives: 13.3 us -> 11.1 us  [local(): stats = lax.all_to_all(stat, ('y', 'x'), 0, 0, tiled=True)]
    unnamed x21 -> x23, local copies, waits for them, and re-layouts: 4.32 us -> 4.96 us
  transfers between devices with their start and end apart: 30 -> 27, of which waited for: 7 -> 10; matrix products, arithmetic and copies ran while one was open for 2% -> 2% of each run, Pallas kernels for 1% -> 9%
where the time goes in v2:
time: 107 us
  starting transfers between devices  45.9 us (43%)
  waiting for transfers between devices  22.4 us (21%)
  Pallas kernels  19 us (18%)
  blocking collectives  11.1 us (10%)
  local copies, waits for them, and re-layouts  6.41 us (6%)
  between operations  1.59 us (1%)
    ppermute x27, starting transfers between devices, fetch(): return lax.ppermute(array, AXES, pairs)  45.9 us
    ppermute x27, waiting for transfers between devices, fetch(): return lax.ppermute(array, AXES, pairs)  22.4 us
    pallas_call x16, Pallas kernels, call(): pl.pallas_call(kernel, out_shape=shapes, in_specs=in_specs, out_specs=vme...  19 us
    all_to_all x1, blocking collectives, local(): stats = lax.all_to_all(stat, ('y', 'x'), 0, 0, tiled=True)  11.1 us
    unnamed x23, local copies, waits for them, and re-layouts  4.96 us
  transfers between devices with their start and end apart: 27, of which 10 were waited for; matrix products, arithmetic and copies ran while one was open for 2% of the time, Pallas kernels for 9%

profile of v2, /device:TPU:1, one launch (start us, length us, event | category | flops | bytes accessed | tf_op | source)
XLA Modules:
  0.0 107.1 jit_solution(2564204178021837796)
XLA Ops:
  0.6 0.9 copy-done
  1.5 0.9 copy-done.2
  2.6 2.2 %collective-permute-start.2 = (bf16[80,768]{1,0:T(8,128)(2,1)S(1)}, bf16[80,768]{1,0:T(8,128)(2,1)S(1)}, u32[]{:S(2)}, u32[]{:S(2)}) collective-permute-start(bf16[80,768]{1,0:T(8,128)(2,1)S(1)} %get-tuple-element.26), channel_id=1, source_target_pairs={{6,0},{0,2},{2,4},{4,6},{14,8},{8,10},{10,12},{12,14},{22,16},{16,... | collective-permute-start | bytes 368648 | tf_op jit(solution)/shard_map/ppermute | solution.py:30
  4.8 2.6 %collective-permute-start.1 = (bf16[80,768]{1,0:T(8,128)(2,1)S(1)}, bf16[80,768]{1,0:T(8,128)(2,1)S(1)}, u32[]{:S(2)}, u32[]{:S(2)}) collective-permute-start(bf16[80,768]{1,0:T(8,128)(2,1)S(1)} %get-tuple-element.26), channel_id=1, source_target_pairs={{4,0},{6,2},{0,4},{2,6},{12,8},{14,10},{8,12},{10,14},{20,16},{22,... | collective-permute-start | bytes 368648 | tf_op jit(solution)/shard_map/ppermute | solution.py:30
  7.4 1.1 collective-permute-start
  8.5 1.3 %collective-permute-start.3 = (bf16[80,768]{1,0:T(8,128)(2,1)S(1)}, bf16[80,768]{1,0:T(8,128)(2,1)S(1)}, u32[]{:S(2)}, u32[]{:S(2)}) collective-permute-start(bf16[80,768]{1,0:T(8,128)(2,1)S(1)} %get-tuple-element.27), channel_id=1, source_target_pairs={{32,0},{34,2},{36,4},{38,6},{40,8},{42,10},{44,12},{46,14},{48,16}... | collective-permute-start | bytes 368648 | tf_op jit(solution)/shard_map/ppermute | solution.py:30
  9.9 0.9 collective-permute-done.3
  10.8 1.7 %collective-permute-start.5 = (bf16[160,768]{1,0:T(8,128)(2,1)S(1)}, bf16[160,768]{1,0:T(8,128)(2,1)S(1)}, u32[]{:S(2)}, u32[]{:S(2)}) collective-permute-start(bf16[160,768]{1,0:T(8,128)(2,1)S(1)} %constant_dynamic-update-slice_fusion.4.refs_0_), channel_id=1, source_target_pairs={{64,0},{66,2},{68,4},{70,6},{72,8},{74,10},{76,12},{78,14},{80,16}... | collective-permute-start | bytes 737288 | tf_op jit(solution)/shard_map/ppermute | solution.py:30
  12.5 3.0 %collective-permute-start.4 = (bf16[160,768]{1,0:T(8,128)(2,1)S(1)}, bf16[160,768]{1,0:T(8,128)(2,1)S(1)}, u32[]{:S(2)}, u32[]{:S(2)}) collective-permute-start(bf16[160,768]{1,0:T(8,128)(2,1)S(1)} %constant_dynamic-update-slice_fusion.4.refs_0_), channel_id=1, source_target_pairs={{128,0},{130,2},{132,4},{134,6},{136,8},{138,10},{140,12},{142,14}... | collective-permute-start | bytes 737288 | tf_op jit(solution)/shard_map/ppermute | solution.py:30
  15.6 4.5 %collective-permute-done.5.refs_1_ = bf16[160,768]{1,0:T(8,128)(2,1)S(1)} collective-permute-done((bf16[160,768]{1,0:T(8,128)(2,1)S(1)}, bf16[160,768]{1,0:T(8,128)(2,1)S(1)}, u32[]{:S(2)}, u32[]{:S(2)}) %collective-permute-start.5) | collective-permute-done | bytes 245792 | tf_op jit(solution)/shard_map/ppermute | solution.py:30
  20.1 4.4 %collective-permute-done.4.refs_2_ = bf16[160,768]{1,0:T(8,128)(2,1)S(1)} collective-permute-done((bf16[160,768]{1,0:T(8,128)(2,1)S(1)}, bf16[160,768]{1,0:T(8,128)(2,1)S(1)}, u32[]{:S(2)}, u32[]{:S(2)}) %collective-permute-start.4) | collective-permute-done | bytes 245792 | tf_op jit(solution)/shard_map/ppermute | solution.py:30
  24.8 5.5 %collective-permute-done.7.refs_4_ = bf16[80,768]{1,0:T(8,128)(2,1)S(1)} collective-permute-done((bf16[80,768]{1,0:T(8,128)(2,1)S(1)}, bf16[80,768]{1,0:T(8,128)(2,1)S(1)}, u32[]{:S(2)}, u32[]{:S(2)}) %collective-permute-start.7) | collective-permute-done | bytes 122912 | tf_op jit(solution)/shard_map/ppermute | solution.py:30
  30.4 3.8 %collective-permute-start.8 = (bf16[80,768]{1,0:T(8,128)(2,1)S(1)}, bf16[80,768]{1,0:T(8,128)(2,1)S(1)}, u32[]{:S(2)}, u32[]{:S(2)}) collective-permute-start(bf16[80,768]{1,0:T(8,128)(2,1)S(1)} %collective-permute-done.7.refs_4_), channel_id=1, source_target_pairs={{32,0},{34,2},{36,4},{38,6},{40,8},{42,10},{44,12},{46,14},{48,16}... | collective-permute-start | bytes 368648 | tf_op jit(solution)/shard_map/ppermute | solution.py:30
  34.2 0.6 copy-done.4
  35.0 2.4 %collective-permute-start.9 = (bf16[160,768]{1,0:T(8,128)(2,1)S(1)}, bf16[160,768]{1,0:T(8,128)(2,1)S(1)}, u32[]{:S(2)}, u32[]{:S(2)}) collective-permute-start(bf16[160,768]{1,0:T(8,128)(2,1)S(1)} %collective-permute-done.5.refs_1_), channel_id=1, source_target_pairs={{32,0},{34,2},{36,4},{38,6},{40,8},{42,10},{44,12},{46,14},{48,16}... | collective-permute-start | bytes 737288 | tf_op jit(solution)/shard_map/ppermute | solution.py:30
  38.0 0.6 gather_fusion
  38.6 1.6 %collective-permute-start.14 = (bf16[320,768]{1,0:T(8,128)(2,1)S(1)}, bf16[320,768]{1,0:T(8,128)(2,1)S(1)}, u32[]{:S(2)}, u32[]{:S(2)}) collective-permute-start(bf16[320,768]{1,0:T(8,128)(2,1)S(1)} %constant_dynamic-update-slice_fusion.refs_0_.refs_12_), channel_id=1, source_target_pairs={{16,0},{18,2},{20,4},{22,6},{24,8},{26,10},{28,12},{30,14},{0,16},... | collective-permute-start | bytes 1474568 | tf_op jit(solution)/shard_map/ppermute | solution.py:30
  40.6 0.6 copy-done.6
  41.2 2.4 %collective-permute-start.12 = (bf16[320,768]{1,0:T(8,128)(2,1)S(1)}, bf16[320,768]{1,0:T(8,128)(2,1)S(1)}, u32[]{:S(2)}, u32[]{:S(2)}) collective-permute-start(bf16[320,768]{1,0:T(8,128)(2,1)S(1)} %constant_dynamic-update-slice_fusion.refs_0_.refs_12_), channel_id=1, source_target_pairs={{8,0},{10,2},{12,4},{14,6},{16,8},{18,10},{20,12},{22,14},{24,16},... | collective-permute-start | bytes 1474568 | tf_op jit(solution)/shard_map/ppermute | solution.py:30
  43.6 2.3 %collective-permute-start.10 = (bf16[160,768]{1,0:T(8,128)(2,1)S(1)}, bf16[160,768]{1,0:T(8,128)(2,1)S(1)}, u32[]{:S(2)}, u32[]{:S(2)}) collective-permute-start(bf16[160,768]{1,0:T(8,128)(2,1)S(1)} %collective-permute-done.4.refs_2_), channel_id=1, source_target_pairs={{32,0},{34,2},{36,4},{38,6},{40,8},{42,10},{44,12},{46,14},{48,16}... | collective-permute-start | bytes 737288 | tf_op jit(solution)/shard_map/ppermute | solution.py:30
  46.6 0.5 collective-permute-done.10.refs_7_
  47.1 0.5 collective-permute-done.11.refs_8_
  47.6 0.9 copy-done.5
  48.5 0.9 copy-done.7
  49.4 1.1 shard_map.68.refs_2_.refs_4_.p_all
  50.5 1.6 %shard_map.69 = (bf16[1280,320]{1,0:T(8,128)(2,1)S(1)}, f32[8,320]{1,0:T(8,128)S(1)}) custom-call(f32[1]{0:T(128)} %bitcast.10.temp, bf16[320,768]{1,0:T(8,128)(2,1)S(1)} %constant_dynamic-update-slice_fusion.refs_0_.refs_12_, s32[1,320]{1,0:T(1,128)S(1)} %squeeze.19.refs_1_.refs_8_, bf16[1280,768]{1,0:T(8,128)(2,1)S(1)} %shard_map.68.refs_2_.refs_4_.p_all), custom_call_target="tpu_custom_call" | custom-call | tf_op jit(solution)/shard_map/pallas_call | solution.py:199
  52.1 1.6 %shard_map.71 = (bf16[1280,320]{1,0:T(8,128)(2,1)S(1)}, f32[8,320]{1,0:T(8,128)S(1)}) custom-call(f32[1]{0:T(128)} %bitcast.12.temp, bf16[320,768]{1,0:T(8,128)(2,1)S(1)} %collective-permute-done.14.refs_0_.refs_14_, s32[1,320]{1,0:T(1,128)S(1)} %squeeze.22.refs_1_.refs_10_, bf16[1280,768]{1,0:T(8,128)(2,1)S(1)} %shard_map.68.refs_2_.refs_4_.p_all), custom_call_target="tpu_custom_call" | custom-call | tf_op jit(solution)/shard_map/pallas_call | solution.py:199
  53.7 2.8 %shard_map.70 = (bf16[1280,320]{1,0:T(8,128)(2,1)S(1)}, bf16[1280,320]{1,0:T(8,128)(2,1)S(1)}, f32[8,320]{1,0:T(8,128)S(1)}, f32[8,320]{1,0:T(8,128)S(1)}) custom-call(f32[1]{0:T(128)} %bitcast.11.temp, bf16[320,768]{1,0:T(8,128)(2,1)S(1)} %collective-permute-done.12.refs_0_.refs_13_, bf16[320,768]{1,0:T(8,128)(2,1)S(1)} %collective-permute-done.13.refs_1_.refs_15_, ...), custom_call_target="tpu_custom_call" | custom-call | tf_op jit(solution)/shard_map/pallas_call | solution.py:199
  56.5 1.6 %shard_map.72 = f32[16,2176]{1,0:T(8,128)S(1)} custom-call(s32[16]{0:T(128)S(1)} %fusion.25.slots, f32[8,320]{1,0:T(8,128)S(1)} %get-tuple-element.30.refs_0_.refs_4_, f32[8,320]{1,0:T(8,128)S(1)} %get-tuple-element.31.refs_1_.refs_5_, f32[8,320]{1,0:T(8,128)S(1)} %get-tuple-element.32.refs_2_.refs_6_, f32[8,320]{1,0:T(8,128)S(1)} %get-tuple-element.33.refs_3_.refs_7_), custom_call_target="tpu_custom_call" | custom-call | tf_op jit(solution)/shard_map/pallas_call | solution.py:199
  58.3 11.1 %all_to_all.11 = f32[16,1,2176]{2,1,0:T(1,128)S(1)} all-to-all(f32[16,1,2176]{2,1,0:T(1,128)S(1)} %copy.7), channel_id=1, replica_groups=mesh['zl'=4,'core'=2,'y'=4,'x'=4,'zh'=2] {'y','x'}, dimensions={0} | all-to-all | bytes 278528 | tf_op jit(solution)/shard_map/all_to_all | solution.py:313
  69.4 3.7 %shard_map.73 = (bf16[1280,1280]{1,0:T(8,128)(2,1)S(1)}, bf16[1280,768]{1,0:T(8,128)(2,1)S(1)}, f32[1,2048]{1,0:T(1,128)S(1)}, f32[1,128]{1,0:T(1,128)S(1)}, bf16[800,768]{1,0:T(8,128)(2,1)S(1)}) custom-call(s32[16]{0:T(128)S(1)} %fusion.25.slots, f32[1]{0:T(128)} %bitcast.13.temp, f32[16,2176]{1,0:T(8,128)S(1)} %bitcast.16, ...), custom_call_target="tpu_custom_call" | custom-call | tf_op jit(solution)/shard_map/pallas_call | solution.py:199
  73.1 2.1 %collective-permute-start.21 = (bf16[560,768]{1,0:T(8,128)(2,1)S(1)}, bf16[560,768]{1,0:T(8,128)(2,1)S(1)}, u32[]{:S(2)}, u32[]{:S(2)}) collective-permute-start(bf16[560,768]{1,0:T(8,128)(2,1)S(1)} %slice.82), channel_id=1, source_target_pairs={{32,0},{34,2},{36,4},{38,6},{40,8},{42,10},{44,12},{46,14},{48,16}... | collective-permute-start | bytes 2580488 | tf_op jit(solution)/shard_map/ppermute | solution.py:30
  75.3 3.9 %shard_map.74 = (bf16[320,768]{1,0:T(8,128)(2,1)S(1)}, bf16[320,768]{1,0:T(8,128)(2,1)}, bf16[320,768]{1,0:T(8,128)(2,1)}, bf16[320,768]{1,0:T(8,128)(2,1)}) custom-call(f32[1]{0:T(128)} %bitcast.14.temp, bf16[1280,1280]{1,0:T(8,128)(2,1)S(1)} %get-tuple-element.40.delta, bf16[1280,768]{1,0:T(8,128)(2,1)S(1)} %shard_map.68.refs_2_.refs_4_.p_all), custom_call_target="tpu_custom_call" | custom-call | tf_op jit(solution)/shard_map/pallas_call | solution.py:199
  79.5 1.5 %collective-permute-start.16 = (bf16[320,768]{1,0:T(8,128)(2,1)}, bf16[320,768]{1,0:T(8,128)(2,1)S(1)}, u32[]{:S(2)}, u32[]{:S(2)}) collective-permute-start(bf16[320,768]{1,0:T(8,128)(2,1)} %get-tuple-element.43), channel_id=1, source_target_pairs={{16,0},{18,2},{20,4},{22,6},{24,8},{26,10},{28,12},{30,14},{0,16},... | collective-permute-start | bytes 1474568 | tf_op jit(solution)/shard_map/ppermute | solution.py:30
  81.0 1.2 %collective-permute-start.17 = (bf16[320,768]{1,0:T(8,128)(2,1)}, bf16[320,768]{1,0:T(8,128)(2,1)S(1)}, u32[]{:S(2)}, u32[]{:S(2)}) collective-permute-start(bf16[320,768]{1,0:T(8,128)(2,1)} %get-tuple-element.44), channel_id=1, source_target_pairs={{8,0},{10,2},{12,4},{14,6},{16,8},{18,10},{20,12},{22,14},{24,16},... | collective-permute-start | bytes 1474568 | tf_op jit(solution)/shard_map/ppermute | solution.py:30
  82.2 1.1 %shard_map.76 = bf16[480,768]{1,0:T(8,128)(2,1)S(1)} custom-call(f32[1]{0:T(128)} %bitcast.15.temp, bf16[1280,1280]{1,0:T(8,128)(2,1)S(1)} %get-tuple-element.40.delta, bf16[1280,768]{1,0:T(8,128)(2,1)S(1)} %get-tuple-element.45.q_all), custom_call_target="tpu_custom_call" | custom-call | tf_op jit(solution)/shard_map/pallas_call | solution.py:199
  83.4 2.5 %collective-permute-start.24 = (bf16[80,768]{1,0:T(8,128)(2,1)S(1)}, bf16[80,768]{1,0:T(8,128)(2,1)S(1)}, u32[]{:S(2)}, u32[]{:S(2)}) collective-permute-start(bf16[80,768]{1,0:T(8,128)(2,1)S(1)} %shard_map.79), channel_id=1, source_target_pairs={{129,0},{131,2},{133,4},{135,6},{137,8},{139,10},{141,12},{143,14}... | collective-permute-start | bytes 368648 | tf_op jit(solution)/shard_map/ppermute | solution.py:30
  86.0 1.4 %collective-permute-start.23 = (bf16[160,768]{1,0:T(8,128)(2,1)S(1)}, bf16[160,768]{1,0:T(8,128)(2,1)S(1)}, u32[]{:S(2)}, u32[]{:S(2)}) collective-permute-start(bf16[160,768]{1,0:T(8,128)(2,1)S(1)} %shard_map.78), channel_id=1, source_target_pairs={{193,0},{195,2},{197,4},{199,6},{201,8},{203,10},{205,12},{207,14}... | collective-permute-start | bytes 737288 | tf_op jit(solution)/shard_map/ppermute | solution.py:30
  87.6 1.7 %collective-permute-done.24 = bf16[80,768]{1,0:T(8,128)(2,1)S(1)} collective-permute-done((bf16[80,768]{1,0:T(8,128)(2,1)S(1)}, bf16[80,768]{1,0:T(8,128)(2,1)S(1)}, u32[]{:S(2)}, u32[]{:S(2)}) %collective-permute-start.24) | collective-permute-done | bytes 122912 | tf_op jit(solution)/shard_map/ppermute | solution.py:30
  89.3 3.8 %collective-permute-start.22 = (bf16[160,768]{1,0:T(8,128)(2,1)S(1)}, bf16[160,768]{1,0:T(8,128)(2,1)S(1)}, u32[]{:S(2)}, u32[]{:S(2)}) collective-permute-start(bf16[160,768]{1,0:T(8,128)(2,1)S(1)} %shard_map.77), channel_id=1, source_target_pairs={{193,0},{195,2},{197,4},{199,6},{201,8},{203,10},{205,12},{207,14}... | collective-permute-start | bytes 737288 | tf_op jit(solution)/shard_map/ppermute | solution.py:30
  93.4 1.8 %collective-permute-start.25 = (bf16[160,768]{1,0:T(8,128)(2,1)S(1)}, bf16[160,768]{1,0:T(8,128)(2,1)S(1)}, u32[]{:S(2)}, u32[]{:S(2)}) collective-permute-start(bf16[160,768]{1,0:T(8,128)(2,1)S(1)} %shard_map.80), channel_id=1, source_target_pairs={{129,0},{131,2},{133,4},{135,6},{137,8},{139,10},{141,12},{143,14}... | collective-permute-start | bytes 737288 | tf_op jit(solution)/shard_map/ppermute | solution.py:30
  95.5 1.0 collective-permute-start.20
  96.5 1.2 %collective-permute-start.19 = (bf16[80,768]{1,0:T(8,128)(2,1)S(1)}, bf16[80,768]{1,0:T(8,128)(2,1)S(1)}, u32[]{:S(2)}, u32[]{:S(2)}) collective-permute-start(bf16[80,768]{1,0:T(8,128)(2,1)S(1)} %get-tuple-element.56), channel_id=1, source_target_pairs={{4,0},{6,2},{0,4},{2,6},{12,8},{14,10},{8,12},{10,14},{20,16},{22,... | collective-permute-start | bytes 368648 | tf_op jit(solution)/shard_map/ppermute | solution.py:30
  97.7 3.7 %collective-permute-done.25.refs_2_ = bf16[160,768]{1,0:T(8,128)(2,1)S(1)} collective-permute-done((bf16[160,768]{1,0:T(8,128)(2,1)S(1)}, bf16[160,768]{1,0:T(8,128)(2,1)S(1)}, u32[]{:S(2)}, u32[]{:S(2)}) %collective-permute-start.25) | collective-permute-done | bytes 245792 | tf_op jit(solution)/shard_map/ppermute | solution.py:30
  101.5 3.7 %collective-permute-start.26 = (bf16[80,768]{1,0:T(8,128)(2,1)S(1)}, bf16[80,768]{1,0:T(8,128)(2,1)S(1)}, u32[]{:S(2)}, u32[]{:S(2)}) collective-permute-start(bf16[80,768]{1,0:T(8,128)(2,1)S(1)} %get-tuple-element.59), channel_id=1, source_target_pairs={{32,0},{34,2},{36,4},{38,6},{40,8},{42,10},{44,12},{46,14},{48,16}... | collective-permute-start | bytes 368648 | tf_op jit(solution)/shard_map/ppermute | solution.py:30
  105.2 0.6 subtract_bitcast_fusion
  105.8 0.4 collective-permute-done.26.p1
  106.1 0.9 shard_map.82
  (72 shorter events, 3.4 us)
Async XLA Ops:
  0.6 0.9 copy-start
  1.5 0.9 copy-start.2
  2.4 22.3 %copy-start.8 = (s32[2560]{0:T(1024)S(1)}, s32[2560]{0:T(1024)}, u32[]{:S(2)}) copy-start(s32[2560]{0:T(1024)} %param.6) | copy-start | bytes 30724
  2.6 13.0 %collective-permute-start.2 = (bf16[80,768]{1,0:T(8,128)(2,1)S(1)}, bf16[80,768]{1,0:T(8,128)(2,1)S(1)}, u32[]{:S(2)}, u32[]{:S(2)}) collective-permute-start(bf16[80,768]{1,0:T(8,128)(2,1)S(1)} %get-tuple-element.26), channel_id=1, source_target_pairs={{6,0},{0,2},{2,4},{4,6},{14,8},{8,10},{10,12},{12,14},{22,16},{16,... | collective-permute-start | bytes 368648 | tf_op jit(solution)/shard_map/ppermute | solution.py:30
  4.8 10.7 %collective-permute-start.1 = (bf16[80,768]{1,0:T(8,128)(2,1)S(1)}, bf16[80,768]{1,0:T(8,128)(2,1)S(1)}, u32[]{:S(2)}, u32[]{:S(2)}) collective-permute-start(bf16[80,768]{1,0:T(8,128)(2,1)S(1)} %get-tuple-element.26), channel_id=1, source_target_pairs={{4,0},{6,2},{0,4},{2,6},{12,8},{14,10},{8,12},{10,14},{20,16},{22,... | collective-permute-start | bytes 368648 | tf_op jit(solution)/shard_map/ppermute | solution.py:30
  7.4 8.1 %collective-permute-start = (bf16[80,768]{1,0:T(8,128)(2,1)S(1)}, bf16[80,768]{1,0:T(8,128)(2,1)S(1)}, u32[]{:S(2)}, u32[]{:S(2)}) collective-permute-start(bf16[80,768]{1,0:T(8,128)(2,1)S(1)} %get-tuple-element.26), channel_id=1, source_target_pairs={{2,0},{4,2},{6,4},{0,6},{10,8},{12,10},{14,12},{8,14},{18,16},{20,... | collective-permute-start | bytes 368648 | tf_op jit(solution)/shard_map/ppermute | solution.py:30
  8.5 2.3 %collective-permute-start.3 = (bf16[80,768]{1,0:T(8,128)(2,1)S(1)}, bf16[80,768]{1,0:T(8,128)(2,1)S(1)}, u32[]{:S(2)}, u32[]{:S(2)}) collective-permute-start(bf16[80,768]{1,0:T(8,128)(2,1)S(1)} %get-tuple-element.27), channel_id=1, source_target_pairs={{32,0},{34,2},{36,4},{38,6},{40,8},{42,10},{44,12},{46,14},{48,16}... | collective-permute-start | bytes 368648 | tf_op jit(solution)/shard_map/ppermute | solution.py:30
  10.8 9.2 %collective-permute-start.5 = (bf16[160,768]{1,0:T(8,128)(2,1)S(1)}, bf16[160,768]{1,0:T(8,128)(2,1)S(1)}, u32[]{:S(2)}, u32[]{:S(2)}) collective-permute-start(bf16[160,768]{1,0:T(8,128)(2,1)S(1)} %constant_dynamic-update-slice_fusion.4.refs_0_), channel_id=1, source_target_pairs={{64,0},{66,2},{68,4},{70,6},{72,8},{74,10},{76,12},{78,14},{80,16}... | collective-permute-start | bytes 737288 | tf_op jit(solution)/shard_map/ppermute | solution.py:30
  12.5 11.9 %collective-permute-start.4 = (bf16[160,768]{1,0:T(8,128)(2,1)S(1)}, bf16[160,768]{1,0:T(8,128)(2,1)S(1)}, u32[]{:S(2)}, u32[]{:S(2)}) collective-permute-start(bf16[160,768]{1,0:T(8,128)(2,1)S(1)} %constant_dynamic-update-slice_fusion.4.refs_0_), channel_id=1, source_target_pairs={{128,0},{130,2},{132,4},{134,6},{136,8},{138,10},{140,12},{142,14}... | collective-permute-start | bytes 737288 | tf_op jit(solution)/shard_map/ppermute | solution.py:30
  24.4 6.0 %collective-permute-start.7 = (bf16[80,768]{1,0:T(8,128)(2,1)S(1)}, bf16[80,768]{1,0:T(8,128)(2,1)S(1)}, u32[]{:S(2)}, u32[]{:S(2)}) collective-permute-start(bf16[80,768]{1,0:T(8,128)(2,1)S(1)} %slice.71), channel_id=1, source_target_pairs={{128,0},{130,2},{132,4},{134,6},{136,8},{138,10},{140,12},{142,14}... | collective-permute-start | bytes 368648 | tf_op jit(solution)/shard_map/ppermute | solution.py:30
  30.4 10.2 %collective-permute-start.8 = (bf16[80,768]{1,0:T(8,128)(2,1)S(1)}, bf16[80,768]{1,0:T(8,128)(2,1)S(1)}, u32[]{:S(2)}, u32[]{:S(2)}) collective-permute-start(bf16[80,768]{1,0:T(8,128)(2,1)S(1)} %collective-permute-done.7.refs_4_), channel_id=1, source_target_pairs={{32,0},{34,2},{36,4},{38,6},{40,8},{42,10},{44,12},{46,14},{48,16}... | collective-permute-start | bytes 368648 | tf_op jit(solution)/shard_map/ppermute | solution.py:30
  34.2 0.6 copy-start.4
  34.9 11.1 %collective-permute-start.6 = (bf16[160,768]{1,0:T(8,128)(2,1)S(1)}, bf16[160,768]{1,0:T(8,128)(2,1)S(1)}, u32[]{:S(2)}, u32[]{:S(2)}) collective-permute-start(bf16[160,768]{1,0:T(8,128)(2,1)S(1)} %collective-permute-done.4.refs_2_), channel_id=1, source_target_pairs={{64,0},{66,2},{68,4},{70,6},{72,8},{74,10},{76,12},{78,14},{80,16}... | collective-permute-start | bytes 737288 | tf_op jit(solution)/shard_map/ppermute | solution.py:30
  35.0 8.7 %collective-permute-start.9 = (bf16[160,768]{1,0:T(8,128)(2,1)S(1)}, bf16[160,768]{1,0:T(8,128)(2,1)S(1)}, u32[]{:S(2)}, u32[]{:S(2)}) collective-permute-start(bf16[160,768]{1,0:T(8,128)(2,1)S(1)} %collective-permute-done.5.refs_1_), channel_id=1, source_target_pairs={{32,0},{34,2},{36,4},{38,6},{40,8},{42,10},{44,12},{46,14},{48,16}... | collective-permute-start | bytes 737288 | tf_op jit(solution)/shard_map/ppermute | solution.py:30
  38.6 13.5 %collective-permute-start.14 = (bf16[320,768]{1,0:T(8,128)(2,1)S(1)}, bf16[320,768]{1,0:T(8,128)(2,1)S(1)}, u32[]{:S(2)}, u32[]{:S(2)}) collective-permute-start(bf16[320,768]{1,0:T(8,128)(2,1)S(1)} %constant_dynamic-update-slice_fusion.refs_0_.refs_12_), channel_id=1, source_target_pairs={{16,0},{18,2},{20,4},{22,6},{24,8},{26,10},{28,12},{30,14},{0,16},... | collective-permute-start | bytes 1474568 | tf_op jit(solution)/shard_map/ppermute | solution.py:30
  40.2 13.5 %collective-permute-start.13 = (bf16[320,768]{1,0:T(8,128)(2,1)S(1)}, bf16[320,768]{1,0:T(8,128)(2,1)S(1)}, u32[]{:S(2)}, u32[]{:S(2)}) collective-permute-start(bf16[320,768]{1,0:T(8,128)(2,1)S(1)} %constant_dynamic-update-slice_fusion.refs_0_.refs_12_), channel_id=1, source_target_pairs={{24,0},{26,2},{28,4},{30,6},{0,8},{2,10},{4,12},{6,14},{8,16},{10,... | collective-permute-start | bytes 1474568 | tf_op jit(solution)/shard_map/ppermute | solution.py:30
  40.6 0.6 copy-start.6
  41.2 12.5 %collective-permute-start.12 = (bf16[320,768]{1,0:T(8,128)(2,1)S(1)}, bf16[320,768]{1,0:T(8,128)(2,1)S(1)}, u32[]{:S(2)}, u32[]{:S(2)}) collective-permute-start(bf16[320,768]{1,0:T(8,128)(2,1)S(1)} %constant_dynamic-update-slice_fusion.refs_0_.refs_12_), channel_id=1, source_target_pairs={{8,0},{10,2},{12,4},{14,6},{16,8},{18,10},{20,12},{22,14},{24,16},... | collective-permute-start | bytes 1474568 | tf_op jit(solution)/shard_map/ppermute | solution.py:30
  43.6 3.4 %collective-permute-start.10 = (bf16[160,768]{1,0:T(8,128)(2,1)S(1)}, bf16[160,768]{1,0:T(8,128)(2,1)S(1)}, u32[]{:S(2)}, u32[]{:S(2)}) collective-permute-start(bf16[160,768]{1,0:T(8,128)(2,1)S(1)} %collective-permute-done.4.refs_2_), channel_id=1, source_target_pairs={{32,0},{34,2},{36,4},{38,6},{40,8},{42,10},{44,12},{46,14},{48,16}... | collective-permute-start | bytes 737288 | tf_op jit(solution)/shard_map/ppermute | solution.py:30
  46.0 1.6 %collective-permute-start.11 = (bf16[160,768]{1,0:T(8,128)(2,1)S(1)}, bf16[160,768]{1,0:T(8,128)(2,1)}, u32[]{:S(2)}, u32[]{:S(2)}) collective-permute-start(bf16[160,768]{1,0:T(8,128)(2,1)S(1)} %collective-permute-done.6.refs_3_), channel_id=1, source_target_pairs={{32,0},{34,2},{36,4},{38,6},{40,8},{42,10},{44,12},{46,14},{48,16}... | collective-permute-start | bytes 737288 | tf_op jit(solution)/shard_map/ppermute | solution.py:30
  47.6 0.9 copy-start.5
  48.5 0.9 copy-start.7
  73.1 10.2 %collective-permute-start.21 = (bf16[560,768]{1,0:T(8,128)(2,1)S(1)}, bf16[560,768]{1,0:T(8,128)(2,1)S(1)}, u32[]{:S(2)}, u32[]{:S(2)}) collective-permute-start(bf16[560,768]{1,0:T(8,128)(2,1)S(1)} %slice.82), channel_id=1, source_target_pairs={{32,0},{34,2},{36,4},{38,6},{40,8},{42,10},{44,12},{46,14},{48,16}... | collective-permute-start | bytes 2580488 | tf_op jit(solution)/shard_map/ppermute | solution.py:30
  79.2 16.0 %collective-permute-start.15 = (bf16[320,768]{1,0:T(8,128)(2,1)}, bf16[320,768]{1,0:T(8,128)(2,1)S(1)}, u32[]{:S(2)}, u32[]{:S(2)}) collective-permute-start(bf16[320,768]{1,0:T(8,128)(2,1)} %get-tuple-element.42), channel_id=1, source_target_pairs={{24,0},{26,2},{28,4},{30,6},{0,8},{2,10},{4,12},{6,14},{8,16},{10,... | collective-permute-start | bytes 1474568 | tf_op jit(solution)/shard_map/ppermute | solution.py:30
  79.5 15.7 %collective-permute-start.16 = (bf16[320,768]{1,0:T(8,128)(2,1)}, bf16[320,768]{1,0:T(8,128)(2,1)S(1)}, u32[]{:S(2)}, u32[]{:S(2)}) collective-permute-start(bf16[320,768]{1,0:T(8,128)(2,1)} %get-tuple-element.43), channel_id=1, source_target_pairs={{16,0},{18,2},{20,4},{22,6},{24,8},{26,10},{28,12},{30,14},{0,16},... | collective-permute-start | bytes 1474568 | tf_op jit(solution)/shard_map/ppermute | solution.py:30
  81.0 14.2 %collective-permute-start.17 = (bf16[320,768]{1,0:T(8,128)(2,1)}, bf16[320,768]{1,0:T(8,128)(2,1)S(1)}, u32[]{:S(2)}, u32[]{:S(2)}) collective-permute-start(bf16[320,768]{1,0:T(8,128)(2,1)} %get-tuple-element.44), channel_id=1, source_target_pairs={{8,0},{10,2},{12,4},{14,6},{16,8},{18,10},{20,12},{22,14},{24,16},... | collective-permute-start | bytes 1474568 | tf_op jit(solution)/shard_map/ppermute | solution.py:30
  83.4 5.9 %collective-permute-start.24 = (bf16[80,768]{1,0:T(8,128)(2,1)S(1)}, bf16[80,768]{1,0:T(8,128)(2,1)S(1)}, u32[]{:S(2)}, u32[]{:S(2)}) collective-permute-start(bf16[80,768]{1,0:T(8,128)(2,1)S(1)} %shard_map.79), channel_id=1, source_target_pairs={{129,0},{131,2},{133,4},{135,6},{137,8},{139,10},{141,12},{143,14}... | collective-permute-start | bytes 368648 | tf_op jit(solution)/shard_map/ppermute | solution.py:30
  86.0 7.3 %collective-permute-start.23 = (bf16[160,768]{1,0:T(8,128)(2,1)S(1)}, bf16[160,768]{1,0:T(8,128)(2,1)S(1)}, u32[]{:S(2)}, u32[]{:S(2)}) collective-permute-start(bf16[160,768]{1,0:T(8,128)(2,1)S(1)} %shard_map.78), channel_id=1, source_target_pairs={{193,0},{195,2},{197,4},{199,6},{201,8},{203,10},{205,12},{207,14}... | collective-permute-start | bytes 737288 | tf_op jit(solution)/shard_map/ppermute | solution.py:30
  89.3 8.4 %collective-permute-start.22 = (bf16[160,768]{1,0:T(8,128)(2,1)S(1)}, bf16[160,768]{1,0:T(8,128)(2,1)S(1)}, u32[]{:S(2)}, u32[]{:S(2)}) collective-permute-start(bf16[160,768]{1,0:T(8,128)(2,1)S(1)} %shard_map.77), channel_id=1, source_target_pairs={{193,0},{195,2},{197,4},{199,6},{201,8},{203,10},{205,12},{207,14}... | collective-permute-start | bytes 737288 | tf_op jit(solution)/shard_map/ppermute | solution.py:30
  93.4 7.9 %collective-permute-start.25 = (bf16[160,768]{1,0:T(8,128)(2,1)S(1)}, bf16[160,768]{1,0:T(8,128)(2,1)S(1)}, u32[]{:S(2)}, u32[]{:S(2)}) collective-permute-start(bf16[160,768]{1,0:T(8,128)(2,1)S(1)} %shard_map.80), channel_id=1, source_target_pairs={{129,0},{131,2},{133,4},{135,6},{137,8},{139,10},{141,12},{143,14}... | collective-permute-start | bytes 737288 | tf_op jit(solution)/shard_map/ppermute | solution.py:30
  95.2 11.0 %copy-start.1 = (bf16[80,768]{1,0:T(8,128)(2,1)S(1)}, bf16[80,768]{1,0:T(8,128)(2,1)}, u32[]{:S(2)}) copy-start(bf16[80,768]{1,0:T(8,128)(2,1)} %q_ref.3) | copy-start | bytes 368644
  95.2 10.9 %copy-start.3 = (bf16[80,768]{1,0:T(8,128)(2,1)S(1)}, bf16[80,768]{1,0:T(8,128)(2,1)}, u32[]{:S(2)}) copy-start(bf16[80,768]{1,0:T(8,128)(2,1)} %p_ref.3) | copy-start | bytes 368644
  95.5 10.2 %collective-permute-start.20 = (bf16[80,768]{1,0:T(8,128)(2,1)S(1)}, bf16[80,768]{1,0:T(8,128)(2,1)S(1)}, u32[]{:S(2)}, u32[]{:S(2)}) collective-permute-start(bf16[80,768]{1,0:T(8,128)(2,1)S(1)} %get-tuple-element.55), channel_id=1, source_target_pairs={{2,0},{4,2},{6,4},{0,6},{10,8},{12,10},{14,12},{8,14},{18,16},{20,... | collective-permute-start | bytes 368648 | tf_op jit(solution)/shard_map/ppermute | solution.py:30
  96.5 9.3 %collective-permute-start.19 = (bf16[80,768]{1,0:T(8,128)(2,1)S(1)}, bf16[80,768]{1,0:T(8,128)(2,1)S(1)}, u32[]{:S(2)}, u32[]{:S(2)}) collective-permute-start(bf16[80,768]{1,0:T(8,128)(2,1)S(1)} %get-tuple-element.56), channel_id=1, source_target_pairs={{4,0},{6,2},{0,4},{2,6},{12,8},{14,10},{8,12},{10,14},{20,16},{22,... | collective-permute-start | bytes 368648 | tf_op jit(solution)/shard_map/ppermute | solution.py:30
  97.7 8.1 %collective-permute-start.18 = (bf16[80,768]{1,0:T(8,128)(2,1)S(1)}, bf16[80,768]{1,0:T(8,128)(2,1)S(1)}, u32[]{:S(2)}, u32[]{:S(2)}) collective-permute-start(bf16[80,768]{1,0:T(8,128)(2,1)S(1)} %get-tuple-element.57), channel_id=1, source_target_pairs={{6,0},{0,2},{2,4},{4,6},{14,8},{8,10},{10,12},{12,14},{22,16},{16,... | collective-permute-start | bytes 368648 | tf_op jit(solution)/shard_map/ppermute | solution.py:30
  101.5 4.7 %collective-permute-start.26 = (bf16[80,768]{1,0:T(8,128)(2,1)S(1)}, bf16[80,768]{1,0:T(8,128)(2,1)S(1)}, u32[]{:S(2)}, u32[]{:S(2)}) collective-permute-start(bf16[80,768]{1,0:T(8,128)(2,1)S(1)} %get-tuple-element.59), channel_id=1, source_target_pairs={{32,0},{34,2},{36,4},{38,6},{40,8},{42,10},{44,12},{46,14},{48,16}... | collective-permute-start | bytes 368648 | tf_op jit(solution)/shard_map/ppermute | solution.py:30

commit v3 on v2

v3 whole, which is shorter than its diff:
```python
import functools

import jax
import jax.numpy as jnp
from jax import lax
from jax.experimental import pallas as pl
from jax.experimental.pallas import tpu as pltpu
from jax.sharding import Mesh
from jax.sharding import PartitionSpec as P

AXES = ("zl", "core", "y", "x", "zh")
SIZES = (4, 2, 4, 4, 2)
VMEM_LIMIT = 24 * 2**20
F32 = jnp.float32
BF16 = jnp.bfloat16


def device_at(z, core, y, x):
    z, y, x = z % 8, y % 4, x % 4
    return ((((z % 4) * 2 + core) * 4 + y) * 4 + x) * 2 + z // 4


def fetch(array, source):
    pairs = []
    for z in range(8):
        for core in range(2):
            for y in range(4):
                for x in range(4):
                    pairs.append((device_at(*source(z, core, y, x)), device_at(z, core, y, x)))
    return lax.ppermute(array, AXES, pairs)


def swap(array):
    return fetch(array, lambda z, c, y, x: (z, 1 - c, y, x))


def along_z(array, k):
    return fetch(array, lambda z, c, y, x: (z + (k if c == 0 else -k), c, y, x))


def inner(array, k):
    return fetch(array, lambda z, c, y, x: (z, c, y, x + k) if c == 0 else (z, c, y + k, x))


def outer(array, k):
    return fetch(array, lambda z, c, y, x: (z, c, y + k, x) if c == 0 else (z, c, y, x + k))


def place():
    return tuple(lax.axis_index(name) for name in AXES)


def slot_of(k, b):
    _, core, y, x, _ = place()
    step_y = jnp.where(core == 0, k, b)
    step_x = jnp.where(core == 0, b, k)
    return lax.rem(y + step_y, 4) * 4 + lax.rem(x + step_x, 4)


def norm_kernel(q_ref, p_ref, q_low, p_low, q_buf, p_buf, sems):
    copies = [
        pltpu.make_async_copy(src, buf, sems.at[i])
        for i, (src, buf) in enumerate(((q_ref, q_buf), (p_ref, p_buf)))
    ]
    for copy in copies:
        copy.start()
    for copy, buf, dst in zip(copies, (q_buf, p_buf), (q_low, p_low)):
        copy.wait()
        wide = buf[...].astype(F32)
        length = jnp.sqrt(jnp.sum(wide * wide, axis=1, keepdims=True))
        dst[...] = (wide / length).astype(BF16)


def target_kernel(rows, positives, *outs):
    zl, core, y, x, zh = place()
    z = zh * 4 + zl
    for k, out in enumerate(outs):
        for b in range(4):
            wanted = positives[pl.ds(slot_of(k, b) * 2 + zh, 1), :]
            block = lax.div(wanted, rows)
            owner_z = lax.rem(block, 2) * 4 + lax.div(block, 64)
            other = (lax.rem(lax.div(block, 32), 2) != core).astype(jnp.int32)
            away = lax.rem(jnp.where(core == 0, owner_z - z, z - owner_z) + 8, 8)
            slot = jnp.where(
                away < 4,
                2 * away + other,
                jnp.where(away == 4, 8 + other, 10 + 2 * (7 - away) + 1 - other),
            )
            owner = lax.rem(lax.div(block, 8), 4) * 4 + lax.rem(lax.div(block, 2), 4)
            row = slot * rows + lax.rem(wanted, rows)
            out[:, b * rows : (b + 1) * rows] = jnp.where(owner == y * 4 + x, row, -1)


def logits_kernel(chunk, temp, *refs):
    parts = (len(refs) - 2) // 4
    q_parts, targets, p_all = refs[:parts], refs[parts : 2 * parts], refs[2 * parts]
    e_outs, row_outs = refs[2 * parts + 1 : 3 * parts + 1], refs[3 * parts + 1 : 4 * parts + 1]
    logits = refs[-1]
    count = p_all.shape[0]
    scale = temp[0]
    for q, target, e_out, row_out in zip(q_parts, targets, e_outs, row_outs):
        tops = []
        for at in range(0, count, chunk):
            part = slice(at, at + chunk)
            values = scale * lax.dot_general(
                p_all[part, :], q[...], (((1,), (1,)), ((), ())), preferred_element_type=F32
            )
            logits[part, :] = values
            tops.append(jnp.max(values, axis=0, keepdims=True))
        top = functools.reduce(jnp.maximum, tops)
        total = jnp.zeros_like(top)
        positive = jnp.zeros_like(top)
        for at in range(0, count, chunk):
            part = slice(at, at + chunk)
            values = logits[part, :]
            hit = lax.broadcasted_iota(jnp.int32, values.shape, 0) + at == target[...]
            positive = positive + jnp.sum(jnp.where(hit, values, 0.0), axis=0, keepdims=True)
            e = jnp.exp(values - top)
            total = total + jnp.sum(e, axis=0, keepdims=True)
            e_out[part, :] = e.astype(BF16)
        row_out[0:1, :] = top
        row_out[1:2, :] = top + jnp.log(total)
        row_out[2:3, :] = positive


def join_kernel(*refs):
    out = refs[-1]
    at = 0
    for part in refs[:-1]:
        size = min(part.shape[0], out.shape[0] - at)
        out[at : at + size, :] = part[:size, :]
        at += size


def stat_kernel(rows, *refs):
    stat = refs[-1]
    stat[...] = jnp.zeros_like(stat)
    positive = jnp.zeros((16, rows), F32)
    dest = lax.broadcasted_iota(jnp.int32, (16, rows), 0)
    for k, part in enumerate(refs[:-1]):
        for b in range(4):
            slot = slot_of(k, b)
            lanes = slice(b * rows, (b + 1) * rows)
            stat[:, pl.ds(pl.multiple_of(slot * 128, 128), rows)] = jnp.broadcast_to(
                part[1:2, lanes], (16, rows)
            )
            positive = jnp.where(dest == slot, part[2:3, lanes], positive)
    stat[:, 2048 : 2048 + rows] = positive


def delta_kernel(rows, chunk, stat, *refs):
    e_parts, row_parts, targets, deltas = refs[:4], refs[4:8], refs[8:12], refs[12:16]
    loss, totals, lane = refs[16:]
    count = e_parts[0].shape[0]
    sums = stat[:, :2048]
    top = jnp.max(sums, axis=0, keepdims=True)
    totals[0:1, :] = top + jnp.log(jnp.sum(jnp.exp(sums - top), axis=0, keepdims=True))
    own = totals[0:1, pl.ds(pl.multiple_of(slot_of(0, 0) * 128, 128), rows)]
    loss[...] = own - jnp.sum(stat[:, 2048:], axis=0, keepdims=True)[:, :rows]
    for k in range(4):
        for b in range(4):
            lane[k : k + 1, b * rows : (b + 1) * rows] = totals[
                0:1, pl.ds(pl.multiple_of(slot_of(k, b) * 128, 128), rows)
            ]
    for k in range(4):
        total = lane[k : k + 1, :]
        factor = jnp.exp(row_parts[k][0:1, :] - total)
        at_hit = jnp.exp(row_parts[k][2:3, :] - total) - 1.0
        for at in range(0, count, chunk):
            part = slice(at, at + chunk)
            prob = e_parts[k][part, :].astype(F32) * factor
            hit = lax.broadcasted_iota(jnp.int32, prob.shape, 0) + at == targets[k][...]
            deltas[k][part, :] = jnp.where(hit, at_hit, prob).astype(BF16)


def p_grads_kernel(first, temp, *refs):
    deltas, q_parts, outs = refs[:4], refs[4:8], refs[8:]
    at = first
    for out in outs:
        size = out.shape[0]
        total = jnp.zeros(out.shape, F32)
        for delta, q in zip(deltas, q_parts):
            total = total + jnp.dot(
                delta[at : at + size, :], q[...], preferred_element_type=F32
            )
        out[...] = (temp[0] * total).astype(BF16)
        at += size


def q_grads_kernel(temp, delta, p_all, out):
    out[...] = (
        temp[0]
        * lax.dot_general(
            delta[...], p_all[...], (((0,), (0,)), ((), ())), preferred_element_type=F32
        )
    ).astype(BF16)


def add_kernel(starts, *refs):
    terms, outs = refs[: len(starts)], refs[len(starts) :]
    at = 0
    for out in outs:
        size = out.shape[0]
        total = None
        for term, start in zip(terms, starts):
            if start + at + size > term.shape[0]:
                continue
            value = term[start + at : start + at + size, :].astype(F32)
            total = value if total is None else total + value
        out[...] = total.astype(out.dtype)
        at += size


def final_kernel(q_ref, p_ref, q0, q1, q2, q3, p0, p1, q_out, p_out):
    def back(src, grad, dst):
        wide = src[...].astype(F32)
        length = jnp.sqrt(jnp.sum(wide * wide, axis=1, keepdims=True))
        unit = wide / length
        along = jnp.sum(unit * grad, axis=1, keepdims=True)
        dst[...] = ((grad - unit * along) / length).astype(BF16)

    q_sum = q0[...].astype(F32) + q1[...].astype(F32) + q2[...].astype(F32) + q3[...].astype(F32)
    back(q_ref, q_sum, q_out)
    back(p_ref, p0[...].astype(F32) + p1[...].astype(F32), p_out)


def vmem(n):
    return [pl.BlockSpec(memory_space=pltpu.VMEM)] * n


def anywhere(n):
    return [pl.BlockSpec(memory_space=pl.ANY)] * n


def smem(n):
    return [pl.BlockSpec(memory_space=pltpu.SMEM)] * n


def call(kernel, shapes, in_specs, args, scratch=()):
    multi = isinstance(shapes, (list, tuple))
    return pl.pallas_call(
        kernel,
        out_shape=shapes,
        in_specs=in_specs,
        out_specs=vmem(len(shapes)) if multi else vmem(1)[0],
        scratch_shapes=list(scratch),
        compiler_params=pltpu.CompilerParams(vmem_limit_bytes=VMEM_LIMIT),
    )(*args)


def join(rows, *parts):
    return call(
        join_kernel,
        jax.ShapeDtypeStruct((rows, parts[0].shape[1]), BF16),
        vmem(len(parts)),
        parts,
    )


def after(array, *others):
    return lax.optimization_barrier((array, *others))[0]


def gather(q_low, p_low):
    rows = q_low.shape[0]
    pair = join(2 * rows, p_low, swap(p_low))
    near = join(4 * rows, q_low, *(inner(q_low, k) for k in (1, 2, 3)))
    one = along_z(pair, 1)
    two = along_z(pair, 2)
    near = after(near, one)
    far = [outer(near, k) for k in (1, 2, 3)]
    relay = after(two, near)
    three = along_z(relay, 1)
    four = along_z(join(rows, relay), 2)
    one_b = swap(after(one, *far))
    two_b = swap(after(two, *far))
    return [near, *far], [pair, one, two, three, four, swap(four), one_b, two_b, swap(three)]


def add(sizes, *terms):
    width = terms[0][0].shape[1]
    return call(
        functools.partial(add_kernel, [start for _, start in terms]),
        [jax.ShapeDtypeStruct((size, width), BF16) for size in sizes],
        vmem(len(terms)),
        [array for array, _ in terms],
    )


def scatter_queries(parts, rows):
    terms = [parts[0]] + [outer(parts[k], -k) for k in (1, 2, 3)]
    near = add([rows] * 4, *((term, 0) for term in terms))
    return [near[0]] + [inner(near[k], -k) for k in (1, 2, 3)]


def scatter_passages(pair, one, two, three, four, rest, rows):
    crossed = swap(rest)
    (three,) = add([2 * rows], (three, 0), (crossed, 5 * rows))
    (four,) = add([rows], (four, 0), (crossed, 0))
    from_three = along_z(three, -1)
    from_four = along_z(four, -2)
    (one,) = add([2 * rows], (one, 0), (crossed, rows))
    from_one = along_z(one, -1)
    two = add([rows] * 2, (two, 0), (crossed, 3 * rows), (from_three, 0), (from_four, 0))
    from_two = along_z(join(2 * rows, *two), -2)
    here, there = add([rows] * 2, (pair, 0), (from_one, 0), (from_two, 0))
    return here, swap(there)


def local(queries, passages, positives, inv_temp):
    rows, width = queries.shape
    count = rows * 16
    part_rows = 4 * rows
    chunk = 256
    shape = jax.ShapeDtypeStruct
    temp = inv_temp.reshape(1)
    q_low, p_low = call(
        norm_kernel,
        [shape((rows, width), BF16)] * 2,
        anywhere(2),
        (queries, passages),
        [pltpu.VMEM((rows, width), BF16)] * 2 + [pltpu.SemaphoreType.DMA((2,))],
    )
    q_parts, p_parts = gather(q_low, p_low)
    targets = call(
        functools.partial(target_kernel, rows),
        [shape((1, part_rows), jnp.int32)] * 4,
        vmem(1),
        (positives.reshape(32, rows),),
    )
    p_all = join(count, *p_parts)

    def logits(*ks):
        out = call(
            functools.partial(logits_kernel, chunk),
            [shape((count, part_rows), BF16)] * len(ks) + [shape((8, part_rows), F32)] * len(ks),
            smem(1) + vmem(2 * len(ks) + 1),
            (temp, *(q_parts[k] for k in ks), *(targets[k] for k in ks), p_all),
            [pltpu.VMEM((count, part_rows), F32)],
        )
        return dict(zip(ks, zip(out[: len(ks)], out[len(ks) :])))

    found = {**logits(0), **logits(1, 3), **logits(2)}
    e_parts = [found[k][0] for k in range(4)]
    row_parts = [found[k][1] for k in range(4)]
    stat = call(
        functools.partial(stat_kernel, rows), shape((16, 17 * 128), F32), vmem(4), row_parts
    )
    stats = lax.all_to_all(stat, ("y", "x"), 0, 0, tiled=True)

    *deltas, loss = call(
        functools.partial(delta_kernel, rows, chunk),
        [shape((count, part_rows), BF16)] * 4 + [shape((1, rows), F32)],
        vmem(13),
        (stats, *e_parts, *row_parts, *targets),
        [pltpu.VMEM((8, 16 * 128), F32), pltpu.VMEM((8, part_rows), F32)],
    )

    def p_grads(first, *sizes):
        return call(
            functools.partial(p_grads_kernel, first * rows),
            [shape((size * rows, width), BF16) for size in sizes],
            smem(1) + vmem(8),
            (temp, *deltas, *q_parts),
        )

    three, four, rest = p_grads(6, 2, 1, 7)
    q_grads = [
        call(q_grads_kernel, shape((part_rows, width), BF16), smem(1) + vmem(2), (temp, delta, p_all))
        for delta in deltas
    ]
    pair, one, two = p_grads(0, 2, 2, 2)
    q_terms = scatter_queries(q_grads, rows)
    p_terms = scatter_passages(pair, one, two, three, four, rest, rows)
    query_grads, passage_grads = call(
        final_kernel,
        [shape((rows, width), BF16)] * 2,
        vmem(8),
        (queries, passages, *q_terms, *p_terms),
    )
    return (loss.reshape(rows), query_grads, passage_grads)


def solution(mesh):
    fine = Mesh(mesh.devices.reshape(SIZES), AXES)
    return jax.shard_map(
        local,
        mesh=fine,
        in_specs=(P(AXES, None), P(AXES, None), P(("zl", "core")), P()),
        out_specs=(P(AXES), P(AXES, None), P(AXES, None)),
        check_vma=False,
    )
```

time: 107 us -> 102 us (0.953)
  waiting for transfers between devices: 22.4 us -> 16 us
  blocking collectives: 11.1 us -> 17 us
  local copies, waits for them, and re-layouts: 6.41 us -> 2.04 us
  Pallas kernels: 19 us -> 20.7 us
  starting transfers between devices: 45.9 us -> 44.6 us
    ppermute x27, waiting for transfers between devices: 22.4 us -> 16 us  [fetch(): return lax.ppermute(array, AXES, pairs)]
    all_to_all x1, blocking collectives: 11.1 us -> 17 us  [local(): stats = lax.all_to_all(stat, ('y', 'x'), 0, 0, tiled=True)]
    unnamed x23 -> x11, local copies, waits for them, and re-layouts: 4.96 us -> 1.82 us
    pallas_call x16 -> x25, Pallas kernels: 19 us -> 20.7 us  [call(): pl.pallas_call(kernel, out_shape=shapes, in_specs=in_specs, out_specs=vme...]
    ppermute x27, starting transfers between devices: 45.9 us -> 44.6 us  [fetch(): return lax.ppermute(array, AXES, pairs)]
  transfers between devices with their start and end apart: 27 -> 27, of which waited for: 10 -> 8; matrix products, arithmetic and copies ran while one was open for 2% -> 0% of each run, Pallas kernels for 9% -> 6%
where the time goes in v3:
time: 102 us
  starting transfers between devices  44.6 us (44%)
  Pallas kernels  20.7 us (20%)
  blocking collectives  17 us (17%)
  waiting for transfers between devices  16 us (16%)
  local copies, waits for them, and re-layouts  2.04 us (2%)
  between operations  1.55 us (2%)
    ppermute x27, starting transfers between devices, fetch(): return lax.ppermute(array, AXES, pairs)  44.6 us
    pallas_call x25, Pallas kernels, call(): pl.pallas_call(kernel, out_shape=shapes, in_specs=in_specs, out_specs=vme...  20.7 us
    all_to_all x1, blocking collectives, local(): stats = lax.all_to_all(stat, ('y', 'x'), 0, 0, tiled=True)  17 us
    ppermute x27, waiting for transfers between devices, fetch(): return lax.ppermute(array, AXES, pairs)  16 us
  transfers between devices with their start and end apart: 27, of which 8 were waited for; matrix products, arithmetic and copies ran while one was open for 0% of the time, Pallas kernels for 6%

profile of v3, /device:TPU:1, one launch (start us, length us, event | category | flops | bytes accessed | tf_op | source)
XLA Modules:
  0.0 101.9 jit_solution(696263014545499657)
XLA Ops:
  0.6 0.9 copy-done
  1.5 0.9 copy-done.2
  2.4 0.6 shard_map.67
  3.0 3.3 %collective-permute-start.3 = (bf16[80,768]{1,0:T(8,128)(2,1)S(1)}, bf16[80,768]{1,0:T(8,128)(2,1)S(1)}, u32[]{:S(2)}, u32[]{:S(2)}) collective-permute-start(bf16[80,768]{1,0:T(8,128)(2,1)S(1)} %get-tuple-element.43.refs_0_), channel_id=1, source_target_pairs={{32,0},{34,2},{36,4},{38,6},{40,8},{42,10},{44,12},{46,14},{48,16}... | collective-permute-start | bytes 368648 | tf_op jit(solution)/shard_map/ppermute | solution.py:30
  6.3 1.0 collective-permute-done.3.refs_1_
  7.4 1.2 %collective-permute-start.2 = (bf16[80,768]{1,0:T(8,128)(2,1)S(1)}, bf16[80,768]{1,0:T(8,128)(2,1)S(1)}, u32[]{:S(2)}, u32[]{:S(2)}) collective-permute-start(bf16[80,768]{1,0:T(8,128)(2,1)S(1)} %get-tuple-element.42.refs_0_), channel_id=1, source_target_pairs={{6,0},{0,2},{2,4},{4,6},{14,8},{8,10},{10,12},{12,14},{22,16},{16,... | collective-permute-start | bytes 368648 | tf_op jit(solution)/shard_map/ppermute | solution.py:30
  8.6 2.6 %collective-permute-start.1 = (bf16[80,768]{1,0:T(8,128)(2,1)S(1)}, bf16[80,768]{1,0:T(8,128)(2,1)S(1)}, u32[]{:S(2)}, u32[]{:S(2)}) collective-permute-start(bf16[80,768]{1,0:T(8,128)(2,1)S(1)} %get-tuple-element.42.refs_0_), channel_id=1, source_target_pairs={{4,0},{6,2},{0,4},{2,6},{12,8},{14,10},{8,12},{10,14},{20,16},{22,... | collective-permute-start | bytes 368648 | tf_op jit(solution)/shard_map/ppermute | solution.py:30
  11.2 1.1 %collective-permute-start = (bf16[80,768]{1,0:T(8,128)(2,1)S(1)}, bf16[80,768]{1,0:T(8,128)(2,1)S(1)}, u32[]{:S(2)}, u32[]{:S(2)}) collective-permute-start(bf16[80,768]{1,0:T(8,128)(2,1)S(1)} %get-tuple-element.42.refs_0_), channel_id=1, source_target_pairs={{2,0},{4,2},{6,4},{0,6},{10,8},{12,10},{14,12},{8,14},{18,16},{20,... | collective-permute-start | bytes 368648 | tf_op jit(solution)/shard_map/ppermute | solution.py:30
  12.3 3.0 %collective-permute-start.5 = (bf16[160,768]{1,0:T(8,128)(2,1)S(1)}, bf16[160,768]{1,0:T(8,128)(2,1)S(1)}, u32[]{:S(2)}, u32[]{:S(2)}) collective-permute-start(bf16[160,768]{1,0:T(8,128)(2,1)S(1)} %shard_map.69.refs_0_), channel_id=1, source_target_pairs={{128,0},{130,2},{132,4},{134,6},{136,8},{138,10},{140,12},{142,14}... | collective-permute-start | bytes 737288 | tf_op jit(solution)/shard_map/ppermute | solution.py:30
  15.3 1.3 %collective-permute-start.11 = (bf16[320,768]{1,0:T(8,128)(2,1)S(1)}, bf16[320,768]{1,0:T(8,128)(2,1)S(1)}, u32[]{:S(2)}, u32[]{:S(2)}) collective-permute-start(bf16[320,768]{1,0:T(8,128)(2,1)S(1)} %shard_map.68.refs_0_.refs_4_), channel_id=1, source_target_pairs={{24,0},{26,2},{28,4},{30,6},{0,8},{2,10},{4,12},{6,14},{8,16},{10,... | collective-permute-start | bytes 1474568 | tf_op jit(solution)/shard_map/ppermute | solution.py:30
  16.6 2.5 %collective-permute-start.10 = (bf16[320,768]{1,0:T(8,128)(2,1)S(1)}, bf16[320,768]{1,0:T(8,128)(2,1)S(1)}, u32[]{:S(2)}, u32[]{:S(2)}) collective-permute-start(bf16[320,768]{1,0:T(8,128)(2,1)S(1)} %shard_map.68.refs_0_.refs_4_), channel_id=1, source_target_pairs={{16,0},{18,2},{20,4},{22,6},{24,8},{26,10},{28,12},{30,14},{0,16},... | collective-permute-start | bytes 1474568 | tf_op jit(solution)/shard_map/ppermute | solution.py:30
  19.1 1.2 %collective-permute-start.9 = (bf16[320,768]{1,0:T(8,128)(2,1)S(1)}, bf16[320,768]{1,0:T(8,128)(2,1)S(1)}, u32[]{:S(2)}, u32[]{:S(2)}) collective-permute-start(bf16[320,768]{1,0:T(8,128)(2,1)S(1)} %shard_map.68.refs_0_.refs_4_), channel_id=1, source_target_pairs={{8,0},{10,2},{12,4},{14,6},{16,8},{18,10},{20,12},{22,14},{24,16},... | collective-permute-start | bytes 1474568 | tf_op jit(solution)/shard_map/ppermute | solution.py:30
  20.2 2.0 %collective-permute-done.5.refs_0_.refs_2_ = bf16[160,768]{1,0:T(8,128)(2,1)S(1)} collective-permute-done((bf16[160,768]{1,0:T(8,128)(2,1)S(1)}, bf16[160,768]{1,0:T(8,128)(2,1)S(1)}, u32[]{:S(2)}, u32[]{:S(2)}) %collective-permute-start.5) | collective-permute-done | bytes 245792 | tf_op jit(solution)/shard_map/ppermute | solution.py:30
  22.3 1.5 %collective-permute-start.6 = (bf16[160,768]{1,0:T(8,128)(2,1)S(1)}, bf16[160,768]{1,0:T(8,128)(2,1)S(1)}, u32[]{:S(2)}, u32[]{:S(2)}) collective-permute-start(bf16[160,768]{1,0:T(8,128)(2,1)S(1)} %collective-permute-done.5.refs_0_.refs_2_), channel_id=1, source_target_pairs={{64,0},{66,2},{68,4},{70,6},{72,8},{74,10},{76,12},{78,14},{80,16}... | collective-permute-start | bytes 737288 | tf_op jit(solution)/shard_map/ppermute | solution.py:30
  23.7 2.6 %collective-permute-start.7 = (bf16[80,768]{1,0:T(8,128)(2,1)S(1)}, bf16[80,768]{1,0:T(8,128)(2,1)}, u32[]{:S(2)}, u32[]{:S(2)}) collective-permute-start(bf16[80,768]{1,0:T(8,128)(2,1)S(1)} %shard_map.71), channel_id=1, source_target_pairs={{128,0},{130,2},{132,4},{134,6},{136,8},{138,10},{140,12},{142,14}... | collective-permute-start | bytes 368648 | tf_op jit(solution)/shard_map/ppermute | solution.py:30
  26.3 2.8 %collective-permute-done.6.refs_3_ = bf16[160,768]{1,0:T(8,128)(2,1)S(1)} collective-permute-done((bf16[160,768]{1,0:T(8,128)(2,1)S(1)}, bf16[160,768]{1,0:T(8,128)(2,1)S(1)}, u32[]{:S(2)}, u32[]{:S(2)}) %collective-permute-start.6) | collective-permute-done | bytes 245792 | tf_op jit(solution)/shard_map/ppermute | solution.py:30
  29.1 5.7 %collective-permute-start.14 = (bf16[160,768]{1,0:T(8,128)(2,1)S(1)}, bf16[160,768]{1,0:T(8,128)(2,1)S(1)}, u32[]{:S(2)}, u32[]{:S(2)}) collective-permute-start(bf16[160,768]{1,0:T(8,128)(2,1)S(1)} %collective-permute-done.6.refs_3_), channel_id=1, source_target_pairs={{32,0},{34,2},{36,4},{38,6},{40,8},{42,10},{44,12},{46,14},{48,16}... | collective-permute-start | bytes 737288 | tf_op jit(solution)/shard_map/ppermute | solution.py:30
  34.9 4.1 %collective-permute-start.12 = (bf16[160,768]{1,0:T(8,128)(2,1)S(1)}, bf16[160,768]{1,0:T(8,128)(2,1)S(1)}, u32[]{:S(2)}, u32[]{:S(2)}) collective-permute-start(bf16[160,768]{1,0:T(8,128)(2,1)S(1)} %collective-permute-done.4.refs_1_), channel_id=1, source_target_pairs={{32,0},{34,2},{36,4},{38,6},{40,8},{42,10},{44,12},{46,14},{48,16}... | collective-permute-start | bytes 737288 | tf_op jit(solution)/shard_map/ppermute | solution.py:30
  38.9 0.5 collective-permute-start.8
  40.2 0.2 shard_map.70
  40.4 0.5 collective-permute-done.8.refs_5_
  40.9 1.2 %shard_map.72.refs_2_.refs_4_.p_all = bf16[1280,768]{1,0:T(8,128)(2,1)S(1)} custom-call(bf16[160,768]{1,0:T(8,128)(2,1)S(1)} %shard_map.69.refs_0_, bf16[160,768]{1,0:T(8,128)(2,1)S(1)} %collective-permute-done.4.refs_1_, bf16[160,768]{1,0:T(8,128)(2,1)S(1)} %collective-permute-done.5.refs_0_.refs_2_, bf16[160,768]{1,0:T(8,128)(2,1)S(1)} %collective-permute-done.6.refs_3_, ...), custom_call_target="tpu_custom_call" | custom-call | tf_op jit(solution)/shard_map/pallas_call | solution.py:241
  42.1 1.6 %shard_map.73 = (bf16[1280,320]{1,0:T(8,128)(2,1)S(1)}, f32[8,320]{1,0:T(8,128)S(1)}) custom-call(f32[1]{0:T(128)} %bitcast.6.temp, bf16[320,768]{1,0:T(8,128)(2,1)S(1)} %shard_map.68.refs_0_.refs_4_, s32[1,320]{1,0:T(1,128)S(1)} %get-tuple-element.45.refs_1_.refs_8_, bf16[1280,768]{1,0:T(8,128)(2,1)S(1)} %shard_map.72.refs_2_.refs_4_.p_all), custom_call_target="tpu_custom_call" | custom-call | tf_op jit(solution)/shard_map/pallas_call | solution.py:241
  43.8 1.6 %shard_map.75 = (bf16[1280,320]{1,0:T(8,128)(2,1)S(1)}, f32[8,320]{1,0:T(8,128)S(1)}) custom-call(f32[1]{0:T(128)} %bitcast.8.temp, bf16[320,768]{1,0:T(8,128)(2,1)S(1)} %collective-permute-done.10.refs_0_.refs_6_, s32[1,320]{1,0:T(1,128)S(1)} %get-tuple-element.53.refs_1_.refs_10_, bf16[1280,768]{1,0:T(8,128)(2,1)S(1)} %shard_map.72.refs_2_.refs_4_.p_all), custom_call_target="tpu_custom_call" | custom-call | tf_op jit(solution)/shard_map/pallas_call | solution.py:241
  45.4 2.8 %shard_map.74 = (bf16[1280,320]{1,0:T(8,128)(2,1)S(1)}, bf16[1280,320]{1,0:T(8,128)(2,1)S(1)}, f32[8,320]{1,0:T(8,128)S(1)}, f32[8,320]{1,0:T(8,128)S(1)}) custom-call(f32[1]{0:T(128)} %bitcast.7.temp, bf16[320,768]{1,0:T(8,128)(2,1)S(1)} %collective-permute-done.9.refs_0_.refs_5_, bf16[320,768]{1,0:T(8,128)(2,1)S(1)} %collective-permute-done.11.refs_1_.refs_7_, ...), custom_call_target="tpu_custom_call" | custom-call | tf_op jit(solution)/shard_map/pallas_call | solution.py:241
  48.1 1.1 %shard_map.76 = f32[16,2176]{1,0:T(8,128)S(1)} custom-call(f32[8,320]{1,0:T(8,128)S(1)} %get-tuple-element.49.refs_0_.refs_4_, f32[8,320]{1,0:T(8,128)S(1)} %get-tuple-element.52.refs_1_.refs_5_, f32[8,320]{1,0:T(8,128)S(1)} %get-tuple-element.54.refs_2_.refs_6_, f32[8,320]{1,0:T(8,128)S(1)} %get-tuple-element.55.refs_3_.refs_7_), custom_call_target="tpu_custom_call" | custom-call | tf_op jit(solution)/shard_map/pallas_call | solution.py:241
  49.3 0.1 copy.7
  49.4 17.0 %all_to_all.11 = f32[16,1,2176]{2,1,0:T(1,128)S(1)} all-to-all(f32[16,1,2176]{2,1,0:T(1,128)S(1)} %copy.7), channel_id=1, replica_groups=mesh['zl'=4,'core'=2,'y'=4,'x'=4,'zh'=2] {'y','x'}, dimensions={0} | all-to-all | bytes 278528 | tf_op jit(solution)/shard_map/all_to_all | solution.py:349
  66.4 2.0 %shard_map.77 = (bf16[1280,320]{1,0:T(8,128)(2,1)S(1)}, bf16[1280,320]{1,0:T(8,128)(2,1)S(1)}, bf16[1280,320]{1,0:T(8,128)(2,1)S(1)}, bf16[1280,320]{1,0:T(8,128)(2,1)S(1)}, f32[1,80]{1,0:T(1,128)}) custom-call(f32[16,2176]{1,0:T(8,128)S(1)} %bitcast.15, bf16[1280,320]{1,0:T(8,128)(2,1)S(1)} %get-tuple-element.56.refs_0_, ...), custom_call_target="tpu_custom_call" | custom-call | tf_op jit(solution)/shard_map/pallas_call | solution.py:241
  68.3 2.9 %shard_map.84 = (bf16[160,768]{1,0:T(8,128)(2,1)S(1)}, bf16[80,768]{1,0:T(8,128)(2,1)S(1)}, bf16[560,768]{1,0:T(8,128)(2,1)S(1)}) custom-call(f32[1]{0:T(128)} %bitcast.14.temp, bf16[1280,320]{1,0:T(8,128)(2,1)S(1)} %get-tuple-element.61.delta.refs_0_, bf16[1280,320]{1,0:T(8,128)(2,1)S(1)} %get-tuple-element.62.delta.refs_1_, ...), custom_call_target="tpu_custom_call" | custom-call | tf_op jit(solution)/shard_map/pallas_call | solution.py:241
  71.2 2.1 %collective-permute-start.21 = (bf16[560,768]{1,0:T(8,128)(2,1)S(1)}, bf16[560,768]{1,0:T(8,128)(2,1)S(1)}, u32[]{:S(2)}, u32[]{:S(2)}) collective-permute-start(bf16[560,768]{1,0:T(8,128)(2,1)S(1)} %get-tuple-element.71), channel_id=1, source_target_pairs={{32,0},{34,2},{36,4},{38,6},{40,8},{42,10},{44,12},{46,14},{48,16}... | collective-permute-start | bytes 2580488 | tf_op jit(solution)/shard_map/ppermute | solution.py:30
  73.3 0.9 shard_map.79
  74.2 0.9 shard_map.80
  75.1 0.9 shard_map.81
  76.0 0.7 collective-permute-start.17
  76.7 1.5 %collective-permute-start.16 = (bf16[320,768]{1,0:T(8,128)(2,1)S(1)}, bf16[320,768]{1,0:T(8,128)(2,1)S(1)}, u32[]{:S(2)}, u32[]{:S(2)}) collective-permute-start(bf16[320,768]{1,0:T(8,128)(2,1)S(1)} %shard_map.80), channel_id=1, source_target_pairs={{16,0},{18,2},{20,4},{22,6},{24,8},{26,10},{28,12},{30,14},{0,16},... | collective-permute-start | bytes 1474568 | tf_op jit(solution)/shard_map/ppermute | solution.py:30
  78.5 1.7 %shard_map.83 = (bf16[160,768]{1,0:T(8,128)(2,1)S(1)}, bf16[160,768]{1,0:T(8,128)(2,1)S(1)}, bf16[160,768]{1,0:T(8,128)(2,1)S(1)}) custom-call(f32[1]{0:T(128)} %bitcast.13.temp, bf16[1280,320]{1,0:T(8,128)(2,1)S(1)} %get-tuple-element.61.delta.refs_0_, bf16[1280,320]{1,0:T(8,128)(2,1)S(1)} %get-tuple-element.62.delta.refs_1_, ...), custom_call_target="tpu_custom_call" | custom-call | tf_op jit(solution)/shard_map/pallas_call | solution.py:241
  80.2 4.5 %collective-permute-done.24.refs_3_ = bf16[80,768]{1,0:T(8,128)(2,1)S(1)} collective-permute-done((bf16[80,768]{1,0:T(8,128)(2,1)S(1)}, bf16[80,768]{1,0:T(8,128)(2,1)S(1)}, u32[]{:S(2)}, u32[]{:S(2)}) %collective-permute-start.24) | collective-permute-done | bytes 122912 | tf_op jit(solution)/shard_map/ppermute | solution.py:30
  84.7 3.7 %collective-permute-start.22 = (bf16[160,768]{1,0:T(8,128)(2,1)S(1)}, bf16[160,768]{1,0:T(8,128)(2,1)S(1)}, u32[]{:S(2)}, u32[]{:S(2)}) collective-permute-start(bf16[160,768]{1,0:T(8,128)(2,1)S(1)} %shard_map.85), channel_id=1, source_target_pairs={{193,0},{195,2},{197,4},{199,6},{201,8},{203,10},{205,12},{207,14}... | collective-permute-start | bytes 737288 | tf_op jit(solution)/shard_map/ppermute | solution.py:30
  88.6 0.9 shard_map.78.refs_0_
  89.5 1.9 %collective-permute-done.15.refs_1_ = bf16[320,768]{1,0:T(8,128)(2,1)S(1)} collective-permute-done((bf16[320,768]{1,0:T(8,128)(2,1)S(1)}, bf16[320,768]{1,0:T(8,128)(2,1)S(1)}, u32[]{:S(2)}, u32[]{:S(2)}) %collective-permute-start.15) | collective-permute-done | bytes 491552 | tf_op jit(solution)/shard_map/ppermute | solution.py:30
  91.5 0.2 shard_map.82
  91.8 1.9 %collective-permute-start.19 = (bf16[80,768]{1,0:T(8,128)(2,1)S(1)}, bf16[80,768]{1,0:T(8,128)(2,1)S(1)}, u32[]{:S(2)}, u32[]{:S(2)}) collective-permute-start(bf16[80,768]{1,0:T(8,128)(2,1)S(1)} %get-tuple-element.67), channel_id=1, source_target_pairs={{4,0},{6,2},{0,4},{2,6},{12,8},{14,10},{8,12},{10,14},{20,16},{22,... | collective-permute-start | bytes 368648 | tf_op jit(solution)/shard_map/ppermute | solution.py:30
  93.7 0.8 collective-permute-start.20
  94.5 2.3 %collective-permute-done.25.refs_2_ = bf16[160,768]{1,0:T(8,128)(2,1)S(1)} collective-permute-done((bf16[160,768]{1,0:T(8,128)(2,1)S(1)}, bf16[160,768]{1,0:T(8,128)(2,1)S(1)}, u32[]{:S(2)}, u32[]{:S(2)}) %collective-permute-start.25) | collective-permute-done | bytes 245792 | tf_op jit(solution)/shard_map/ppermute | solution.py:30
  96.9 3.1 %collective-permute-start.26 = (bf16[80,768]{1,0:T(8,128)(2,1)S(1)}, bf16[80,768]{1,0:T(8,128)(2,1)S(1)}, u32[]{:S(2)}, u32[]{:S(2)}) collective-permute-start(bf16[80,768]{1,0:T(8,128)(2,1)S(1)} %get-tuple-element.78), channel_id=1, source_target_pairs={{32,0},{34,2},{36,4},{38,6},{40,8},{42,10},{44,12},{46,14},{48,16}... | collective-permute-start | bytes 368648 | tf_op jit(solution)/shard_map/ppermute | solution.py:30
  100.0 1.0 collective-permute-done.26.p1
  101.0 0.9 shard_map.91
  (45 shorter events, 1.0 us)
Async XLA Ops:
  0.6 0.9 copy-start
  1.5 0.9 copy-start.2
  2.4 37.7 %copy-start.4 = (s32[2560]{0:T(1024)S(1)}, s32[2560]{0:T(1024)}, u32[]{:S(2)}) copy-start(s32[2560]{0:T(1024)} %param.6) | copy-start | bytes 30724
  3.0 4.3 %collective-permute-start.3 = (bf16[80,768]{1,0:T(8,128)(2,1)S(1)}, bf16[80,768]{1,0:T(8,128)(2,1)S(1)}, u32[]{:S(2)}, u32[]{:S(2)}) collective-permute-start(bf16[80,768]{1,0:T(8,128)(2,1)S(1)} %get-tuple-element.43.refs_0_), channel_id=1, source_target_pairs={{32,0},{34,2},{36,4},{38,6},{40,8},{42,10},{44,12},{46,14},{48,16}... | collective-permute-start | bytes 368648 | tf_op jit(solution)/shard_map/ppermute | solution.py:30
  7.3 8.0 %collective-permute-start.4 = (bf16[160,768]{1,0:T(8,128)(2,1)S(1)}, bf16[160,768]{1,0:T(8,128)(2,1)S(1)}, u32[]{:S(2)}, u32[]{:S(2)}) collective-permute-start(bf16[160,768]{1,0:T(8,128)(2,1)S(1)} %shard_map.69.refs_0_), channel_id=1, source_target_pairs={{64,0},{66,2},{68,4},{70,6},{72,8},{74,10},{76,12},{78,14},{80,16}... | collective-permute-start | bytes 737288 | tf_op jit(solution)/shard_map/ppermute | solution.py:30
  7.4 7.9 %collective-permute-start.2 = (bf16[80,768]{1,0:T(8,128)(2,1)S(1)}, bf16[80,768]{1,0:T(8,128)(2,1)S(1)}, u32[]{:S(2)}, u32[]{:S(2)}) collective-permute-start(bf16[80,768]{1,0:T(8,128)(2,1)S(1)} %get-tuple-element.42.refs_0_), channel_id=1, source_target_pairs={{6,0},{0,2},{2,4},{4,6},{14,8},{8,10},{10,12},{12,14},{22,16},{16,... | collective-permute-start | bytes 368648 | tf_op jit(solution)/shard_map/ppermute | solution.py:30
  8.6 6.7 %collective-permute-start.1 = (bf16[80,768]{1,0:T(8,128)(2,1)S(1)}, bf16[80,768]{1,0:T(8,128)(2,1)S(1)}, u32[]{:S(2)}, u32[]{:S(2)}) collective-permute-start(bf16[80,768]{1,0:T(8,128)(2,1)S(1)} %get-tuple-element.42.refs_0_), channel_id=1, source_target_pairs={{4,0},{6,2},{0,4},{2,6},{12,8},{14,10},{8,12},{10,14},{20,16},{22,... | collective-permute-start | bytes 368648 | tf_op jit(solution)/shard_map/ppermute | solution.py:30
  11.2 4.1 %collective-permute-start = (bf16[80,768]{1,0:T(8,128)(2,1)S(1)}, bf16[80,768]{1,0:T(8,128)(2,1)S(1)}, u32[]{:S(2)}, u32[]{:S(2)}) collective-permute-start(bf16[80,768]{1,0:T(8,128)(2,1)S(1)} %get-tuple-element.42.refs_0_), channel_id=1, source_target_pairs={{2,0},{4,2},{6,4},{0,6},{10,8},{12,10},{14,12},{8,14},{18,16},{20,... | collective-permute-start | bytes 368648 | tf_op jit(solution)/shard_map/ppermute | solution.py:30
  12.3 10.0 %collective-permute-start.5 = (bf16[160,768]{1,0:T(8,128)(2,1)S(1)}, bf16[160,768]{1,0:T(8,128)(2,1)S(1)}, u32[]{:S(2)}, u32[]{:S(2)}) collective-permute-start(bf16[160,768]{1,0:T(8,128)(2,1)S(1)} %shard_map.69.refs_0_), channel_id=1, source_target_pairs={{128,0},{130,2},{132,4},{134,6},{136,8},{138,10},{140,12},{142,14}... | collective-permute-start | bytes 737288 | tf_op jit(solution)/shard_map/ppermute | solution.py:30
  15.3 19.5 %collective-permute-start.11 = (bf16[320,768]{1,0:T(8,128)(2,1)S(1)}, bf16[320,768]{1,0:T(8,128)(2,1)S(1)}, u32[]{:S(2)}, u32[]{:S(2)}) collective-permute-start(bf16[320,768]{1,0:T(8,128)(2,1)S(1)} %shard_map.68.refs_0_.refs_4_), channel_id=1, source_target_pairs={{24,0},{26,2},{28,4},{30,6},{0,8},{2,10},{4,12},{6,14},{8,16},{10,... | collective-permute-start | bytes 1474568 | tf_op jit(solution)/shard_map/ppermute | solution.py:30
  16.6 18.2 %collective-permute-start.10 = (bf16[320,768]{1,0:T(8,128)(2,1)S(1)}, bf16[320,768]{1,0:T(8,128)(2,1)S(1)}, u32[]{:S(2)}, u32[]{:S(2)}) collective-permute-start(bf16[320,768]{1,0:T(8,128)(2,1)S(1)} %shard_map.68.refs_0_.refs_4_), channel_id=1, source_target_pairs={{16,0},{18,2},{20,4},{22,6},{24,8},{26,10},{28,12},{30,14},{0,16},... | collective-permute-start | bytes 1474568 | tf_op jit(solution)/shard_map/ppermute | solution.py:30
  19.1 15.8 %collective-permute-start.9 = (bf16[320,768]{1,0:T(8,128)(2,1)S(1)}, bf16[320,768]{1,0:T(8,128)(2,1)S(1)}, u32[]{:S(2)}, u32[]{:S(2)}) collective-permute-start(bf16[320,768]{1,0:T(8,128)(2,1)S(1)} %shard_map.68.refs_0_.refs_4_), channel_id=1, source_target_pairs={{8,0},{10,2},{12,4},{14,6},{16,8},{18,10},{20,12},{22,14},{24,16},... | collective-permute-start | bytes 1474568 | tf_op jit(solution)/shard_map/ppermute | solution.py:30
  22.3 6.8 %collective-permute-start.6 = (bf16[160,768]{1,0:T(8,128)(2,1)S(1)}, bf16[160,768]{1,0:T(8,128)(2,1)S(1)}, u32[]{:S(2)}, u32[]{:S(2)}) collective-permute-start(bf16[160,768]{1,0:T(8,128)(2,1)S(1)} %collective-permute-done.5.refs_0_.refs_2_), channel_id=1, source_target_pairs={{64,0},{66,2},{68,4},{70,6},{72,8},{74,10},{76,12},{78,14},{80,16}... | collective-permute-start | bytes 737288 | tf_op jit(solution)/shard_map/ppermute | solution.py:30
  23.7 15.2 %collective-permute-start.7 = (bf16[80,768]{1,0:T(8,128)(2,1)S(1)}, bf16[80,768]{1,0:T(8,128)(2,1)}, u32[]{:S(2)}, u32[]{:S(2)}) collective-permute-start(bf16[80,768]{1,0:T(8,128)(2,1)S(1)} %shard_map.71), channel_id=1, source_target_pairs={{128,0},{130,2},{132,4},{134,6},{136,8},{138,10},{140,12},{142,14}... | collective-permute-start | bytes 368648 | tf_op jit(solution)/shard_map/ppermute | solution.py:30
  29.1 11.8 %collective-permute-start.14 = (bf16[160,768]{1,0:T(8,128)(2,1)S(1)}, bf16[160,768]{1,0:T(8,128)(2,1)S(1)}, u32[]{:S(2)}, u32[]{:S(2)}) collective-permute-start(bf16[160,768]{1,0:T(8,128)(2,1)S(1)} %collective-permute-done.6.refs_3_), channel_id=1, source_target_pairs={{32,0},{34,2},{36,4},{38,6},{40,8},{42,10},{44,12},{46,14},{48,16}... | collective-permute-start | bytes 737288 | tf_op jit(solution)/shard_map/ppermute | solution.py:30
  34.9 6.1 %collective-permute-start.12 = (bf16[160,768]{1,0:T(8,128)(2,1)S(1)}, bf16[160,768]{1,0:T(8,128)(2,1)S(1)}, u32[]{:S(2)}, u32[]{:S(2)}) collective-permute-start(bf16[160,768]{1,0:T(8,128)(2,1)S(1)} %collective-permute-done.4.refs_1_), channel_id=1, source_target_pairs={{32,0},{34,2},{36,4},{38,6},{40,8},{42,10},{44,12},{46,14},{48,16}... | collective-permute-start | bytes 737288 | tf_op jit(solution)/shard_map/ppermute | solution.py:30
  38.9 2.0 %collective-permute-start.13 = (bf16[160,768]{1,0:T(8,128)(2,1)S(1)}, bf16[160,768]{1,0:T(8,128)(2,1)}, u32[]{:S(2)}, u32[]{:S(2)}) collective-permute-start(bf16[160,768]{1,0:T(8,128)(2,1)S(1)} %collective-permute-done.5.refs_0_.refs_2_), channel_id=1, source_target_pairs={{32,0},{34,2},{36,4},{38,6},{40,8},{42,10},{44,12},{46,14},{48,16}... | collective-permute-start | bytes 737288 | tf_op jit(solution)/shard_map/ppermute | solution.py:30
  38.9 2.0 %collective-permute-start.8 = (bf16[80,768]{1,0:T(8,128)(2,1)}, bf16[80,768]{1,0:T(8,128)(2,1)}, u32[]{:S(2)}, u32[]{:S(2)}) collective-permute-start(bf16[80,768]{1,0:T(8,128)(2,1)} %collective-permute-done.7.refs_4_), channel_id=1, source_target_pairs={{32,0},{34,2},{36,4},{38,6},{40,8},{42,10},{44,12},{46,14},{48,16}... | collective-permute-start | bytes 368648 | tf_op jit(solution)/shard_map/ppermute | solution.py:30
  71.2 6.9 %collective-permute-start.21 = (bf16[560,768]{1,0:T(8,128)(2,1)S(1)}, bf16[560,768]{1,0:T(8,128)(2,1)S(1)}, u32[]{:S(2)}, u32[]{:S(2)}) collective-permute-start(bf16[560,768]{1,0:T(8,128)(2,1)S(1)} %get-tuple-element.71), channel_id=1, source_target_pairs={{32,0},{34,2},{36,4},{38,6},{40,8},{42,10},{44,12},{46,14},{48,16}... | collective-permute-start | bytes 2580488 | tf_op jit(solution)/shard_map/ppermute | solution.py:30
  76.0 13.5 %collective-permute-start.17 = (bf16[320,768]{1,0:T(8,128)(2,1)S(1)}, bf16[320,768]{1,0:T(8,128)(2,1)S(1)}, u32[]{:S(2)}, u32[]{:S(2)}) collective-permute-start(bf16[320,768]{1,0:T(8,128)(2,1)S(1)} %shard_map.81), channel_id=1, source_target_pairs={{8,0},{10,2},{12,4},{14,6},{16,8},{18,10},{20,12},{22,14},{24,16},... | collective-permute-start | bytes 1474568 | tf_op jit(solution)/shard_map/ppermute | solution.py:30
  76.7 12.8 %collective-permute-start.16 = (bf16[320,768]{1,0:T(8,128)(2,1)S(1)}, bf16[320,768]{1,0:T(8,128)(2,1)S(1)}, u32[]{:S(2)}, u32[]{:S(2)}) collective-permute-start(bf16[320,768]{1,0:T(8,128)(2,1)S(1)} %shard_map.80), channel_id=1, source_target_pairs={{16,0},{18,2},{20,4},{22,6},{24,8},{26,10},{28,12},{30,14},{0,16},... | collective-permute-start | bytes 1474568 | tf_op jit(solution)/shard_map/ppermute | solution.py:30
  78.2 13.3 %collective-permute-start.15 = (bf16[320,768]{1,0:T(8,128)(2,1)S(1)}, bf16[320,768]{1,0:T(8,128)(2,1)S(1)}, u32[]{:S(2)}, u32[]{:S(2)}) collective-permute-start(bf16[320,768]{1,0:T(8,128)(2,1)S(1)} %shard_map.79), channel_id=1, source_target_pairs={{24,0},{26,2},{28,4},{30,6},{0,8},{2,10},{4,12},{6,14},{8,16},{10,... | collective-permute-start | bytes 1474568 | tf_op jit(solution)/shard_map/ppermute | solution.py:30
  78.2 10.2 %collective-permute-start.23 = (bf16[160,768]{1,0:T(8,128)(2,1)S(1)}, bf16[160,768]{1,0:T(8,128)(2,1)S(1)}, u32[]{:S(2)}, u32[]{:S(2)}) collective-permute-start(bf16[160,768]{1,0:T(8,128)(2,1)S(1)} %shard_map.86), channel_id=1, source_target_pairs={{193,0},{195,2},{197,4},{199,6},{201,8},{203,10},{205,12},{207,14}... | collective-permute-start | bytes 737288 | tf_op jit(solution)/shard_map/ppermute | solution.py:30
  78.4 6.4 %collective-permute-start.24 = (bf16[80,768]{1,0:T(8,128)(2,1)S(1)}, bf16[80,768]{1,0:T(8,128)(2,1)S(1)}, u32[]{:S(2)}, u32[]{:S(2)}) collective-permute-start(bf16[80,768]{1,0:T(8,128)(2,1)S(1)} %shard_map.87), channel_id=1, source_target_pairs={{129,0},{131,2},{133,4},{135,6},{137,8},{139,10},{141,12},{143,14}... | collective-permute-start | bytes 368648 | tf_op jit(solution)/shard_map/ppermute | solution.py:30
  84.7 9.8 %collective-permute-start.22 = (bf16[160,768]{1,0:T(8,128)(2,1)S(1)}, bf16[160,768]{1,0:T(8,128)(2,1)S(1)}, u32[]{:S(2)}, u32[]{:S(2)}) collective-permute-start(bf16[160,768]{1,0:T(8,128)(2,1)S(1)} %shard_map.85), channel_id=1, source_target_pairs={{193,0},{195,2},{197,4},{199,6},{201,8},{203,10},{205,12},{207,14}... | collective-permute-start | bytes 737288 | tf_op jit(solution)/shard_map/ppermute | solution.py:30
  88.5 8.3 %collective-permute-start.25 = (bf16[160,768]{1,0:T(8,128)(2,1)S(1)}, bf16[160,768]{1,0:T(8,128)(2,1)S(1)}, u32[]{:S(2)}, u32[]{:S(2)}) collective-permute-start(bf16[160,768]{1,0:T(8,128)(2,1)S(1)} %shard_map.89), channel_id=1, source_target_pairs={{129,0},{131,2},{133,4},{135,6},{137,8},{139,10},{141,12},{143,14}... | collective-permute-start | bytes 737288 | tf_op jit(solution)/shard_map/ppermute | solution.py:30
  89.5 11.5 %copy-start.1 = (bf16[80,768]{1,0:T(8,128)(2,1)S(1)}, bf16[80,768]{1,0:T(8,128)(2,1)}, u32[]{:S(2)}) copy-start(bf16[80,768]{1,0:T(8,128)(2,1)} %q_ref.3) | copy-start | bytes 368644
  89.5 11.5 %copy-start.3 = (bf16[80,768]{1,0:T(8,128)(2,1)S(1)}, bf16[80,768]{1,0:T(8,128)(2,1)}, u32[]{:S(2)}) copy-start(bf16[80,768]{1,0:T(8,128)(2,1)} %p_ref.3) | copy-start | bytes 368644
  91.7 8.3 %collective-permute-start.18 = (bf16[80,768]{1,0:T(8,128)(2,1)S(1)}, bf16[80,768]{1,0:T(8,128)(2,1)S(1)}, u32[]{:S(2)}, u32[]{:S(2)}) collective-permute-start(bf16[80,768]{1,0:T(8,128)(2,1)S(1)} %get-tuple-element.66), channel_id=1, source_target_pairs={{6,0},{0,2},{2,4},{4,6},{14,8},{8,10},{10,12},{12,14},{22,16},{16,... | collective-permute-start | bytes 368648 | tf_op jit(solution)/shard_map/ppermute | solution.py:30
  91.8 8.2 %collective-permute-start.19 = (bf16[80,768]{1,0:T(8,128)(2,1)S(1)}, bf16[80,768]{1,0:T(8,128)(2,1)S(1)}, u32[]{:S(2)}, u32[]{:S(2)}) collective-permute-start(bf16[80,768]{1,0:T(8,128)(2,1)S(1)} %get-tuple-element.67), channel_id=1, source_target_pairs={{4,0},{6,2},{0,4},{2,6},{12,8},{14,10},{8,12},{10,14},{20,16},{22,... | collective-permute-start | bytes 368648 | tf_op jit(solution)/shard_map/ppermute | solution.py:30
  93.7 6.3 %collective-permute-start.20 = (bf16[80,768]{1,0:T(8,128)(2,1)S(1)}, bf16[80,768]{1,0:T(8,128)(2,1)S(1)}, u32[]{:S(2)}, u32[]{:S(2)}) collective-permute-start(bf16[80,768]{1,0:T(8,128)(2,1)S(1)} %get-tuple-element.68), channel_id=1, source_target_pairs={{2,0},{4,2},{6,4},{0,6},{10,8},{12,10},{14,12},{8,14},{18,16},{20,... | collective-permute-start | bytes 368648 | tf_op jit(solution)/shard_map/ppermute | solution.py:30
  96.9 4.1 %collective-permute-start.26 = (bf16[80,768]{1,0:T(8,128)(2,1)S(1)}, bf16[80,768]{1,0:T(8,128)(2,1)S(1)}, u32[]{:S(2)}, u32[]{:S(2)}) collective-permute-start(bf16[80,768]{1,0:T(8,128)(2,1)S(1)} %get-tuple-element.78), channel_id=1, source_target_pairs={{32,0},{34,2},{36,4},{38,6},{40,8},{42,10},{44,12},{46,14},{48,16}... | collective-permute-start | bytes 368648 | tf_op jit(solution)/shard_map/ppermute | solution.py:30

commit v4 on v3

--- a/solution.py
+++ b/solution.py
@@ -57,18 +57,10 @@
     return lax.rem(y + step_y, 4) * 4 + lax.rem(x + step_x, 4)
 
 
-def norm_kernel(q_ref, p_ref, q_low, p_low, q_buf, p_buf, sems):
-    copies = [
-        pltpu.make_async_copy(src, buf, sems.at[i])
-        for i, (src, buf) in enumerate(((q_ref, q_buf), (p_ref, p_buf)))
-    ]
-    for copy in copies:
-        copy.start()
-    for copy, buf, dst in zip(copies, (q_buf, p_buf), (q_low, p_low)):
-        copy.wait()
-        wide = buf[...].astype(F32)
-        length = jnp.sqrt(jnp.sum(wide * wide, axis=1, keepdims=True))
-        dst[...] = (wide / length).astype(BF16)
+def norm_kernel(src, dst):
+    wide = src[...].astype(F32)
+    length = jnp.sqrt(jnp.sum(wide * wide, axis=1, keepdims=True))
+    dst[...] = (wide / length).astype(BF16)
 
 
 def target_kernel(rows, positives, *outs):
@@ -91,36 +83,49 @@
             out[:, b * rows : (b + 1) * rows] = jnp.where(owner == y * 4 + x, row, -1)
 
 
-def logits_kernel(chunk, temp, *refs):
-    parts = (len(refs) - 2) // 4
-    q_parts, targets, p_all = refs[:parts], refs[parts : 2 * parts], refs[2 * parts]
-    e_outs, row_outs = refs[2 * parts + 1 : 3 * parts + 1], refs[3 * parts + 1 : 4 * parts + 1]
-    logits = refs[-1]
+def logits_kernel(rows, chunk, temp, *refs):
+    q_parts, targets, p_parts = refs[:4], refs[4:8], refs[8:17]
+    p_all, stat, e_outs, row_outs, logits = refs[17], refs[18], refs[19:23], refs[23:27], refs[27]
     count = p_all.shape[0]
     scale = temp[0]
-    for q, target, e_out, row_out in zip(q_parts, targets, e_outs, row_outs):
+    at = 0
+    for part in p_parts:
+        p_all[at : at + part.shape[0], :] = part[...]
+        at += part.shape[0]
+    stat[...] = jnp.zeros_like(stat)
+    dest = lax.broadcasted_iota(jnp.int32, (16, rows), 0)
+    for_dest = jnp.zeros((16, rows), F32)
+    for k in range(4):
         tops = []
         for at in range(0, count, chunk):
             part = slice(at, at + chunk)
             values = scale * lax.dot_general(
-                p_all[part, :], q[...], (((1,), (1,)), ((), ())), preferred_element_type=F32
+                p_all[part, :], q_parts[k][...], (((1,), (1,)), ((), ())), preferred_element_type=F32
             )
-            logits[part, :] = values
+            logits[k % 2, part, :] = values
             tops.append(jnp.max(values, axis=0, keepdims=True))
         top = functools.reduce(jnp.maximum, tops)
         total = jnp.zeros_like(top)
         positive = jnp.zeros_like(top)
         for at in range(0, count, chunk):
             part = slice(at, at + chunk)
-            values = logits[part, :]
-            hit = lax.broadcasted_iota(jnp.int32, values.shape, 0) + at == target[...]
+            values = logits[k % 2, part, :]
+            hit = lax.broadcasted_iota(jnp.int32, values.shape, 0) + at == targets[k][...]
             positive = positive + jnp.sum(jnp.where(hit, values, 0.0), axis=0, keepdims=True)
             e = jnp.exp(values - top)
             total = total + jnp.sum(e, axis=0, keepdims=True)
-            e_out[part, :] = e.astype(BF16)
-        row_out[0:1, :] = top
-        row_out[1:2, :] = top + jnp.log(total)
-        row_out[2:3, :] = positive
+            e_outs[k][part, :] = e.astype(BF16)
+        row_outs[k][0:1, :] = top
+        row_outs[k][1:2, :] = positive
+        log_sum = top + jnp.log(total)
+        for b in range(4):
+            slot = slot_of(k, b)
+            lanes = slice(b * rows, (b + 1) * rows)
+            stat[:, pl.ds(pl.multiple_of(slot * 128, 128), rows)] = jnp.broadcast_to(
+                log_sum[:, lanes], (16, rows)
+            )
+            for_dest = jnp.where(dest == slot, positive[:, lanes], for_dest)
+    stat[:, 2048 : 2048 + rows] = for_dest
 
 
 def join_kernel(*refs):
@@ -130,22 +135,6 @@
         size = min(part.shape[0], out.shape[0] - at)
         out[at : at + size, :] = part[:size, :]
         at += size
-
-
-def stat_kernel(rows, *refs):
-    stat = refs[-1]
-    stat[...] = jnp.zeros_like(stat)
-    positive = jnp.zeros((16, rows), F32)
-    dest = lax.broadcasted_iota(jnp.int32, (16, rows), 0)
-    for k, part in enumerate(refs[:-1]):
-        for b in range(4):
-            slot = slot_of(k, b)
-            lanes = slice(b * rows, (b + 1) * rows)
-            stat[:, pl.ds(pl.multiple_of(slot * 128, 128), rows)] = jnp.broadcast_to(
-                part[1:2, lanes], (16, rows)
-            )
-            positive = jnp.where(dest == slot, part[2:3, lanes], positive)
-    stat[:, 2048 : 2048 + rows] = positive
 
 
 def delta_kernel(rows, chunk, stat, *refs):
@@ -165,7 +154,7 @@
     for k in range(4):
         total = lane[k : k + 1, :]
         factor = jnp.exp(row_parts[k][0:1, :] - total)
-        at_hit = jnp.exp(row_parts[k][2:3, :] - total) - 1.0
+        at_hit = jnp.exp(row_parts[k][1:2, :] - total) - 1.0
         for at in range(0, count, chunk):
             part = slice(at, at + chunk)
             prob = e_parts[k][part, :].astype(F32) * factor
@@ -187,13 +176,22 @@
         at += size
 
 
-def q_grads_kernel(temp, delta, p_all, out):
-    out[...] = (
-        temp[0]
+def q_grads(scale, delta, p_all):
+    return (
+        scale
         * lax.dot_general(
             delta[...], p_all[...], (((0,), (0,)), ((), ())), preferred_element_type=F32
         )
     ).astype(BF16)
+
+
+def q_grads_kernel(temp, delta, p_all, out):
+    out[...] = q_grads(temp[0], delta, p_all)
+
+
+def local_grads_kernel(temp, p_all, *refs):
+    p_grads_kernel(0, temp, *refs[:-1])
+    refs[-1][...] = q_grads(temp[0], refs[0], p_all)
 
 
 def add_kernel(starts, *refs):
@@ -211,25 +209,19 @@
         at += size
 
 
-def final_kernel(q_ref, p_ref, q0, q1, q2, q3, p0, p1, q_out, p_out):
-    def back(src, grad, dst):
-        wide = src[...].astype(F32)
-        length = jnp.sqrt(jnp.sum(wide * wide, axis=1, keepdims=True))
-        unit = wide / length
-        along = jnp.sum(unit * grad, axis=1, keepdims=True)
-        dst[...] = ((grad - unit * along) / length).astype(BF16)
-
-    q_sum = q0[...].astype(F32) + q1[...].astype(F32) + q2[...].astype(F32) + q3[...].astype(F32)
-    back(q_ref, q_sum, q_out)
-    back(p_ref, p0[...].astype(F32) + p1[...].astype(F32), p_out)
+def final_kernel(src, *refs):
+    grad = refs[0][...].astype(F32)
+    for ref in refs[1:-1]:
+        grad = grad + ref[...].astype(F32)
+    wide = src[...].astype(F32)
+    length = jnp.sqrt(jnp.sum(wide * wide, axis=1, keepdims=True))
+    unit = wide / length
+    along = jnp.sum(unit * grad, axis=1, keepdims=True)
+    refs[-1][...] = ((grad - unit * along) / length).astype(BF16)
 
 
 def vmem(n):
     return [pl.BlockSpec(memory_space=pltpu.VMEM)] * n
-
-
-def anywhere(n):
-    return [pl.BlockSpec(memory_space=pl.ANY)] * n
 
 
 def smem(n):
@@ -267,13 +259,13 @@
     near = join(4 * rows, q_low, *(inner(q_low, k) for k in (1, 2, 3)))
     one = along_z(pair, 1)
     two = along_z(pair, 2)
-    near = after(near, one)
+    near = after(near, pair)
     far = [outer(near, k) for k in (1, 2, 3)]
     relay = after(two, near)
     three = along_z(relay, 1)
     four = along_z(join(rows, relay), 2)
-    one_b = swap(after(one, *far))
-    two_b = swap(after(two, *far))
+    one_b = swap(after(one, far[0]))
+    two_b = swap(two)
     return [near, *far], [pair, one, two, three, four, swap(four), one_b, two_b, swap(three)]
 
 
@@ -314,12 +306,9 @@
     chunk = 256
     shape = jax.ShapeDtypeStruct
     temp = inv_temp.reshape(1)
-    q_low, p_low = call(
-        norm_kernel,
-        [shape((rows, width), BF16)] * 2,
-        anywhere(2),
-        (queries, passages),
-        [pltpu.VMEM((rows, width), BF16)] * 2 + [pltpu.SemaphoreType.DMA((2,))],
+    p_low, q_low = (
+        call(norm_kernel, shape((rows, width), BF16), vmem(1), (array,))
+        for array in (passages, queries)
     )
     q_parts, p_parts = gather(q_low, p_low)
     targets = call(
@@ -328,24 +317,16 @@
         vmem(1),
         (positives.reshape(32, rows),),
     )
-    p_all = join(count, *p_parts)
-
-    def logits(*ks):
-        out = call(
-            functools.partial(logits_kernel, chunk),
-            [shape((count, part_rows), BF16)] * len(ks) + [shape((8, part_rows), F32)] * len(ks),
-            smem(1) + vmem(2 * len(ks) + 1),
-            (temp, *(q_parts[k] for k in ks), *(targets[k] for k in ks), p_all),
-            [pltpu.VMEM((count, part_rows), F32)],
-        )
-        return dict(zip(ks, zip(out[: len(ks)], out[len(ks) :])))
-
-    found = {**logits(0), **logits(1, 3), **logits(2)}
-    e_parts = [found[k][0] for k in range(4)]
-    row_parts = [found[k][1] for k in range(4)]
-    stat = call(
-        functools.partial(stat_kernel, rows), shape((16, 17 * 128), F32), vmem(4), row_parts
-    )
+    p_all, stat, *found = call(
+        functools.partial(logits_kernel, rows, chunk),
+        [shape((count, width), BF16), shape((16, 17 * 128), F32)]
+        + [shape((count, part_rows), BF16)] * 4
+        + [shape((8, part_rows), F32)] * 4,
+        smem(1) + vmem(17),
+        (temp, *q_parts, *targets, *p_parts),
+        [pltpu.VMEM((2, count, part_rows), F32)],
+    )
+    e_parts, row_parts = found[:4], found[4:]
     stats = lax.all_to_all(stat, ("y", "x"), 0, 0, tiled=True)
 
     *deltas, loss = call(
@@ -356,27 +337,27 @@
         [pltpu.VMEM((8, 16 * 128), F32), pltpu.VMEM((8, part_rows), F32)],
     )
 
-    def p_grads(first, *sizes):
-        return call(
-            functools.partial(p_grads_kernel, first * rows),
-            [shape((size * rows, width), BF16) for size in sizes],
-            smem(1) + vmem(8),
-            (temp, *deltas, *q_parts),
-        )
-
-    three, four, rest = p_grads(6, 2, 1, 7)
-    q_grads = [
+    three, four, rest = call(
+        functools.partial(p_grads_kernel, 6 * rows),
+        [shape((size * rows, width), BF16) for size in (2, 1, 7)],
+        smem(1) + vmem(8),
+        (temp, *deltas, *q_parts),
+    )
+    sent = [
         call(q_grads_kernel, shape((part_rows, width), BF16), smem(1) + vmem(2), (temp, delta, p_all))
-        for delta in deltas
+        for delta in deltas[1:]
     ]
-    pair, one, two = p_grads(0, 2, 2, 2)
-    q_terms = scatter_queries(q_grads, rows)
+    pair, one, two, own = call(
+        local_grads_kernel,
+        [shape((size * rows, width), BF16) for size in (2, 2, 2, 4)],
+        smem(1) + vmem(9),
+        (temp, p_all, *deltas, *q_parts),
+    )
+    q_terms = scatter_queries([own, *sent], rows)
     p_terms = scatter_passages(pair, one, two, three, four, rest, rows)
-    query_grads, passage_grads = call(
-        final_kernel,
-        [shape((rows, width), BF16)] * 2,
-        vmem(8),
-        (queries, passages, *q_terms, *p_terms),
+    query_grads, passage_grads = (
+        call(final_kernel, shape((rows, width), BF16), vmem(1 + len(terms)), (array, *terms))
+        for array, terms in ((queries, q_terms), (passages, p_terms))
     )
     return (loss.reshape(rows), query_grads, passage_grads)
 

time: 102 us -> 94.1 us (0.923)
  the two profiles are of different devices: /device:TPU:1 before, /device:TPU:49 now
where the time goes in v4:
time: 94.1 us; the launch traced here: 93.8 us
  starting transfers between devices  47 us (50%)
  Pallas kernels  19.6 us (21%)
  waiting for transfers between devices  11.7 us (12%)
  blocking collectives  8.82 us (9%)
  local copies, waits for them, and re-layouts  5.16 us (5%)
  between operations  1.49 us (2%)
    ppermute x27, starting transfers between devices, fetch(): return lax.ppermute(array, AXES, pairs)  47 us
    pallas_call x22, Pallas kernels, call(): pl.pallas_call(kernel, out_shape=shapes, in_specs=in_specs, out_specs=vme...  19.6 us
    ppermute x27, waiting for transfers between devices, fetch(): return lax.ppermute(array, AXES, pairs)  11.7 us
    all_to_all x1, blocking collectives, local(): stats = lax.all_to_all(stat, ('y', 'x'), 0, 0, tiled=True)  8.82 us
    unnamed x19, local copies, waits for them, and re-layouts  4.92 us
  transfers between devices with their start and end apart: 27, of which 9 were waited for; matrix products, arithmetic and copies ran while one was open for 0% of the time, Pallas kernels for 7%

profile of v4, /device:TPU:49, one launch (start us, length us, event | category | flops | bytes accessed | tf_op | source)
XLA Modules:
  0.0 93.8 jit_solution(9238374075357233879)
XLA Ops:
  0.6 0.9 copy-done.2
  1.7 0.8 collective-permute-start.3
  2.4 0.9 copy-done
  3.4 1.1 %collective-permute-start.2 = (bf16[80,768]{1,0:T(8,128)(2,1)S(1)}, bf16[80,768]{1,0:T(8,128)(2,1)S(1)}, u32[]{:S(2)}, u32[]{:S(2)}) collective-permute-start(bf16[80,768]{1,0:T(8,128)(2,1)S(1)} %shard_map.67.refs_0_), channel_id=1, source_target_pairs={{6,0},{0,2},{2,4},{4,6},{14,8},{8,10},{10,12},{12,14},{22,16},{16,... | collective-permute-start | bytes 368648 | tf_op jit(solution)/shard_map/ppermute | solution.py:30
  4.5 0.3 collective-permute-start.1
  4.9 0.9 collective-permute-start
  5.8 3.1 %collective-permute-start.8 = (bf16[160,768]{1,0:T(8,128)(2,1)S(1)}, bf16[160,768]{1,0:T(8,128)(2,1)S(1)}, u32[]{:S(2)}, u32[]{:S(2)}) collective-permute-start(bf16[160,768]{1,0:T(8,128)(2,1)S(1)} %shard_map.70.refs_8_), channel_id=1, source_target_pairs={{128,0},{130,2},{132,4},{134,6},{136,8},{138,10},{140,12},{142,14}... | collective-permute-start | bytes 737288 | tf_op jit(solution)/shard_map/ppermute | solution.py:30
  8.9 0.9 collective-permute-done.1.refs_2_
  9.8 0.9 collective-permute-done.refs_1_
  10.7 2.3 %collective-permute-start.4 = (bf16[320,768]{1,0:T(8,128)(2,1)S(1)}, bf16[320,768]{1,0:T(8,128)(2,1)S(1)}, u32[]{:S(2)}, u32[]{:S(2)}) collective-permute-start(bf16[320,768]{1,0:T(8,128)(2,1)S(1)} %shard_map.68.refs_0_.refs_4_), channel_id=1, source_target_pairs={{8,0},{10,2},{12,4},{14,6},{16,8},{18,10},{20,12},{22,14},{24,16},... | collective-permute-start | bytes 1474568 | tf_op jit(solution)/shard_map/ppermute | solution.py:30
  13.0 1.6 %collective-permute-start.7 = (bf16[160,768]{1,0:T(8,128)(2,1)S(1)}, bf16[160,768]{1,0:T(8,128)(2,1)S(1)}, u32[]{:S(2)}, u32[]{:S(2)}) collective-permute-start(bf16[160,768]{1,0:T(8,128)(2,1)S(1)} %shard_map.70.refs_8_), channel_id=1, source_target_pairs={{64,0},{66,2},{68,4},{70,6},{72,8},{74,10},{76,12},{78,14},{80,16}... | collective-permute-start | bytes 737288 | tf_op jit(solution)/shard_map/ppermute | solution.py:30
  14.6 2.7 %collective-permute-done.8.refs_0_.refs_10_ = bf16[160,768]{1,0:T(8,128)(2,1)S(1)} collective-permute-done((bf16[160,768]{1,0:T(8,128)(2,1)S(1)}, bf16[160,768]{1,0:T(8,128)(2,1)S(1)}, u32[]{:S(2)}, u32[]{:S(2)}) %collective-permute-start.8) | collective-permute-done | bytes 245792 | tf_op jit(solution)/shard_map/ppermute | solution.py:30
  17.5 4.0 %collective-permute-start.10 = (bf16[80,768]{1,0:T(8,128)(2,1)S(1)}, bf16[80,768]{1,0:T(8,128)(2,1)S(1)}, u32[]{:S(2)}, u32[]{:S(2)}) collective-permute-start(bf16[80,768]{1,0:T(8,128)(2,1)S(1)} %shard_map.72), channel_id=1, source_target_pairs={{128,0},{130,2},{132,4},{134,6},{136,8},{138,10},{140,12},{142,14}... | collective-permute-start | bytes 368648 | tf_op jit(solution)/shard_map/ppermute | solution.py:30
  21.5 2.8 %collective-permute-start.5 = (bf16[320,768]{1,0:T(8,128)(2,1)S(1)}, bf16[320,768]{1,0:T(8,128)(2,1)S(1)}, u32[]{:S(2)}, u32[]{:S(2)}) collective-permute-start(bf16[320,768]{1,0:T(8,128)(2,1)S(1)} %shard_map.68.refs_0_.refs_4_), channel_id=1, source_target_pairs={{16,0},{18,2},{20,4},{22,6},{24,8},{26,10},{28,12},{30,14},{0,16},... | collective-permute-start | bytes 1474568 | tf_op jit(solution)/shard_map/ppermute | solution.py:30
  24.4 1.8 %collective-permute-done.10.refs_12_ = bf16[80,768]{1,0:T(8,128)(2,1)S(1)} collective-permute-done((bf16[80,768]{1,0:T(8,128)(2,1)S(1)}, bf16[80,768]{1,0:T(8,128)(2,1)S(1)}, u32[]{:S(2)}, u32[]{:S(2)}) %collective-permute-start.10) | collective-permute-done | bytes 122912 | tf_op jit(solution)/shard_map/ppermute | solution.py:30
  26.2 4.8 %collective-permute-start.11 = (bf16[80,768]{1,0:T(8,128)(2,1)S(1)}, bf16[80,768]{1,0:T(8,128)(2,1)S(1)}, u32[]{:S(2)}, u32[]{:S(2)}) collective-permute-start(bf16[80,768]{1,0:T(8,128)(2,1)S(1)} %collective-permute-done.10.refs_12_), channel_id=1, source_target_pairs={{32,0},{34,2},{36,4},{38,6},{40,8},{42,10},{44,12},{46,14},{48,16}... | collective-permute-start | bytes 368648 | tf_op jit(solution)/shard_map/ppermute | solution.py:30
  31.0 0.6 copy-done.4
  31.6 0.5 collective-permute-start.14
  32.1 0.6 copy-done.6
  32.8 0.2 collective-permute-start.12
  33.7 0.2 shard_map.71
  34.0 0.5 collective-permute-done.12.refs_14_
  34.4 0.9 copy-done.5
  35.3 0.9 copy-done.7
  36.2 6.8 %shard_map.73 = (bf16[1280,768]{1,0:T(8,128)(2,1)S(1)}, f32[16,2176]{1,0:T(8,128)S(1)}, bf16[1280,320]{1,0:T(8,128)(2,1)S(1)}, bf16[1280,320]{1,0:T(8,128)(2,1)S...) custom-call(f32[1]{0:T(128)} %bitcast.6.temp, ...), custom_call_target="tpu_custom_call" | custom-call | tf_op jit(solution)/shard_map/pallas_call | solution.py:233
  43.3 8.8 %all_to_all.11 = f32[16,1,2176]{2,1,0:T(1,128)S(1)} all-to-all(f32[16,1,2176]{2,1,0:T(1,128)S(1)} %copy.7), channel_id=1, replica_groups=mesh['zl'=4,'core'=2,'y'=4,'x'=4,'zh'=2] {'y','x'}, dimensions={0} | all-to-all | bytes 278528 | tf_op jit(solution)/shard_map/all_to_all | solution.py:330
  52.1 2.0 %shard_map.74 = (bf16[1280,320]{1,0:T(8,128)(2,1)S(1)}, bf16[1280,320]{1,0:T(8,128)(2,1)S(1)}, bf16[1280,320]{1,0:T(8,128)(2,1)S(1)}, bf16[1280,320]{1,0:T(8,128)(2,1)S(1)}, f32[1,80]{1,0:T(1,128)}) custom-call(f32[16,2176]{1,0:T(8,128)S(1)} %bitcast.12, bf16[1280,320]{1,0:T(8,128)(2,1)S(1)} %get-tuple-element.48.refs_0_, ...), custom_call_target="tpu_custom_call" | custom-call | tf_op jit(solution)/shard_map/pallas_call | solution.py:233
  54.1 2.9 %shard_map.81 = (bf16[160,768]{1,0:T(8,128)(2,1)S(1)}, bf16[80,768]{1,0:T(8,128)(2,1)S(1)}, bf16[560,768]{1,0:T(8,128)(2,1)S(1)}) custom-call(f32[1]{0:T(128)} %bitcast.11.temp, bf16[1280,320]{1,0:T(8,128)(2,1)S(1)} %get-tuple-element.58.refs_0_, bf16[1280,320]{1,0:T(8,128)(2,1)S(1)} %get-tuple-element.59.refs_1_.delta, ...), custom_call_target="tpu_custom_call" | custom-call | tf_op jit(solution)/shard_map/pallas_call | solution.py:233
  57.0 4.5 %collective-permute-start.21 = (bf16[560,768]{1,0:T(8,128)(2,1)S(1)}, bf16[560,768]{1,0:T(8,128)(2,1)S(1)}, u32[]{:S(2)}, u32[]{:S(2)}) collective-permute-start(bf16[560,768]{1,0:T(8,128)(2,1)S(1)} %get-tuple-element.69), channel_id=1, source_target_pairs={{32,0},{34,2},{36,4},{38,6},{40,8},{42,10},{44,12},{46,14},{48,16}... | collective-permute-start | bytes 2580488 | tf_op jit(solution)/shard_map/ppermute | solution.py:30
  61.4 0.9 shard_map.76
  62.3 0.9 shard_map.77
  63.2 0.9 shard_map.78
  64.1 1.0 %collective-permute-start.17 = (bf16[320,768]{1,0:T(8,128)(2,1)S(1)}, bf16[320,768]{1,0:T(8,128)(2,1)S(1)}, u32[]{:S(2)}, u32[]{:S(2)}) collective-permute-start(bf16[320,768]{1,0:T(8,128)(2,1)S(1)} %shard_map.78), channel_id=1, source_target_pairs={{8,0},{10,2},{12,4},{14,6},{16,8},{18,10},{20,12},{22,14},{24,16},... | collective-permute-start | bytes 1474568 | tf_op jit(solution)/shard_map/ppermute | solution.py:30
  65.1 1.1 %collective-permute-start.16 = (bf16[320,768]{1,0:T(8,128)(2,1)S(1)}, bf16[320,768]{1,0:T(8,128)(2,1)S(1)}, u32[]{:S(2)}, u32[]{:S(2)}) collective-permute-start(bf16[320,768]{1,0:T(8,128)(2,1)S(1)} %shard_map.77), channel_id=1, source_target_pairs={{16,0},{18,2},{20,4},{22,6},{24,8},{26,10},{28,12},{30,14},{0,16},... | collective-permute-start | bytes 1474568 | tf_op jit(solution)/shard_map/ppermute | solution.py:30
  66.4 1.3 %collective-permute-start.24 = (bf16[80,768]{1,0:T(8,128)(2,1)S(1)}, bf16[80,768]{1,0:T(8,128)(2,1)S(1)}, u32[]{:S(2)}, u32[]{:S(2)}) collective-permute-start(bf16[80,768]{1,0:T(8,128)(2,1)S(1)} %shard_map.84), channel_id=1, source_target_pairs={{129,0},{131,2},{133,4},{135,6},{137,8},{139,10},{141,12},{143,14}... | collective-permute-start | bytes 368648 | tf_op jit(solution)/shard_map/ppermute | solution.py:30
  67.8 2.4 %shard_map.75 = (bf16[160,768]{1,0:T(8,128)(2,1)S(1)}, bf16[160,768]{1,0:T(8,128)(2,1)S(1)}, bf16[160,768]{1,0:T(8,128)(2,1)S(1)}, bf16[320,768]{1,0:T(8,128)(2,1)S(1)}) custom-call(f32[1]{0:T(128)} %bitcast.7.temp, bf16[1280,768]{1,0:T(8,128)(2,1)S(1)} %get-tuple-element.57.p_all, bf16[1280,320]{1,0:T(8,128)(2,1)S(1)} %get-tuple-element.58.refs_0_, ...), custom_call_target="tpu_custom_call" | custom-call | tf_op jit(solution)/shard_map/pallas_call | solution.py:233
  70.2 1.9 %collective-permute-done.24.refs_3_ = bf16[80,768]{1,0:T(8,128)(2,1)S(1)} collective-permute-done((bf16[80,768]{1,0:T(8,128)(2,1)S(1)}, bf16[80,768]{1,0:T(8,128)(2,1)S(1)}, u32[]{:S(2)}, u32[]{:S(2)}) %collective-permute-start.24) | collective-permute-done | bytes 122912 | tf_op jit(solution)/shard_map/ppermute | solution.py:30
  72.1 3.5 %collective-permute-start.22 = (bf16[160,768]{1,0:T(8,128)(2,1)S(1)}, bf16[160,768]{1,0:T(8,128)(2,1)S(1)}, u32[]{:S(2)}, u32[]{:S(2)}) collective-permute-start(bf16[160,768]{1,0:T(8,128)(2,1)S(1)} %shard_map.82), channel_id=1, source_target_pairs={{193,0},{195,2},{197,4},{199,6},{201,8},{203,10},{205,12},{207,14}... | collective-permute-start | bytes 737288 | tf_op jit(solution)/shard_map/ppermute | solution.py:30
  75.7 2.0 %collective-permute-start.25 = (bf16[160,768]{1,0:T(8,128)(2,1)S(1)}, bf16[160,768]{1,0:T(8,128)(2,1)S(1)}, u32[]{:S(2)}, u32[]{:S(2)}) collective-permute-start(bf16[160,768]{1,0:T(8,128)(2,1)S(1)} %shard_map.86), channel_id=1, source_target_pairs={{129,0},{131,2},{133,4},{135,6},{137,8},{139,10},{141,12},{143,14}... | collective-permute-start | bytes 737288 | tf_op jit(solution)/shard_map/ppermute | solution.py:30
  77.7 1.8 %collective-permute-done.15.refs_1_ = bf16[320,768]{1,0:T(8,128)(2,1)S(1)} collective-permute-done((bf16[320,768]{1,0:T(8,128)(2,1)S(1)}, bf16[320,768]{1,0:T(8,128)(2,1)S(1)}, u32[]{:S(2)}, u32[]{:S(2)}) %collective-permute-start.15) | collective-permute-done | bytes 491552 | tf_op jit(solution)/shard_map/ppermute | solution.py:30
  79.5 0.2 shard_map.79
  79.8 1.3 %collective-permute-start.18 = (bf16[80,768]{1,0:T(8,128)(2,1)S(1)}, bf16[80,768]{1,0:T(8,128)(2,1)S(1)}, u32[]{:S(2)}, u32[]{:S(2)}) collective-permute-start(bf16[80,768]{1,0:T(8,128)(2,1)S(1)} %get-tuple-element.64), channel_id=1, source_target_pairs={{6,0},{0,2},{2,4},{4,6},{14,8},{8,10},{10,12},{12,14},{22,16},{16,... | collective-permute-start | bytes 368648 | tf_op jit(solution)/shard_map/ppermute | solution.py:30
  81.1 1.1 %collective-permute-start.19 = (bf16[80,768]{1,0:T(8,128)(2,1)S(1)}, bf16[80,768]{1,0:T(8,128)(2,1)S(1)}, u32[]{:S(2)}, u32[]{:S(2)}) collective-permute-start(bf16[80,768]{1,0:T(8,128)(2,1)S(1)} %get-tuple-element.65), channel_id=1, source_target_pairs={{4,0},{6,2},{0,4},{2,6},{12,8},{14,10},{8,12},{10,14},{20,16},{22,... | collective-permute-start | bytes 368648 | tf_op jit(solution)/shard_map/ppermute | solution.py:30
  82.2 2.0 %collective-permute-start.20 = (bf16[80,768]{1,0:T(8,128)(2,1)S(1)}, bf16[80,768]{1,0:T(8,128)(2,1)S(1)}, u32[]{:S(2)}, u32[]{:S(2)}) collective-permute-start(bf16[80,768]{1,0:T(8,128)(2,1)S(1)} %get-tuple-element.66), channel_id=1, source_target_pairs={{2,0},{4,2},{6,4},{0,6},{10,8},{12,10},{14,12},{8,14},{18,16},{20,... | collective-permute-start | bytes 368648 | tf_op jit(solution)/shard_map/ppermute | solution.py:30
  84.2 1.1 %collective-permute-done.25.refs_2_ = bf16[160,768]{1,0:T(8,128)(2,1)S(1)} collective-permute-done((bf16[160,768]{1,0:T(8,128)(2,1)S(1)}, bf16[160,768]{1,0:T(8,128)(2,1)S(1)}, u32[]{:S(2)}, u32[]{:S(2)}) %collective-permute-start.25) | collective-permute-done | bytes 245792 | tf_op jit(solution)/shard_map/ppermute | solution.py:30
  85.4 6.5 %collective-permute-start.26 = (bf16[80,768]{1,0:T(8,128)(2,1)S(1)}, bf16[80,768]{1,0:T(8,128)(2,1)S(1)}, u32[]{:S(2)}, u32[]{:S(2)}) collective-permute-start(bf16[80,768]{1,0:T(8,128)(2,1)S(1)} %get-tuple-element.76), channel_id=1, source_target_pairs={{32,0},{34,2},{36,4},{38,6},{40,8},{42,10},{44,12},{46,14},{48,16}... | collective-permute-start | bytes 368648 | tf_op jit(solution)/shard_map/ppermute | solution.py:30
  92.0 0.9 shard_map.80
  93.0 0.9 shard_map.88
  (50 shorter events, 1.4 us)
Async XLA Ops:
  0.6 0.9 copy-start.2
  1.5 32.1 %copy-start.8 = (s32[2560]{0:T(1024)S(1)}, s32[2560]{0:T(1024)}, u32[]{:S(2)}) copy-start(s32[2560]{0:T(1024)} %param.6) | copy-start | bytes 30724
  1.7 4.2 %collective-permute-start.3 = (bf16[80,768]{1,0:T(8,128)(2,1)S(1)}, bf16[80,768]{1,0:T(8,128)(2,1)S(1)}, u32[]{:S(2)}, u32[]{:S(2)}) collective-permute-start(bf16[80,768]{1,0:T(8,128)(2,1)S(1)} %shard_map.69.refs_0_), channel_id=1, source_target_pairs={{32,0},{34,2},{36,4},{38,6},{40,8},{42,10},{44,12},{46,14},{48,16}... | collective-permute-start | bytes 368648 | tf_op jit(solution)/shard_map/ppermute | solution.py:30
  2.4 0.9 copy-start
  3.4 5.5 %collective-permute-start.2 = (bf16[80,768]{1,0:T(8,128)(2,1)S(1)}, bf16[80,768]{1,0:T(8,128)(2,1)S(1)}, u32[]{:S(2)}, u32[]{:S(2)}) collective-permute-start(bf16[80,768]{1,0:T(8,128)(2,1)S(1)} %shard_map.67.refs_0_), channel_id=1, source_target_pairs={{6,0},{0,2},{2,4},{4,6},{14,8},{8,10},{10,12},{12,14},{22,16},{16,... | collective-permute-start | bytes 368648 | tf_op jit(solution)/shard_map/ppermute | solution.py:30
  4.5 5.2 %collective-permute-start.1 = (bf16[80,768]{1,0:T(8,128)(2,1)S(1)}, bf16[80,768]{1,0:T(8,128)(2,1)S(1)}, u32[]{:S(2)}, u32[]{:S(2)}) collective-permute-start(bf16[80,768]{1,0:T(8,128)(2,1)S(1)} %shard_map.67.refs_0_), channel_id=1, source_target_pairs={{4,0},{6,2},{0,4},{2,6},{12,8},{14,10},{8,12},{10,14},{20,16},{22,... | collective-permute-start | bytes 368648 | tf_op jit(solution)/shard_map/ppermute | solution.py:30
  4.9 5.8 %collective-permute-start = (bf16[80,768]{1,0:T(8,128)(2,1)S(1)}, bf16[80,768]{1,0:T(8,128)(2,1)S(1)}, u32[]{:S(2)}, u32[]{:S(2)}) collective-permute-start(bf16[80,768]{1,0:T(8,128)(2,1)S(1)} %shard_map.67.refs_0_), channel_id=1, source_target_pairs={{2,0},{4,2},{6,4},{0,6},{10,8},{12,10},{14,12},{8,14},{18,16},{20,... | collective-permute-start | bytes 368648 | tf_op jit(solution)/shard_map/ppermute | solution.py:30
  5.8 11.5 %collective-permute-start.8 = (bf16[160,768]{1,0:T(8,128)(2,1)S(1)}, bf16[160,768]{1,0:T(8,128)(2,1)S(1)}, u32[]{:S(2)}, u32[]{:S(2)}) collective-permute-start(bf16[160,768]{1,0:T(8,128)(2,1)S(1)} %shard_map.70.refs_8_), channel_id=1, source_target_pairs={{128,0},{130,2},{132,4},{134,6},{136,8},{138,10},{140,12},{142,14}... | collective-permute-start | bytes 737288 | tf_op jit(solution)/shard_map/ppermute | solution.py:30
  10.7 20.9 %collective-permute-start.4 = (bf16[320,768]{1,0:T(8,128)(2,1)S(1)}, bf16[320,768]{1,0:T(8,128)(2,1)S(1)}, u32[]{:S(2)}, u32[]{:S(2)}) collective-permute-start(bf16[320,768]{1,0:T(8,128)(2,1)S(1)} %shard_map.68.refs_0_.refs_4_), channel_id=1, source_target_pairs={{8,0},{10,2},{12,4},{14,6},{16,8},{18,10},{20,12},{22,14},{24,16},... | collective-permute-start | bytes 1474568 | tf_op jit(solution)/shard_map/ppermute | solution.py:30
  13.0 8.5 %collective-permute-start.7 = (bf16[160,768]{1,0:T(8,128)(2,1)S(1)}, bf16[160,768]{1,0:T(8,128)(2,1)S(1)}, u32[]{:S(2)}, u32[]{:S(2)}) collective-permute-start(bf16[160,768]{1,0:T(8,128)(2,1)S(1)} %shard_map.70.refs_8_), channel_id=1, source_target_pairs={{64,0},{66,2},{68,4},{70,6},{72,8},{74,10},{76,12},{78,14},{80,16}... | collective-permute-start | bytes 737288 | tf_op jit(solution)/shard_map/ppermute | solution.py:30
  14.6 19.3 %collective-permute-start.6 = (bf16[320,768]{1,0:T(8,128)(2,1)S(1)}, bf16[320,768]{1,0:T(8,128)(2,1)S(1)}, u32[]{:S(2)}, u32[]{:S(2)}) collective-permute-start(bf16[320,768]{1,0:T(8,128)(2,1)S(1)} %shard_map.68.refs_0_.refs_4_), channel_id=1, source_target_pairs={{24,0},{26,2},{28,4},{30,6},{0,8},{2,10},{4,12},{6,14},{8,16},{10,... | collective-permute-start | bytes 1474568 | tf_op jit(solution)/shard_map/ppermute | solution.py:30
  17.4 14.3 %collective-permute-start.9 = (bf16[160,768]{1,0:T(8,128)(2,1)S(1)}, bf16[160,768]{1,0:T(8,128)(2,1)S(1)}, u32[]{:S(2)}, u32[]{:S(2)}) collective-permute-start(bf16[160,768]{1,0:T(8,128)(2,1)S(1)} %collective-permute-done.8.refs_0_.refs_10_), channel_id=1, source_target_pairs={{64,0},{66,2},{68,4},{70,6},{72,8},{74,10},{76,12},{78,14},{80,16}... | collective-permute-start | bytes 737288 | tf_op jit(solution)/shard_map/ppermute | solution.py:30
  17.5 8.7 %collective-permute-start.10 = (bf16[80,768]{1,0:T(8,128)(2,1)S(1)}, bf16[80,768]{1,0:T(8,128)(2,1)S(1)}, u32[]{:S(2)}, u32[]{:S(2)}) collective-permute-start(bf16[80,768]{1,0:T(8,128)(2,1)S(1)} %shard_map.72), channel_id=1, source_target_pairs={{128,0},{130,2},{132,4},{134,6},{136,8},{138,10},{140,12},{142,14}... | collective-permute-start | bytes 368648 | tf_op jit(solution)/shard_map/ppermute | solution.py:30
  21.5 12.4 %collective-permute-start.5 = (bf16[320,768]{1,0:T(8,128)(2,1)S(1)}, bf16[320,768]{1,0:T(8,128)(2,1)S(1)}, u32[]{:S(2)}, u32[]{:S(2)}) collective-permute-start(bf16[320,768]{1,0:T(8,128)(2,1)S(1)} %shard_map.68.refs_0_.refs_4_), channel_id=1, source_target_pairs={{16,0},{18,2},{20,4},{22,6},{24,8},{26,10},{28,12},{30,14},{0,16},... | collective-permute-start | bytes 1474568 | tf_op jit(solution)/shard_map/ppermute | solution.py:30
  26.2 5.9 %collective-permute-start.11 = (bf16[80,768]{1,0:T(8,128)(2,1)S(1)}, bf16[80,768]{1,0:T(8,128)(2,1)S(1)}, u32[]{:S(2)}, u32[]{:S(2)}) collective-permute-start(bf16[80,768]{1,0:T(8,128)(2,1)S(1)} %collective-permute-done.10.refs_12_), channel_id=1, source_target_pairs={{32,0},{34,2},{36,4},{38,6},{40,8},{42,10},{44,12},{46,14},{48,16}... | collective-permute-start | bytes 368648 | tf_op jit(solution)/shard_map/ppermute | solution.py:30
  31.0 0.6 copy-start.4
  31.6 2.3 %collective-permute-start.13 = (bf16[160,768]{1,0:T(8,128)(2,1)S(1)}, bf16[160,768]{1,0:T(8,128)(2,1)S(1)}, u32[]{:S(2)}, u32[]{:S(2)}) collective-permute-start(bf16[160,768]{1,0:T(8,128)(2,1)S(1)} %collective-permute-done.8.refs_0_.refs_10_), channel_id=1, source_target_pairs={{32,0},{34,2},{36,4},{38,6},{40,8},{42,10},{44,12},{46,14},{48,16}... | collective-permute-start | bytes 737288 | tf_op jit(solution)/shard_map/ppermute | solution.py:30
  31.6 2.3 %collective-permute-start.14 = (bf16[160,768]{1,0:T(8,128)(2,1)S(1)}, bf16[160,768]{1,0:T(8,128)(2,1)S(1)}, u32[]{:S(2)}, u32[]{:S(2)}) collective-permute-start(bf16[160,768]{1,0:T(8,128)(2,1)S(1)} %collective-permute-done.9.refs_11_), channel_id=1, source_target_pairs={{32,0},{34,2},{36,4},{38,6},{40,8},{42,10},{44,12},{46,14},{48,16}... | collective-permute-start | bytes 737288 | tf_op jit(solution)/shard_map/ppermute | solution.py:30
  32.1 0.6 copy-start.6
  32.8 1.6 %collective-permute-start.12 = (bf16[160,768]{1,0:T(8,128)(2,1)S(1)}, bf16[160,768]{1,0:T(8,128)(2,1)}, u32[]{:S(2)}, u32[]{:S(2)}) collective-permute-start(bf16[160,768]{1,0:T(8,128)(2,1)S(1)} %collective-permute-done.7.refs_9_), channel_id=1, source_target_pairs={{32,0},{34,2},{36,4},{38,6},{40,8},{42,10},{44,12},{46,14},{48,16}... | collective-permute-start | bytes 737288 | tf_op jit(solution)/shard_map/ppermute | solution.py:30
  34.4 0.9 copy-start.5
  35.3 0.9 copy-start.7
  57.0 9.2 %collective-permute-start.21 = (bf16[560,768]{1,0:T(8,128)(2,1)S(1)}, bf16[560,768]{1,0:T(8,128)(2,1)S(1)}, u32[]{:S(2)}, u32[]{:S(2)}) collective-permute-start(bf16[560,768]{1,0:T(8,128)(2,1)S(1)} %get-tuple-element.69), channel_id=1, source_target_pairs={{32,0},{34,2},{36,4},{38,6},{40,8},{42,10},{44,12},{46,14},{48,16}... | collective-permute-start | bytes 2580488 | tf_op jit(solution)/shard_map/ppermute | solution.py:30
  64.1 13.6 %collective-permute-start.17 = (bf16[320,768]{1,0:T(8,128)(2,1)S(1)}, bf16[320,768]{1,0:T(8,128)(2,1)S(1)}, u32[]{:S(2)}, u32[]{:S(2)}) collective-permute-start(bf16[320,768]{1,0:T(8,128)(2,1)S(1)} %shard_map.78), channel_id=1, source_target_pairs={{8,0},{10,2},{12,4},{14,6},{16,8},{18,10},{20,12},{22,14},{24,16},... | collective-permute-start | bytes 1474568 | tf_op jit(solution)/shard_map/ppermute | solution.py:30
  65.1 12.7 %collective-permute-start.16 = (bf16[320,768]{1,0:T(8,128)(2,1)S(1)}, bf16[320,768]{1,0:T(8,128)(2,1)S(1)}, u32[]{:S(2)}, u32[]{:S(2)}) collective-permute-start(bf16[320,768]{1,0:T(8,128)(2,1)S(1)} %shard_map.77), channel_id=1, source_target_pairs={{16,0},{18,2},{20,4},{22,6},{24,8},{26,10},{28,12},{30,14},{0,16},... | collective-permute-start | bytes 1474568 | tf_op jit(solution)/shard_map/ppermute | solution.py:30
  66.1 13.4 %collective-permute-start.15 = (bf16[320,768]{1,0:T(8,128)(2,1)S(1)}, bf16[320,768]{1,0:T(8,128)(2,1)S(1)}, u32[]{:S(2)}, u32[]{:S(2)}) collective-permute-start(bf16[320,768]{1,0:T(8,128)(2,1)S(1)} %shard_map.76), channel_id=1, source_target_pairs={{24,0},{26,2},{28,4},{30,6},{0,8},{2,10},{4,12},{6,14},{8,16},{10,... | collective-permute-start | bytes 1474568 | tf_op jit(solution)/shard_map/ppermute | solution.py:30
  66.3 9.2 %collective-permute-start.23 = (bf16[160,768]{1,0:T(8,128)(2,1)S(1)}, bf16[160,768]{1,0:T(8,128)(2,1)S(1)}, u32[]{:S(2)}, u32[]{:S(2)}) collective-permute-start(bf16[160,768]{1,0:T(8,128)(2,1)S(1)} %shard_map.83), channel_id=1, source_target_pairs={{193,0},{195,2},{197,4},{199,6},{201,8},{203,10},{205,12},{207,14}... | collective-permute-start | bytes 737288 | tf_op jit(solution)/shard_map/ppermute | solution.py:30
  66.4 5.6 %collective-permute-start.24 = (bf16[80,768]{1,0:T(8,128)(2,1)S(1)}, bf16[80,768]{1,0:T(8,128)(2,1)S(1)}, u32[]{:S(2)}, u32[]{:S(2)}) collective-permute-start(bf16[80,768]{1,0:T(8,128)(2,1)S(1)} %shard_map.84), channel_id=1, source_target_pairs={{129,0},{131,2},{133,4},{135,6},{137,8},{139,10},{141,12},{143,14}... | collective-permute-start | bytes 368648 | tf_op jit(solution)/shard_map/ppermute | solution.py:30
  72.1 12.1 %collective-permute-start.22 = (bf16[160,768]{1,0:T(8,128)(2,1)S(1)}, bf16[160,768]{1,0:T(8,128)(2,1)S(1)}, u32[]{:S(2)}, u32[]{:S(2)}) collective-permute-start(bf16[160,768]{1,0:T(8,128)(2,1)S(1)} %shard_map.82), channel_id=1, source_target_pairs={{193,0},{195,2},{197,4},{199,6},{201,8},{203,10},{205,12},{207,14}... | collective-permute-start | bytes 737288 | tf_op jit(solution)/shard_map/ppermute | solution.py:30
  75.6 16.3 %copy-start.1 = (bf16[80,768]{1,0:T(8,128)(2,1)S(1)}, bf16[80,768]{1,0:T(8,128)(2,1)}, u32[]{:S(2)}) copy-start(bf16[80,768]{1,0:T(8,128)(2,1)} %src.6) | copy-start | bytes 368644
  75.7 17.3 %copy-start.3 = (bf16[80,768]{1,0:T(8,128)(2,1)S(1)}, bf16[80,768]{1,0:T(8,128)(2,1)}, u32[]{:S(2)}) copy-start(bf16[80,768]{1,0:T(8,128)(2,1)} %src.7) | copy-start | bytes 368644
  75.7 9.6 %collective-permute-start.25 = (bf16[160,768]{1,0:T(8,128)(2,1)S(1)}, bf16[160,768]{1,0:T(8,128)(2,1)S(1)}, u32[]{:S(2)}, u32[]{:S(2)}) collective-permute-start(bf16[160,768]{1,0:T(8,128)(2,1)S(1)} %shard_map.86), channel_id=1, source_target_pairs={{129,0},{131,2},{133,4},{135,6},{137,8},{139,10},{141,12},{143,14}... | collective-permute-start | bytes 737288 | tf_op jit(solution)/shard_map/ppermute | solution.py:30
  79.8 12.2 %collective-permute-start.18 = (bf16[80,768]{1,0:T(8,128)(2,1)S(1)}, bf16[80,768]{1,0:T(8,128)(2,1)S(1)}, u32[]{:S(2)}, u32[]{:S(2)}) collective-permute-start(bf16[80,768]{1,0:T(8,128)(2,1)S(1)} %get-tuple-element.64), channel_id=1, source_target_pairs={{6,0},{0,2},{2,4},{4,6},{14,8},{8,10},{10,12},{12,14},{22,16},{16,... | collective-permute-start | bytes 368648 | tf_op jit(solution)/shard_map/ppermute | solution.py:30
  81.1 10.9 %collective-permute-start.19 = (bf16[80,768]{1,0:T(8,128)(2,1)S(1)}, bf16[80,768]{1,0:T(8,128)(2,1)S(1)}, u32[]{:S(2)}, u32[]{:S(2)}) collective-permute-start(bf16[80,768]{1,0:T(8,128)(2,1)S(1)} %get-tuple-element.65), channel_id=1, source_target_pairs={{4,0},{6,2},{0,4},{2,6},{12,8},{14,10},{8,12},{10,14},{20,16},{22,... | collective-permute-start | bytes 368648 | tf_op jit(solution)/shard_map/ppermute | solution.py:30
  82.2 9.8 %collective-permute-start.20 = (bf16[80,768]{1,0:T(8,128)(2,1)S(1)}, bf16[80,768]{1,0:T(8,128)(2,1)S(1)}, u32[]{:S(2)}, u32[]{:S(2)}) collective-permute-start(bf16[80,768]{1,0:T(8,128)(2,1)S(1)} %get-tuple-element.66), channel_id=1, source_target_pairs={{2,0},{4,2},{6,4},{0,6},{10,8},{12,10},{14,12},{8,14},{18,16},{20,... | collective-permute-start | bytes 368648 | tf_op jit(solution)/shard_map/ppermute | solution.py:30
  85.4 7.5 %collective-permute-start.26 = (bf16[80,768]{1,0:T(8,128)(2,1)S(1)}, bf16[80,768]{1,0:T(8,128)(2,1)S(1)}, u32[]{:S(2)}, u32[]{:S(2)}) collective-permute-start(bf16[80,768]{1,0:T(8,128)(2,1)S(1)} %get-tuple-element.76), channel_id=1, source_target_pairs={{32,0},{34,2},{36,4},{38,6},{40,8},{42,10},{44,12},{46,14},{48,16}... | collective-permute-start | bytes 368648 | tf_op jit(solution)/shard_map/ppermute | solution.py:30

commit v5 on v4

--- a/solution.py
+++ b/solution.py
@@ -76,7 +76,7 @@
             slot = jnp.where(
                 away < 4,
                 2 * away + other,
-                jnp.where(away == 4, 8 + other, 10 + 2 * (7 - away) + 1 - other),
+                jnp.where(away == 4, 8 + 7 * other, 9 + 2 * (7 - away) + 1 - other),
             )
             owner = lax.rem(lax.div(block, 8), 4) * 4 + lax.rem(lax.div(block, 2), 4)
             row = slot * rows + lax.rem(wanted, rows)
@@ -84,8 +84,8 @@
 
 
 def logits_kernel(rows, chunk, temp, *refs):
-    q_parts, targets, p_parts = refs[:4], refs[4:8], refs[8:17]
-    p_all, stat, e_outs, row_outs, logits = refs[17], refs[18], refs[19:23], refs[23:27], refs[27]
+    q_parts, targets, p_parts = refs[:4], refs[4:8], refs[8:15]
+    p_all, stat, e_outs, row_outs, logits = refs[15], refs[16], refs[17:21], refs[21:25], refs[25]
     count = p_all.shape[0]
     scale = temp[0]
     at = 0
@@ -257,16 +257,17 @@
     rows = q_low.shape[0]
     pair = join(2 * rows, p_low, swap(p_low))
     near = join(4 * rows, q_low, *(inner(q_low, k) for k in (1, 2, 3)))
-    one = along_z(pair, 1)
     two = along_z(pair, 2)
     near = after(near, pair)
     far = [outer(near, k) for k in (1, 2, 3)]
     relay = after(two, near)
+    one = along_z(after(pair, relay), 1)
     three = along_z(relay, 1)
     four = along_z(join(rows, relay), 2)
-    one_b = swap(after(one, far[0]))
-    two_b = swap(two)
-    return [near, *far], [pair, one, two, three, four, swap(four), one_b, two_b, swap(three)]
+    one_b = swap(after(one, far[0], far[2]))
+    two_b = swap(after(two, far[1]))
+    last = join(3 * rows, three, four)
+    return [near, *far], [pair, one, two, last, one_b, two_b, swap(last)]
 
 
 def add(sizes, *terms):
@@ -287,13 +288,13 @@
 
 def scatter_passages(pair, one, two, three, four, rest, rows):
     crossed = swap(rest)
-    (three,) = add([2 * rows], (three, 0), (crossed, 5 * rows))
-    (four,) = add([rows], (four, 0), (crossed, 0))
+    (three,) = add([2 * rows], (three, 0), (crossed, 4 * rows))
+    (four,) = add([rows], (four, 0), (crossed, 6 * rows))
     from_three = along_z(three, -1)
     from_four = along_z(four, -2)
-    (one,) = add([2 * rows], (one, 0), (crossed, rows))
+    (one,) = add([2 * rows], (one, 0), (crossed, 0))
     from_one = along_z(one, -1)
-    two = add([rows] * 2, (two, 0), (crossed, 3 * rows), (from_three, 0), (from_four, 0))
+    two = add([rows] * 2, (two, 0), (crossed, 2 * rows), (from_three, 0), (from_four, 0))
     from_two = along_z(join(2 * rows, *two), -2)
     here, there = add([rows] * 2, (pair, 0), (from_one, 0), (from_two, 0))
     return here, swap(there)
@@ -322,7 +323,7 @@
         [shape((count, width), BF16), shape((16, 17 * 128), F32)]
         + [shape((count, part_rows), BF16)] * 4
         + [shape((8, part_rows), F32)] * 4,
-        smem(1) + vmem(17),
+        smem(1) + vmem(15),
         (temp, *q_parts, *targets, *p_parts),
         [pltpu.VMEM((2, count, part_rows), F32)],
     )

time: 94.1 us -> 95.1 us (1.011)
  the two profiles are of different devices: /device:TPU:49 before, /device:TPU:1 now
where the time goes in v5:
time: 95.1 us; the launch traced here: 94.9 us
  starting transfers between devices  45.4 us (48%)
  Pallas kernels  19.7 us (21%)
  waiting for transfers between devices  15.9 us (17%)
  blocking collectives  10.3 us (11%)
  local copies, waits for them, and re-layouts  2.06 us (2%)
  between operations  1.49 us (2%)
    ppermute x26, starting transfers between devices, fetch(): return lax.ppermute(array, AXES, pairs)  45.4 us
    pallas_call x23, Pallas kernels, call(): pl.pallas_call(kernel, out_shape=shapes, in_specs=in_specs, out_specs=vme...  19.7 us
    ppermute x26, waiting for transfers between devices, fetch(): return lax.ppermute(array, AXES, pairs)  15.9 us
    all_to_all x1, blocking collectives, local(): stats = lax.all_to_all(stat, ('y', 'x'), 0, 0, tiled=True)  10.3 us
  transfers between devices with their start and end apart: 26, of which 9 were waited for; matrix products, arithmetic and copies ran while one was open for 0% of the time, Pallas kernels for 7%

profile of v5, /device:TPU:1, one launch (start us, length us, event | category | flops | bytes accessed | tf_op | source)
XLA Modules:
  0.0 94.9 jit_solution(10848322846994951721)
XLA Ops:
  0.6 0.9 copy-done.2
  1.5 0.1 shard_map.69.refs_0_
  1.7 3.3 %collective-permute-start.3 = (bf16[80,768]{1,0:T(8,128)(2,1)S(1)}, bf16[80,768]{1,0:T(8,128)(2,1)S(1)}, u32[]{:S(2)}, u32[]{:S(2)}) collective-permute-start(bf16[80,768]{1,0:T(8,128)(2,1)S(1)} %shard_map.69.refs_0_), channel_id=1, source_target_pairs={{32,0},{34,2},{36,4},{38,6},{40,8},{42,10},{44,12},{46,14},{48,16}... | collective-permute-start | bytes 368648 | tf_op jit(solution)/shard_map/ppermute | solution.py:30
  5.0 0.9 copy-done
  5.9 0.1 shard_map.67.refs_0_
  6.1 2.2 %collective-permute-start.1 = (bf16[80,768]{1,0:T(8,128)(2,1)S(1)}, bf16[80,768]{1,0:T(8,128)(2,1)S(1)}, u32[]{:S(2)}, u32[]{:S(2)}) collective-permute-start(bf16[80,768]{1,0:T(8,128)(2,1)S(1)} %shard_map.67.refs_0_), channel_id=1, source_target_pairs={{4,0},{6,2},{0,4},{2,6},{12,8},{14,10},{8,12},{10,14},{20,16},{22,... | collective-permute-start | bytes 368648 | tf_op jit(solution)/shard_map/ppermute | solution.py:30
  8.3 1.1 %collective-permute-start = (bf16[80,768]{1,0:T(8,128)(2,1)S(1)}, bf16[80,768]{1,0:T(8,128)(2,1)S(1)}, u32[]{:S(2)}, u32[]{:S(2)}) collective-permute-start(bf16[80,768]{1,0:T(8,128)(2,1)S(1)} %shard_map.67.refs_0_), channel_id=1, source_target_pairs={{2,0},{4,2},{6,4},{0,6},{10,8},{12,10},{14,12},{8,14},{18,16},{20,... | collective-permute-start | bytes 368648 | tf_op jit(solution)/shard_map/ppermute | solution.py:30
  9.4 3.1 %collective-permute-start.7 = (bf16[160,768]{1,0:T(8,128)(2,1)S(1)}, bf16[160,768]{1,0:T(8,128)(2,1)S(1)}, u32[]{:S(2)}, u32[]{:S(2)}) collective-permute-start(bf16[160,768]{1,0:T(8,128)(2,1)S(1)} %shard_map.70.refs_8_), channel_id=1, source_target_pairs={{128,0},{130,2},{132,4},{134,6},{136,8},{138,10},{140,12},{142,14}... | collective-permute-start | bytes 737288 | tf_op jit(solution)/shard_map/ppermute | solution.py:30
  12.4 0.2 collective-permute-done.2.refs_3_
  12.6 0.6 collective-permute-done.refs_1_
  13.3 2.1 %collective-permute-start.5 = (bf16[320,768]{1,0:T(8,128)(2,1)S(1)}, bf16[320,768]{1,0:T(8,128)(2,1)S(1)}, u32[]{:S(2)}, u32[]{:S(2)}) collective-permute-start(bf16[320,768]{1,0:T(8,128)(2,1)S(1)} %shard_map.68.refs_0_.refs_4_), channel_id=1, source_target_pairs={{16,0},{18,2},{20,4},{22,6},{24,8},{26,10},{28,12},{30,14},{0,16},... | collective-permute-start | bytes 1474568 | tf_op jit(solution)/shard_map/ppermute | solution.py:30
  15.3 0.3 collective-permute-start.6
  15.6 2.4 %collective-permute-start.4 = (bf16[320,768]{1,0:T(8,128)(2,1)S(1)}, bf16[320,768]{1,0:T(8,128)(2,1)S(1)}, u32[]{:S(2)}, u32[]{:S(2)}) collective-permute-start(bf16[320,768]{1,0:T(8,128)(2,1)S(1)} %shard_map.68.refs_0_.refs_4_), channel_id=1, source_target_pairs={{8,0},{10,2},{12,4},{14,6},{16,8},{18,10},{20,12},{22,14},{24,16},... | collective-permute-start | bytes 1474568 | tf_op jit(solution)/shard_map/ppermute | solution.py:30
  18.0 1.6 %collective-permute-done.7.refs_0_.refs_10_ = bf16[160,768]{1,0:T(8,128)(2,1)S(1)} collective-permute-done((bf16[160,768]{1,0:T(8,128)(2,1)S(1)}, bf16[160,768]{1,0:T(8,128)(2,1)S(1)}, u32[]{:S(2)}, u32[]{:S(2)}) %collective-permute-start.7) | collective-permute-done | bytes 245792 | tf_op jit(solution)/shard_map/ppermute | solution.py:30
  19.7 2.7 %collective-permute-start.10 = (bf16[80,768]{1,0:T(8,128)(2,1)S(1)}, bf16[80,768]{1,0:T(8,128)(2,1)S(1)}, u32[]{:S(2)}, u32[]{:S(2)}) collective-permute-start(bf16[80,768]{1,0:T(8,128)(2,1)S(1)} %shard_map.72), channel_id=1, source_target_pairs={{128,0},{130,2},{132,4},{134,6},{136,8},{138,10},{140,12},{142,14}... | collective-permute-start | bytes 368648 | tf_op jit(solution)/shard_map/ppermute | solution.py:30
  22.4 0.6 collective-permute-start.9
  23.0 4.7 %collective-permute-done.10.refs_1_ = bf16[80,768]{1,0:T(8,128)(2,1)S(1)} collective-permute-done((bf16[80,768]{1,0:T(8,128)(2,1)S(1)}, bf16[80,768]{1,0:T(8,128)(2,1)S(1)}, u32[]{:S(2)}, u32[]{:S(2)}) %collective-permute-start.10) | collective-permute-done | bytes 122912 | tf_op jit(solution)/shard_map/ppermute | solution.py:30
  27.7 1.6 %collective-permute-start.8 = (bf16[160,768]{1,0:T(8,128)(2,1)S(1)}, bf16[160,768]{1,0:T(8,128)(2,1)S(1)}, u32[]{:S(2)}, u32[]{:S(2)}) collective-permute-start(bf16[160,768]{1,0:T(8,128)(2,1)S(1)} %shard_map.70.refs_8_), channel_id=1, source_target_pairs={{64,0},{66,2},{68,4},{70,6},{72,8},{74,10},{76,12},{78,14},{80,16}... | collective-permute-start | bytes 737288 | tf_op jit(solution)/shard_map/ppermute | solution.py:30
  29.3 1.7 %collective-permute-done.9.refs_0_ = bf16[160,768]{1,0:T(8,128)(2,1)S(1)} collective-permute-done((bf16[160,768]{1,0:T(8,128)(2,1)S(1)}, bf16[160,768]{1,0:T(8,128)(2,1)S(1)}, u32[]{:S(2)}, u32[]{:S(2)}) %collective-permute-start.9) | collective-permute-done | bytes 245792 | tf_op jit(solution)/shard_map/ppermute | solution.py:30
  31.0 2.9 %collective-permute-start.13 = (bf16[240,768]{1,0:T(8,128)(2,1)S(1)}, bf16[240,768]{1,0:T(8,128)(2,1)S(1)}, u32[]{:S(2)}, u32[]{:S(2)}) collective-permute-start(bf16[240,768]{1,0:T(8,128)(2,1)S(1)} %shard_map.73.refs_11_), channel_id=1, source_target_pairs={{32,0},{34,2},{36,4},{38,6},{40,8},{42,10},{44,12},{46,14},{48,16}... | collective-permute-start | bytes 1105928 | tf_op jit(solution)/shard_map/ppermute | solution.py:30
  34.0 0.1 collective-permute-start.12
  34.1 3.5 %collective-permute-start.11 = (bf16[160,768]{1,0:T(8,128)(2,1)S(1)}, bf16[160,768]{1,0:T(8,128)(2,1)}, u32[]{:S(2)}, u32[]{:S(2)}) collective-permute-start(bf16[160,768]{1,0:T(8,128)(2,1)S(1)} %collective-permute-done.8.refs_9_), channel_id=1, source_target_pairs={{32,0},{34,2},{36,4},{38,6},{40,8},{42,10},{44,12},{46,14},{48,16}... | collective-permute-start | bytes 737288 | tf_op jit(solution)/shard_map/ppermute | solution.py:30
  38.3 0.2 shard_map.71
  38.5 0.3 collective-permute-done.11.refs_12_
  38.8 7.0 %shard_map.74 = (bf16[1280,768]{1,0:T(8,128)(2,1)S(1)}, f32[16,2176]{1,0:T(8,128)S(1)}, bf16[1280,320]{1,0:T(8,128)(2,1)S(1)}, bf16[1280,320]{1,0:T(8,128)(2,1)S...) custom-call(f32[1]{0:T(128)} %bitcast.6.temp, ...), custom_call_target="tpu_custom_call" | custom-call | tf_op jit(solution)/shard_map/pallas_call | solution.py:233
  45.8 0.2 copy.7
  46.0 10.3 %all_to_all.11 = f32[16,1,2176]{2,1,0:T(1,128)S(1)} all-to-all(f32[16,1,2176]{2,1,0:T(1,128)S(1)} %copy.7), channel_id=1, replica_groups=mesh['zl'=4,'core'=2,'y'=4,'x'=4,'zh'=2] {'y','x'}, dimensions={0} | all-to-all | bytes 278528 | tf_op jit(solution)/shard_map/all_to_all | solution.py:331
  56.3 2.0 %shard_map.75 = (bf16[1280,320]{1,0:T(8,128)(2,1)S(1)}, bf16[1280,320]{1,0:T(8,128)(2,1)S(1)}, bf16[1280,320]{1,0:T(8,128)(2,1)S(1)}, bf16[1280,320]{1,0:T(8,128)(2,1)S(1)}, f32[1,80]{1,0:T(1,128)}) custom-call(f32[16,2176]{1,0:T(8,128)S(1)} %bitcast.12, bf16[1280,320]{1,0:T(8,128)(2,1)S(1)} %get-tuple-element.52.refs_0_, ...), custom_call_target="tpu_custom_call" | custom-call | tf_op jit(solution)/shard_map/pallas_call | solution.py:233
  58.3 2.9 %shard_map.82 = (bf16[160,768]{1,0:T(8,128)(2,1)S(1)}, bf16[80,768]{1,0:T(8,128)(2,1)S(1)}, bf16[560,768]{1,0:T(8,128)(2,1)S(1)}) custom-call(f32[1]{0:T(128)} %bitcast.11.temp, bf16[1280,320]{1,0:T(8,128)(2,1)S(1)} %get-tuple-element.62.refs_0_, bf16[1280,320]{1,0:T(8,128)(2,1)S(1)} %get-tuple-element.63.refs_1_.delta, ...), custom_call_target="tpu_custom_call" | custom-call | tf_op jit(solution)/shard_map/pallas_call | solution.py:233
  61.1 2.1 %collective-permute-start.20 = (bf16[560,768]{1,0:T(8,128)(2,1)S(1)}, bf16[560,768]{1,0:T(8,128)(2,1)S(1)}, u32[]{:S(2)}, u32[]{:S(2)}) collective-permute-start(bf16[560,768]{1,0:T(8,128)(2,1)S(1)} %get-tuple-element.73), channel_id=1, source_target_pairs={{32,0},{34,2},{36,4},{38,6},{40,8},{42,10},{44,12},{46,14},{48,16}... | collective-permute-start | bytes 2580488 | tf_op jit(solution)/shard_map/ppermute | solution.py:30
  63.3 0.9 shard_map.77
  64.1 0.9 shard_map.78
  65.0 0.9 shard_map.79
  65.9 0.7 collective-permute-start.16
  66.6 1.5 %collective-permute-start.15 = (bf16[320,768]{1,0:T(8,128)(2,1)S(1)}, bf16[320,768]{1,0:T(8,128)(2,1)S(1)}, u32[]{:S(2)}, u32[]{:S(2)}) collective-permute-start(bf16[320,768]{1,0:T(8,128)(2,1)S(1)} %shard_map.78), channel_id=1, source_target_pairs={{16,0},{18,2},{20,4},{22,6},{24,8},{26,10},{28,12},{30,14},{0,16},... | collective-permute-start | bytes 1474568 | tf_op jit(solution)/shard_map/ppermute | solution.py:30
  68.1 3.5 %collective-permute-start.22 = (bf16[160,768]{1,0:T(8,128)(2,1)S(1)}, bf16[160,768]{1,0:T(8,128)(2,1)S(1)}, u32[]{:S(2)}, u32[]{:S(2)}) collective-permute-start(bf16[160,768]{1,0:T(8,128)(2,1)S(1)} %shard_map.84), channel_id=1, source_target_pairs={{193,0},{195,2},{197,4},{199,6},{201,8},{203,10},{205,12},{207,14}... | collective-permute-start | bytes 737288 | tf_op jit(solution)/shard_map/ppermute | solution.py:30
  71.6 1.0 %collective-permute-start.23 = (bf16[80,768]{1,0:T(8,128)(2,1)S(1)}, bf16[80,768]{1,0:T(8,128)(2,1)S(1)}, u32[]{:S(2)}, u32[]{:S(2)}) collective-permute-start(bf16[80,768]{1,0:T(8,128)(2,1)S(1)} %shard_map.85), channel_id=1, source_target_pairs={{129,0},{131,2},{133,4},{135,6},{137,8},{139,10},{141,12},{143,14}... | collective-permute-start | bytes 368648 | tf_op jit(solution)/shard_map/ppermute | solution.py:30
  72.6 2.4 %shard_map.76 = (bf16[160,768]{1,0:T(8,128)(2,1)S(1)}, bf16[160,768]{1,0:T(8,128)(2,1)S(1)}, bf16[160,768]{1,0:T(8,128)(2,1)S(1)}, bf16[320,768]{1,0:T(8,128)(2,1)S(1)}) custom-call(f32[1]{0:T(128)} %bitcast.7.temp, bf16[1280,768]{1,0:T(8,128)(2,1)S(1)} %get-tuple-element.61.p_all, bf16[1280,320]{1,0:T(8,128)(2,1)S(1)} %get-tuple-element.62.refs_0_, ...), custom_call_target="tpu_custom_call" | custom-call | tf_op jit(solution)/shard_map/pallas_call | solution.py:233
  75.1 2.3 %collective-permute-done.23.refs_3_ = bf16[80,768]{1,0:T(8,128)(2,1)S(1)} collective-permute-done((bf16[80,768]{1,0:T(8,128)(2,1)S(1)}, bf16[80,768]{1,0:T(8,128)(2,1)S(1)}, u32[]{:S(2)}, u32[]{:S(2)}) %collective-permute-start.23) | collective-permute-done | bytes 122912 | tf_op jit(solution)/shard_map/ppermute | solution.py:30
  77.4 2.9 %collective-permute-start.21 = (bf16[160,768]{1,0:T(8,128)(2,1)S(1)}, bf16[160,768]{1,0:T(8,128)(2,1)S(1)}, u32[]{:S(2)}, u32[]{:S(2)}) collective-permute-start(bf16[160,768]{1,0:T(8,128)(2,1)S(1)} %shard_map.83), channel_id=1, source_target_pairs={{193,0},{195,2},{197,4},{199,6},{201,8},{203,10},{205,12},{207,14}... | collective-permute-start | bytes 737288 | tf_op jit(solution)/shard_map/ppermute | solution.py:30
  80.4 1.2 %collective-permute-start.24 = (bf16[160,768]{1,0:T(8,128)(2,1)S(1)}, bf16[160,768]{1,0:T(8,128)(2,1)S(1)}, u32[]{:S(2)}, u32[]{:S(2)}) collective-permute-start(bf16[160,768]{1,0:T(8,128)(2,1)S(1)} %shard_map.87), channel_id=1, source_target_pairs={{129,0},{131,2},{133,4},{135,6},{137,8},{139,10},{141,12},{143,14}... | collective-permute-start | bytes 737288 | tf_op jit(solution)/shard_map/ppermute | solution.py:30
  81.6 0.2 shard_map.80
  82.0 2.0 %collective-permute-start.18 = (bf16[80,768]{1,0:T(8,128)(2,1)S(1)}, bf16[80,768]{1,0:T(8,128)(2,1)S(1)}, u32[]{:S(2)}, u32[]{:S(2)}) collective-permute-start(bf16[80,768]{1,0:T(8,128)(2,1)S(1)} %get-tuple-element.69), channel_id=1, source_target_pairs={{4,0},{6,2},{0,4},{2,6},{12,8},{14,10},{8,12},{10,14},{20,16},{22,... | collective-permute-start | bytes 368648 | tf_op jit(solution)/shard_map/ppermute | solution.py:30
  84.0 0.7 collective-permute-start.19
  84.7 4.4 %collective-permute-done.24.refs_2_ = bf16[160,768]{1,0:T(8,128)(2,1)S(1)} collective-permute-done((bf16[160,768]{1,0:T(8,128)(2,1)S(1)}, bf16[160,768]{1,0:T(8,128)(2,1)S(1)}, u32[]{:S(2)}, u32[]{:S(2)}) %collective-permute-start.24) | collective-permute-done | bytes 245792 | tf_op jit(solution)/shard_map/ppermute | solution.py:30
  89.2 3.8 %collective-permute-start.25 = (bf16[80,768]{1,0:T(8,128)(2,1)S(1)}, bf16[80,768]{1,0:T(8,128)(2,1)S(1)}, u32[]{:S(2)}, u32[]{:S(2)}) collective-permute-start(bf16[80,768]{1,0:T(8,128)(2,1)S(1)} %get-tuple-element.80), channel_id=1, source_target_pairs={{32,0},{34,2},{36,4},{38,6},{40,8},{42,10},{44,12},{46,14},{48,16}... | collective-permute-start | bytes 368648 | tf_op jit(solution)/shard_map/ppermute | solution.py:30
  93.1 0.9 shard_map.81
  94.0 0.9 shard_map.89
  (41 shorter events, 0.9 us)
Async XLA Ops:
  0.6 0.9 copy-start.2
  1.5 36.7 %copy-start.4 = (s32[2560]{0:T(1024)S(1)}, s32[2560]{0:T(1024)}, u32[]{:S(2)}) copy-start(s32[2560]{0:T(1024)} %param.6) | copy-start | bytes 30724
  1.7 7.7 %collective-permute-start.3 = (bf16[80,768]{1,0:T(8,128)(2,1)S(1)}, bf16[80,768]{1,0:T(8,128)(2,1)S(1)}, u32[]{:S(2)}, u32[]{:S(2)}) collective-permute-start(bf16[80,768]{1,0:T(8,128)(2,1)S(1)} %shard_map.69.refs_0_), channel_id=1, source_target_pairs={{32,0},{34,2},{36,4},{38,6},{40,8},{42,10},{44,12},{46,14},{48,16}... | collective-permute-start | bytes 368648 | tf_op jit(solution)/shard_map/ppermute | solution.py:30
  5.0 0.9 copy-start
  6.0 6.6 %collective-permute-start.2 = (bf16[80,768]{1,0:T(8,128)(2,1)S(1)}, bf16[80,768]{1,0:T(8,128)(2,1)S(1)}, u32[]{:S(2)}, u32[]{:S(2)}) collective-permute-start(bf16[80,768]{1,0:T(8,128)(2,1)S(1)} %shard_map.67.refs_0_), channel_id=1, source_target_pairs={{6,0},{0,2},{2,4},{4,6},{14,8},{8,10},{10,12},{12,14},{22,16},{16,... | collective-permute-start | bytes 368648 | tf_op jit(solution)/shard_map/ppermute | solution.py:30
  6.1 6.5 %collective-permute-start.1 = (bf16[80,768]{1,0:T(8,128)(2,1)S(1)}, bf16[80,768]{1,0:T(8,128)(2,1)S(1)}, u32[]{:S(2)}, u32[]{:S(2)}) collective-permute-start(bf16[80,768]{1,0:T(8,128)(2,1)S(1)} %shard_map.67.refs_0_), channel_id=1, source_target_pairs={{4,0},{6,2},{0,4},{2,6},{12,8},{14,10},{8,12},{10,14},{20,16},{22,... | collective-permute-start | bytes 368648 | tf_op jit(solution)/shard_map/ppermute | solution.py:30
  8.3 4.9 %collective-permute-start = (bf16[80,768]{1,0:T(8,128)(2,1)S(1)}, bf16[80,768]{1,0:T(8,128)(2,1)S(1)}, u32[]{:S(2)}, u32[]{:S(2)}) collective-permute-start(bf16[80,768]{1,0:T(8,128)(2,1)S(1)} %shard_map.67.refs_0_), channel_id=1, source_target_pairs={{2,0},{4,2},{6,4},{0,6},{10,8},{12,10},{14,12},{8,14},{18,16},{20,... | collective-permute-start | bytes 368648 | tf_op jit(solution)/shard_map/ppermute | solution.py:30
  9.4 10.3 %collective-permute-start.7 = (bf16[160,768]{1,0:T(8,128)(2,1)S(1)}, bf16[160,768]{1,0:T(8,128)(2,1)S(1)}, u32[]{:S(2)}, u32[]{:S(2)}) collective-permute-start(bf16[160,768]{1,0:T(8,128)(2,1)S(1)} %shard_map.70.refs_8_), channel_id=1, source_target_pairs={{128,0},{130,2},{132,4},{134,6},{136,8},{138,10},{140,12},{142,14}... | collective-permute-start | bytes 737288 | tf_op jit(solution)/shard_map/ppermute | solution.py:30
  13.3 20.7 %collective-permute-start.5 = (bf16[320,768]{1,0:T(8,128)(2,1)S(1)}, bf16[320,768]{1,0:T(8,128)(2,1)S(1)}, u32[]{:S(2)}, u32[]{:S(2)}) collective-permute-start(bf16[320,768]{1,0:T(8,128)(2,1)S(1)} %shard_map.68.refs_0_.refs_4_), channel_id=1, source_target_pairs={{16,0},{18,2},{20,4},{22,6},{24,8},{26,10},{28,12},{30,14},{0,16},... | collective-permute-start | bytes 1474568 | tf_op jit(solution)/shard_map/ppermute | solution.py:30
  15.3 18.7 %collective-permute-start.6 = (bf16[320,768]{1,0:T(8,128)(2,1)S(1)}, bf16[320,768]{1,0:T(8,128)(2,1)S(1)}, u32[]{:S(2)}, u32[]{:S(2)}) collective-permute-start(bf16[320,768]{1,0:T(8,128)(2,1)S(1)} %shard_map.68.refs_0_.refs_4_), channel_id=1, source_target_pairs={{24,0},{26,2},{28,4},{30,6},{0,8},{2,10},{4,12},{6,14},{8,16},{10,... | collective-permute-start | bytes 1474568 | tf_op jit(solution)/shard_map/ppermute | solution.py:30
  15.6 18.4 %collective-permute-start.4 = (bf16[320,768]{1,0:T(8,128)(2,1)S(1)}, bf16[320,768]{1,0:T(8,128)(2,1)S(1)}, u32[]{:S(2)}, u32[]{:S(2)}) collective-permute-start(bf16[320,768]{1,0:T(8,128)(2,1)S(1)} %shard_map.68.refs_0_.refs_4_), channel_id=1, source_target_pairs={{8,0},{10,2},{12,4},{14,6},{16,8},{18,10},{20,12},{22,14},{24,16},... | collective-permute-start | bytes 1474568 | tf_op jit(solution)/shard_map/ppermute | solution.py:30
  19.7 8.1 %collective-permute-start.10 = (bf16[80,768]{1,0:T(8,128)(2,1)S(1)}, bf16[80,768]{1,0:T(8,128)(2,1)S(1)}, u32[]{:S(2)}, u32[]{:S(2)}) collective-permute-start(bf16[80,768]{1,0:T(8,128)(2,1)S(1)} %shard_map.72), channel_id=1, source_target_pairs={{128,0},{130,2},{132,4},{134,6},{136,8},{138,10},{140,12},{142,14}... | collective-permute-start | bytes 368648 | tf_op jit(solution)/shard_map/ppermute | solution.py:30
  22.4 8.6 %collective-permute-start.9 = (bf16[160,768]{1,0:T(8,128)(2,1)S(1)}, bf16[160,768]{1,0:T(8,128)(2,1)S(1)}, u32[]{:S(2)}, u32[]{:S(2)}) collective-permute-start(bf16[160,768]{1,0:T(8,128)(2,1)S(1)} %collective-permute-done.7.refs_0_.refs_10_), channel_id=1, source_target_pairs={{64,0},{66,2},{68,4},{70,6},{72,8},{74,10},{76,12},{78,14},{80,16}... | collective-permute-start | bytes 737288 | tf_op jit(solution)/shard_map/ppermute | solution.py:30
  27.7 6.3 %collective-permute-start.8 = (bf16[160,768]{1,0:T(8,128)(2,1)S(1)}, bf16[160,768]{1,0:T(8,128)(2,1)S(1)}, u32[]{:S(2)}, u32[]{:S(2)}) collective-permute-start(bf16[160,768]{1,0:T(8,128)(2,1)S(1)} %shard_map.70.refs_8_), channel_id=1, source_target_pairs={{64,0},{66,2},{68,4},{70,6},{72,8},{74,10},{76,12},{78,14},{80,16}... | collective-permute-start | bytes 737288 | tf_op jit(solution)/shard_map/ppermute | solution.py:30
  31.0 7.8 %collective-permute-start.13 = (bf16[240,768]{1,0:T(8,128)(2,1)S(1)}, bf16[240,768]{1,0:T(8,128)(2,1)S(1)}, u32[]{:S(2)}, u32[]{:S(2)}) collective-permute-start(bf16[240,768]{1,0:T(8,128)(2,1)S(1)} %shard_map.73.refs_11_), channel_id=1, source_target_pairs={{32,0},{34,2},{36,4},{38,6},{40,8},{42,10},{44,12},{46,14},{48,16}... | collective-permute-start | bytes 1105928 | tf_op jit(solution)/shard_map/ppermute | solution.py:30
  34.0 4.6 %collective-permute-start.12 = (bf16[160,768]{1,0:T(8,128)(2,1)S(1)}, bf16[160,768]{1,0:T(8,128)(2,1)}, u32[]{:S(2)}, u32[]{:S(2)}) collective-permute-start(bf16[160,768]{1,0:T(8,128)(2,1)S(1)} %collective-permute-done.7.refs_0_.refs_10_), channel_id=1, source_target_pairs={{32,0},{34,2},{36,4},{38,6},{40,8},{42,10},{44,12},{46,14},{48,16}... | collective-permute-start | bytes 737288 | tf_op jit(solution)/shard_map/ppermute | solution.py:30
  34.1 4.8 %collective-permute-start.11 = (bf16[160,768]{1,0:T(8,128)(2,1)S(1)}, bf16[160,768]{1,0:T(8,128)(2,1)}, u32[]{:S(2)}, u32[]{:S(2)}) collective-permute-start(bf16[160,768]{1,0:T(8,128)(2,1)S(1)} %collective-permute-done.8.refs_9_), channel_id=1, source_target_pairs={{32,0},{34,2},{36,4},{38,6},{40,8},{42,10},{44,12},{46,14},{48,16}... | collective-permute-start | bytes 737288 | tf_op jit(solution)/shard_map/ppermute | solution.py:30
  61.1 6.9 %collective-permute-start.20 = (bf16[560,768]{1,0:T(8,128)(2,1)S(1)}, bf16[560,768]{1,0:T(8,128)(2,1)S(1)}, u32[]{:S(2)}, u32[]{:S(2)}) collective-permute-start(bf16[560,768]{1,0:T(8,128)(2,1)S(1)} %get-tuple-element.73), channel_id=1, source_target_pairs={{32,0},{34,2},{36,4},{38,6},{40,8},{42,10},{44,12},{46,14},{48,16}... | collective-permute-start | bytes 2580488 | tf_op jit(solution)/shard_map/ppermute | solution.py:30
  65.9 15.7 %collective-permute-start.16 = (bf16[320,768]{1,0:T(8,128)(2,1)S(1)}, bf16[320,768]{1,0:T(8,128)(2,1)S(1)}, u32[]{:S(2)}, u32[]{:S(2)}) collective-permute-start(bf16[320,768]{1,0:T(8,128)(2,1)S(1)} %shard_map.79), channel_id=1, source_target_pairs={{8,0},{10,2},{12,4},{14,6},{16,8},{18,10},{20,12},{22,14},{24,16},... | collective-permute-start | bytes 1474568 | tf_op jit(solution)/shard_map/ppermute | solution.py:30
  66.6 15.0 %collective-permute-start.15 = (bf16[320,768]{1,0:T(8,128)(2,1)S(1)}, bf16[320,768]{1,0:T(8,128)(2,1)S(1)}, u32[]{:S(2)}, u32[]{:S(2)}) collective-permute-start(bf16[320,768]{1,0:T(8,128)(2,1)S(1)} %shard_map.78), channel_id=1, source_target_pairs={{16,0},{18,2},{20,4},{22,6},{24,8},{26,10},{28,12},{30,14},{0,16},... | collective-permute-start | bytes 1474568 | tf_op jit(solution)/shard_map/ppermute | solution.py:30
  68.1 13.6 %collective-permute-start.14 = (bf16[320,768]{1,0:T(8,128)(2,1)S(1)}, bf16[320,768]{1,0:T(8,128)(2,1)S(1)}, u32[]{:S(2)}, u32[]{:S(2)}) collective-permute-start(bf16[320,768]{1,0:T(8,128)(2,1)S(1)} %shard_map.77), channel_id=1, source_target_pairs={{24,0},{26,2},{28,4},{30,6},{0,8},{2,10},{4,12},{6,14},{8,16},{10,... | collective-permute-start | bytes 1474568 | tf_op jit(solution)/shard_map/ppermute | solution.py:30
  68.1 12.1 %collective-permute-start.22 = (bf16[160,768]{1,0:T(8,128)(2,1)S(1)}, bf16[160,768]{1,0:T(8,128)(2,1)S(1)}, u32[]{:S(2)}, u32[]{:S(2)}) collective-permute-start(bf16[160,768]{1,0:T(8,128)(2,1)S(1)} %shard_map.84), channel_id=1, source_target_pairs={{193,0},{195,2},{197,4},{199,6},{201,8},{203,10},{205,12},{207,14}... | collective-permute-start | bytes 737288 | tf_op jit(solution)/shard_map/ppermute | solution.py:30
  71.6 5.7 %collective-permute-start.23 = (bf16[80,768]{1,0:T(8,128)(2,1)S(1)}, bf16[80,768]{1,0:T(8,128)(2,1)S(1)}, u32[]{:S(2)}, u32[]{:S(2)}) collective-permute-start(bf16[80,768]{1,0:T(8,128)(2,1)S(1)} %shard_map.85), channel_id=1, source_target_pairs={{129,0},{131,2},{133,4},{135,6},{137,8},{139,10},{141,12},{143,14}... | collective-permute-start | bytes 368648 | tf_op jit(solution)/shard_map/ppermute | solution.py:30
  77.4 7.3 %collective-permute-start.21 = (bf16[160,768]{1,0:T(8,128)(2,1)S(1)}, bf16[160,768]{1,0:T(8,128)(2,1)S(1)}, u32[]{:S(2)}, u32[]{:S(2)}) collective-permute-start(bf16[160,768]{1,0:T(8,128)(2,1)S(1)} %shard_map.83), channel_id=1, source_target_pairs={{193,0},{195,2},{197,4},{199,6},{201,8},{203,10},{205,12},{207,14}... | collective-permute-start | bytes 737288 | tf_op jit(solution)/shard_map/ppermute | solution.py:30
  80.3 12.7 %copy-start.1 = (bf16[80,768]{1,0:T(8,128)(2,1)S(1)}, bf16[80,768]{1,0:T(8,128)(2,1)}, u32[]{:S(2)}) copy-start(bf16[80,768]{1,0:T(8,128)(2,1)} %src.6) | copy-start | bytes 368644
  80.3 13.7 %copy-start.3 = (bf16[80,768]{1,0:T(8,128)(2,1)S(1)}, bf16[80,768]{1,0:T(8,128)(2,1)}, u32[]{:S(2)}) copy-start(bf16[80,768]{1,0:T(8,128)(2,1)} %src.7) | copy-start | bytes 368644
  80.4 8.7 %collective-permute-start.24 = (bf16[160,768]{1,0:T(8,128)(2,1)S(1)}, bf16[160,768]{1,0:T(8,128)(2,1)S(1)}, u32[]{:S(2)}, u32[]{:S(2)}) collective-permute-start(bf16[160,768]{1,0:T(8,128)(2,1)S(1)} %shard_map.87), channel_id=1, source_target_pairs={{129,0},{131,2},{133,4},{135,6},{137,8},{139,10},{141,12},{143,14}... | collective-permute-start | bytes 737288 | tf_op jit(solution)/shard_map/ppermute | solution.py:30
  81.9 11.2 %collective-permute-start.17 = (bf16[80,768]{1,0:T(8,128)(2,1)S(1)}, bf16[80,768]{1,0:T(8,128)(2,1)S(1)}, u32[]{:S(2)}, u32[]{:S(2)}) collective-permute-start(bf16[80,768]{1,0:T(8,128)(2,1)S(1)} %get-tuple-element.68), channel_id=1, source_target_pairs={{6,0},{0,2},{2,4},{4,6},{14,8},{8,10},{10,12},{12,14},{22,16},{16,... | collective-permute-start | bytes 368648 | tf_op jit(solution)/shard_map/ppermute | solution.py:30
  82.0 11.1 %collective-permute-start.18 = (bf16[80,768]{1,0:T(8,128)(2,1)S(1)}, bf16[80,768]{1,0:T(8,128)(2,1)S(1)}, u32[]{:S(2)}, u32[]{:S(2)}) collective-permute-start(bf16[80,768]{1,0:T(8,128)(2,1)S(1)} %get-tuple-element.69), channel_id=1, source_target_pairs={{4,0},{6,2},{0,4},{2,6},{12,8},{14,10},{8,12},{10,14},{20,16},{22,... | collective-permute-start | bytes 368648 | tf_op jit(solution)/shard_map/ppermute | solution.py:30
  84.0 9.0 %collective-permute-start.19 = (bf16[80,768]{1,0:T(8,128)(2,1)S(1)}, bf16[80,768]{1,0:T(8,128)(2,1)S(1)}, u32[]{:S(2)}, u32[]{:S(2)}) collective-permute-start(bf16[80,768]{1,0:T(8,128)(2,1)S(1)} %get-tuple-element.70), channel_id=1, source_target_pairs={{2,0},{4,2},{6,4},{0,6},{10,8},{12,10},{14,12},{8,14},{18,16},{20,... | collective-permute-start | bytes 368648 | tf_op jit(solution)/shard_map/ppermute | solution.py:30
  89.2 4.8 %collective-permute-start.25 = (bf16[80,768]{1,0:T(8,128)(2,1)S(1)}, bf16[80,768]{1,0:T(8,128)(2,1)S(1)}, u32[]{:S(2)}, u32[]{:S(2)}) collective-permute-start(bf16[80,768]{1,0:T(8,128)(2,1)S(1)} %get-tuple-element.80), channel_id=1, source_target_pairs={{32,0},{34,2},{36,4},{38,6},{40,8},{42,10},{44,12},{46,14},{48,16}... | collective-permute-start | bytes 368648 | tf_op jit(solution)/shard_map/ppermute | solution.py:30

commit v6 on v4

--- a/solution.py
+++ b/solution.py
@@ -164,15 +164,16 @@
 
 def p_grads_kernel(first, temp, *refs):
     deltas, q_parts, outs = refs[:4], refs[4:8], refs[8:]
-    at = first
+    end = first + sum(out.shape[0] for out in outs)
+    total = None
+    for delta, q in zip(deltas, q_parts):
+        term = jnp.dot(delta[first:end, :], q[...], preferred_element_type=F32)
+        total = term if total is None else total + term
+    low = (temp[0] * total).astype(BF16)
+    at = 0
     for out in outs:
         size = out.shape[0]
-        total = jnp.zeros(out.shape, F32)
-        for delta, q in zip(deltas, q_parts):
-            total = total + jnp.dot(
-                delta[at : at + size, :], q[...], preferred_element_type=F32
-            )
-        out[...] = (temp[0] * total).astype(BF16)
+        out[...] = low[at : at + size, :]
         at += size
 
 

time: 94.1 us -> 94 us (level)
  the two profiles are of different devices: /device:TPU:49 before, /device:TPU:25 now
where the time goes in v6:
time: 94 us; the launch traced here: 93.7 us
  starting transfers between devices  40.6 us (43%)
  Pallas kernels  19.4 us (21%)
  waiting for transfers between devices  18.1 us (19%)
  blocking collectives  8.89 us (9%)
  local copies, waits for them, and re-layouts  5.16 us (5%)
  between operations  1.48 us (2%)
    ppermute x27, starting transfers between devices, fetch(): return lax.ppermute(array, AXES, pairs)  40.6 us
    pallas_call x22, Pallas kernels, call(): pl.pallas_call(kernel, out_shape=shapes, in_specs=in_specs, out_specs=vme...  19.4 us
    ppermute x27, waiting for transfers between devices, fetch(): return lax.ppermute(array, AXES, pairs)  18.1 us
    all_to_all x1, blocking collectives, local(): stats = lax.all_to_all(stat, ('y', 'x'), 0, 0, tiled=True)  8.89 us
    unnamed x19, local copies, waits for them, and re-layouts  4.92 us
  transfers between devices with their start and end apart: 27, of which 11 were waited for; matrix products, arithmetic and copies ran while one was open for 0% of the time, Pallas kernels for 7%

profile of v6, /device:TPU:25, one launch (start us, length us, event | category | flops | bytes accessed | tf_op | source)
XLA Modules:
  0.0 93.7 jit_solution(8127888099358188024)
XLA Ops:
  0.6 0.9 copy-done.2
  1.7 0.8 collective-permute-start.3
  2.4 0.9 copy-done
  3.4 1.8 %collective-permute-start.2 = (bf16[80,768]{1,0:T(8,128)(2,1)S(1)}, bf16[80,768]{1,0:T(8,128)(2,1)S(1)}, u32[]{:S(2)}, u32[]{:S(2)}) collective-permute-start(bf16[80,768]{1,0:T(8,128)(2,1)S(1)} %shard_map.67.refs_0_), channel_id=1, source_target_pairs={{6,0},{0,2},{2,4},{4,6},{14,8},{8,10},{10,12},{12,14},{22,16},{16,... | collective-permute-start | bytes 368648 | tf_op jit(solution)/shard_map/ppermute | solution.py:30
  5.2 0.6 collective-permute-start.1
  5.9 3.0 %collective-permute-start.8 = (bf16[160,768]{1,0:T(8,128)(2,1)S(1)}, bf16[160,768]{1,0:T(8,128)(2,1)S(1)}, u32[]{:S(2)}, u32[]{:S(2)}) collective-permute-start(bf16[160,768]{1,0:T(8,128)(2,1)S(1)} %shard_map.70.refs_8_), channel_id=1, source_target_pairs={{128,0},{130,2},{132,4},{134,6},{136,8},{138,10},{140,12},{142,14}... | collective-permute-start | bytes 737288 | tf_op jit(solution)/shard_map/ppermute | solution.py:30
  8.9 1.9 %collective-permute-done.1.refs_2_ = bf16[80,768]{1,0:T(8,128)(2,1)S(1)} collective-permute-done((bf16[80,768]{1,0:T(8,128)(2,1)S(1)}, bf16[80,768]{1,0:T(8,128)(2,1)S(1)}, u32[]{:S(2)}, u32[]{:S(2)}) %collective-permute-start.1) | collective-permute-done | bytes 122912 | tf_op jit(solution)/shard_map/ppermute | solution.py:30
  10.7 1.0 %collective-permute-done.refs_1_ = bf16[80,768]{1,0:T(8,128)(2,1)S(1)} collective-permute-done((bf16[80,768]{1,0:T(8,128)(2,1)S(1)}, bf16[80,768]{1,0:T(8,128)(2,1)S(1)}, u32[]{:S(2)}, u32[]{:S(2)}) %collective-permute-start) | collective-permute-done | bytes 122912 | tf_op jit(solution)/shard_map/ppermute | solution.py:30
  11.8 1.8 %collective-permute-start.4 = (bf16[320,768]{1,0:T(8,128)(2,1)S(1)}, bf16[320,768]{1,0:T(8,128)(2,1)S(1)}, u32[]{:S(2)}, u32[]{:S(2)}) collective-permute-start(bf16[320,768]{1,0:T(8,128)(2,1)S(1)} %shard_map.68.refs_0_.refs_4_), channel_id=1, source_target_pairs={{8,0},{10,2},{12,4},{14,6},{16,8},{18,10},{20,12},{22,14},{24,16},... | collective-permute-start | bytes 1474568 | tf_op jit(solution)/shard_map/ppermute | solution.py:30
  13.6 1.6 %collective-permute-start.7 = (bf16[160,768]{1,0:T(8,128)(2,1)S(1)}, bf16[160,768]{1,0:T(8,128)(2,1)S(1)}, u32[]{:S(2)}, u32[]{:S(2)}) collective-permute-start(bf16[160,768]{1,0:T(8,128)(2,1)S(1)} %shard_map.70.refs_8_), channel_id=1, source_target_pairs={{64,0},{66,2},{68,4},{70,6},{72,8},{74,10},{76,12},{78,14},{80,16}... | collective-permute-start | bytes 737288 | tf_op jit(solution)/shard_map/ppermute | solution.py:30
  15.2 0.8 collective-permute-done.8.refs_0_.refs_10_
  16.1 3.0 %collective-permute-start.9 = (bf16[160,768]{1,0:T(8,128)(2,1)S(1)}, bf16[160,768]{1,0:T(8,128)(2,1)S(1)}, u32[]{:S(2)}, u32[]{:S(2)}) collective-permute-start(bf16[160,768]{1,0:T(8,128)(2,1)S(1)} %collective-permute-done.8.refs_0_.refs_10_), channel_id=1, source_target_pairs={{64,0},{66,2},{68,4},{70,6},{72,8},{74,10},{76,12},{78,14},{80,16}... | collective-permute-start | bytes 737288 | tf_op jit(solution)/shard_map/ppermute | solution.py:30
  19.1 2.1 %collective-permute-start.10 = (bf16[80,768]{1,0:T(8,128)(2,1)S(1)}, bf16[80,768]{1,0:T(8,128)(2,1)S(1)}, u32[]{:S(2)}, u32[]{:S(2)}) collective-permute-start(bf16[80,768]{1,0:T(8,128)(2,1)S(1)} %shard_map.72), channel_id=1, source_target_pairs={{128,0},{130,2},{132,4},{134,6},{136,8},{138,10},{140,12},{142,14}... | collective-permute-start | bytes 368648 | tf_op jit(solution)/shard_map/ppermute | solution.py:30
  21.2 1.9 %collective-permute-done.7.refs_9_ = bf16[160,768]{1,0:T(8,128)(2,1)S(1)} collective-permute-done((bf16[160,768]{1,0:T(8,128)(2,1)S(1)}, bf16[160,768]{1,0:T(8,128)(2,1)S(1)}, u32[]{:S(2)}, u32[]{:S(2)}) %collective-permute-start.7) | collective-permute-done | bytes 245792 | tf_op jit(solution)/shard_map/ppermute | solution.py:30
  23.1 0.4 collective-permute-start.5
  23.4 5.0 %collective-permute-done.10.refs_12_ = bf16[80,768]{1,0:T(8,128)(2,1)S(1)} collective-permute-done((bf16[80,768]{1,0:T(8,128)(2,1)S(1)}, bf16[80,768]{1,0:T(8,128)(2,1)S(1)}, u32[]{:S(2)}, u32[]{:S(2)}) %collective-permute-start.10) | collective-permute-done | bytes 122912 | tf_op jit(solution)/shard_map/ppermute | solution.py:30
  28.4 3.3 %collective-permute-start.11 = (bf16[80,768]{1,0:T(8,128)(2,1)S(1)}, bf16[80,768]{1,0:T(8,128)(2,1)S(1)}, u32[]{:S(2)}, u32[]{:S(2)}) collective-permute-start(bf16[80,768]{1,0:T(8,128)(2,1)S(1)} %collective-permute-done.10.refs_12_), channel_id=1, source_target_pairs={{32,0},{34,2},{36,4},{38,6},{40,8},{42,10},{44,12},{46,14},{48,16}... | collective-permute-start | bytes 368648 | tf_op jit(solution)/shard_map/ppermute | solution.py:30
  31.7 0.6 copy-done.4
  32.4 0.5 collective-permute-start.14
  32.9 0.6 copy-done.6
  34.4 0.2 shard_map.71
  34.7 0.5 collective-permute-done.12.refs_14_
  35.2 0.9 copy-done.5
  36.1 0.9 copy-done.7
  37.0 6.8 %shard_map.73 = (bf16[1280,768]{1,0:T(8,128)(2,1)S(1)}, f32[16,2176]{1,0:T(8,128)S(1)}, bf16[1280,320]{1,0:T(8,128)(2,1)S(1)}, bf16[1280,320]{1,0:T(8,128)(2,1)S...) custom-call(f32[1]{0:T(128)} %bitcast.6.temp, ...), custom_call_target="tpu_custom_call" | custom-call | tf_op jit(solution)/shard_map/pallas_call | solution.py:234
  44.0 8.9 %all_to_all.11 = f32[16,1,2176]{2,1,0:T(1,128)S(1)} all-to-all(f32[16,1,2176]{2,1,0:T(1,128)S(1)} %copy.7), channel_id=1, replica_groups=mesh['zl'=4,'core'=2,'y'=4,'x'=4,'zh'=2] {'y','x'}, dimensions={0} | all-to-all | bytes 278528 | tf_op jit(solution)/shard_map/all_to_all | solution.py:331
  52.9 2.0 %shard_map.74 = (bf16[1280,320]{1,0:T(8,128)(2,1)S(1)}, bf16[1280,320]{1,0:T(8,128)(2,1)S(1)}, bf16[1280,320]{1,0:T(8,128)(2,1)S(1)}, bf16[1280,320]{1,0:T(8,128)(2,1)S(1)}, f32[1,80]{1,0:T(1,128)}) custom-call(f32[16,2176]{1,0:T(8,128)S(1)} %bitcast.12, bf16[1280,320]{1,0:T(8,128)(2,1)S(1)} %get-tuple-element.48.refs_0_, ...), custom_call_target="tpu_custom_call" | custom-call | tf_op jit(solution)/shard_map/pallas_call | solution.py:234
  54.9 2.7 %shard_map.81 = (bf16[160,768]{1,0:T(8,128)(2,1)S(1)}, bf16[80,768]{1,0:T(8,128)(2,1)S(1)}, bf16[560,768]{1,0:T(8,128)(2,1)S(1)}) custom-call(f32[1]{0:T(128)} %bitcast.11.temp, bf16[1280,320]{1,0:T(8,128)(2,1)S(1)} %get-tuple-element.58.refs_0_, bf16[1280,320]{1,0:T(8,128)(2,1)S(1)} %get-tuple-element.59.refs_1_.delta, ...), custom_call_target="tpu_custom_call" | custom-call | tf_op jit(solution)/shard_map/pallas_call | solution.py:234
  57.6 3.7 %collective-permute-start.21 = (bf16[560,768]{1,0:T(8,128)(2,1)S(1)}, bf16[560,768]{1,0:T(8,128)(2,1)S(1)}, u32[]{:S(2)}, u32[]{:S(2)}) collective-permute-start(bf16[560,768]{1,0:T(8,128)(2,1)S(1)} %get-tuple-element.69), channel_id=1, source_target_pairs={{32,0},{34,2},{36,4},{38,6},{40,8},{42,10},{44,12},{46,14},{48,16}... | collective-permute-start | bytes 2580488 | tf_op jit(solution)/shard_map/ppermute | solution.py:30
  61.4 0.9 shard_map.76
  62.2 0.9 shard_map.77
  63.1 0.9 shard_map.78
  64.0 1.0 %collective-permute-start.17 = (bf16[320,768]{1,0:T(8,128)(2,1)S(1)}, bf16[320,768]{1,0:T(8,128)(2,1)S(1)}, u32[]{:S(2)}, u32[]{:S(2)}) collective-permute-start(bf16[320,768]{1,0:T(8,128)(2,1)S(1)} %shard_map.78), channel_id=1, source_target_pairs={{8,0},{10,2},{12,4},{14,6},{16,8},{18,10},{20,12},{22,14},{24,16},... | collective-permute-start | bytes 1474568 | tf_op jit(solution)/shard_map/ppermute | solution.py:30
  65.0 1.1 %collective-permute-start.16 = (bf16[320,768]{1,0:T(8,128)(2,1)S(1)}, bf16[320,768]{1,0:T(8,128)(2,1)S(1)}, u32[]{:S(2)}, u32[]{:S(2)}) collective-permute-start(bf16[320,768]{1,0:T(8,128)(2,1)S(1)} %shard_map.77), channel_id=1, source_target_pairs={{16,0},{18,2},{20,4},{22,6},{24,8},{26,10},{28,12},{30,14},{0,16},... | collective-permute-start | bytes 1474568 | tf_op jit(solution)/shard_map/ppermute | solution.py:30
  66.2 1.6 %collective-permute-start.23 = (bf16[160,768]{1,0:T(8,128)(2,1)S(1)}, bf16[160,768]{1,0:T(8,128)(2,1)S(1)}, u32[]{:S(2)}, u32[]{:S(2)}) collective-permute-start(bf16[160,768]{1,0:T(8,128)(2,1)S(1)} %shard_map.83), channel_id=1, source_target_pairs={{193,0},{195,2},{197,4},{199,6},{201,8},{203,10},{205,12},{207,14}... | collective-permute-start | bytes 737288 | tf_op jit(solution)/shard_map/ppermute | solution.py:30
  67.9 1.5 %collective-permute-start.24 = (bf16[80,768]{1,0:T(8,128)(2,1)S(1)}, bf16[80,768]{1,0:T(8,128)(2,1)S(1)}, u32[]{:S(2)}, u32[]{:S(2)}) collective-permute-start(bf16[80,768]{1,0:T(8,128)(2,1)S(1)} %shard_map.84), channel_id=1, source_target_pairs={{129,0},{131,2},{133,4},{135,6},{137,8},{139,10},{141,12},{143,14}... | collective-permute-start | bytes 368648 | tf_op jit(solution)/shard_map/ppermute | solution.py:30
  69.3 2.4 %shard_map.75 = (bf16[160,768]{1,0:T(8,128)(2,1)S(1)}, bf16[160,768]{1,0:T(8,128)(2,1)S(1)}, bf16[160,768]{1,0:T(8,128)(2,1)S(1)}, bf16[320,768]{1,0:T(8,128)(2,1)S(1)}) custom-call(f32[1]{0:T(128)} %bitcast.7.temp, bf16[1280,768]{1,0:T(8,128)(2,1)S(1)} %get-tuple-element.57.p_all, bf16[1280,320]{1,0:T(8,128)(2,1)S(1)} %get-tuple-element.58.refs_0_, ...), custom_call_target="tpu_custom_call" | custom-call | tf_op jit(solution)/shard_map/pallas_call | solution.py:234
  71.8 3.9 %collective-permute-done.24.refs_3_ = bf16[80,768]{1,0:T(8,128)(2,1)S(1)} collective-permute-done((bf16[80,768]{1,0:T(8,128)(2,1)S(1)}, bf16[80,768]{1,0:T(8,128)(2,1)S(1)}, u32[]{:S(2)}, u32[]{:S(2)}) %collective-permute-start.24) | collective-permute-done | bytes 122912 | tf_op jit(solution)/shard_map/ppermute | solution.py:30
  75.8 2.3 %collective-permute-start.25 = (bf16[160,768]{1,0:T(8,128)(2,1)S(1)}, bf16[160,768]{1,0:T(8,128)(2,1)S(1)}, u32[]{:S(2)}, u32[]{:S(2)}) collective-permute-start(bf16[160,768]{1,0:T(8,128)(2,1)S(1)} %shard_map.86), channel_id=1, source_target_pairs={{129,0},{131,2},{133,4},{135,6},{137,8},{139,10},{141,12},{143,14}... | collective-permute-start | bytes 737288 | tf_op jit(solution)/shard_map/ppermute | solution.py:30
  78.2 1.4 %collective-permute-done.15.refs_1_ = bf16[320,768]{1,0:T(8,128)(2,1)S(1)} collective-permute-done((bf16[320,768]{1,0:T(8,128)(2,1)S(1)}, bf16[320,768]{1,0:T(8,128)(2,1)S(1)}, u32[]{:S(2)}, u32[]{:S(2)}) %collective-permute-start.15) | collective-permute-done | bytes 491552 | tf_op jit(solution)/shard_map/ppermute | solution.py:30
  79.6 0.2 shard_map.79
  79.8 2.0 %collective-permute-start.18 = (bf16[80,768]{1,0:T(8,128)(2,1)S(1)}, bf16[80,768]{1,0:T(8,128)(2,1)S(1)}, u32[]{:S(2)}, u32[]{:S(2)}) collective-permute-start(bf16[80,768]{1,0:T(8,128)(2,1)S(1)} %get-tuple-element.64), channel_id=1, source_target_pairs={{6,0},{0,2},{2,4},{4,6},{14,8},{8,10},{10,12},{12,14},{22,16},{16,... | collective-permute-start | bytes 368648 | tf_op jit(solution)/shard_map/ppermute | solution.py:30
  81.9 0.6 collective-permute-start.20
  82.5 1.0 %collective-permute-done.22.refs_1_ = bf16[160,768]{1,0:T(8,128)(2,1)S(1)} collective-permute-done((bf16[160,768]{1,0:T(8,128)(2,1)S(1)}, bf16[160,768]{1,0:T(8,128)(2,1)S(1)}, u32[]{:S(2)}, u32[]{:S(2)}) %collective-permute-start.22) | collective-permute-done | bytes 245792 | tf_op jit(solution)/shard_map/ppermute | solution.py:30
  83.5 0.6 collective-permute-done.25.refs_2_
  84.2 7.7 %collective-permute-start.26 = (bf16[80,768]{1,0:T(8,128)(2,1)S(1)}, bf16[80,768]{1,0:T(8,128)(2,1)S(1)}, u32[]{:S(2)}, u32[]{:S(2)}) collective-permute-start(bf16[80,768]{1,0:T(8,128)(2,1)S(1)} %get-tuple-element.76), channel_id=1, source_target_pairs={{32,0},{34,2},{36,4},{38,6},{40,8},{42,10},{44,12},{46,14},{48,16}... | collective-permute-start | bytes 368648 | tf_op jit(solution)/shard_map/ppermute | solution.py:30
  91.9 0.9 shard_map.80
  92.9 0.9 shard_map.88
  (50 shorter events, 1.5 us)
Async XLA Ops:
  0.6 0.9 copy-start.2
  1.5 32.8 %copy-start.8 = (s32[2560]{0:T(1024)S(1)}, s32[2560]{0:T(1024)}, u32[]{:S(2)}) copy-start(s32[2560]{0:T(1024)} %param.6) | copy-start | bytes 30724
  1.7 4.2 %collective-permute-start.3 = (bf16[80,768]{1,0:T(8,128)(2,1)S(1)}, bf16[80,768]{1,0:T(8,128)(2,1)S(1)}, u32[]{:S(2)}, u32[]{:S(2)}) collective-permute-start(bf16[80,768]{1,0:T(8,128)(2,1)S(1)} %shard_map.69.refs_0_), channel_id=1, source_target_pairs={{32,0},{34,2},{36,4},{38,6},{40,8},{42,10},{44,12},{46,14},{48,16}... | collective-permute-start | bytes 368648 | tf_op jit(solution)/shard_map/ppermute | solution.py:30
  2.4 0.9 copy-start
  3.4 5.4 %collective-permute-start.2 = (bf16[80,768]{1,0:T(8,128)(2,1)S(1)}, bf16[80,768]{1,0:T(8,128)(2,1)S(1)}, u32[]{:S(2)}, u32[]{:S(2)}) collective-permute-start(bf16[80,768]{1,0:T(8,128)(2,1)S(1)} %shard_map.67.refs_0_), channel_id=1, source_target_pairs={{6,0},{0,2},{2,4},{4,6},{14,8},{8,10},{10,12},{12,14},{22,16},{16,... | collective-permute-start | bytes 368648 | tf_op jit(solution)/shard_map/ppermute | solution.py:30
  5.2 5.5 %collective-permute-start.1 = (bf16[80,768]{1,0:T(8,128)(2,1)S(1)}, bf16[80,768]{1,0:T(8,128)(2,1)S(1)}, u32[]{:S(2)}, u32[]{:S(2)}) collective-permute-start(bf16[80,768]{1,0:T(8,128)(2,1)S(1)} %shard_map.67.refs_0_), channel_id=1, source_target_pairs={{4,0},{6,2},{0,4},{2,6},{12,8},{14,10},{8,12},{10,14},{20,16},{22,... | collective-permute-start | bytes 368648 | tf_op jit(solution)/shard_map/ppermute | solution.py:30
  5.8 6.0 %collective-permute-start = (bf16[80,768]{1,0:T(8,128)(2,1)S(1)}, bf16[80,768]{1,0:T(8,128)(2,1)S(1)}, u32[]{:S(2)}, u32[]{:S(2)}) collective-permute-start(bf16[80,768]{1,0:T(8,128)(2,1)S(1)} %shard_map.67.refs_0_), channel_id=1, source_target_pairs={{2,0},{4,2},{6,4},{0,6},{10,8},{12,10},{14,12},{8,14},{18,16},{20,... | collective-permute-start | bytes 368648 | tf_op jit(solution)/shard_map/ppermute | solution.py:30
  5.9 10.2 %collective-permute-start.8 = (bf16[160,768]{1,0:T(8,128)(2,1)S(1)}, bf16[160,768]{1,0:T(8,128)(2,1)S(1)}, u32[]{:S(2)}, u32[]{:S(2)}) collective-permute-start(bf16[160,768]{1,0:T(8,128)(2,1)S(1)} %shard_map.70.refs_8_), channel_id=1, source_target_pairs={{128,0},{130,2},{132,4},{134,6},{136,8},{138,10},{140,12},{142,14}... | collective-permute-start | bytes 737288 | tf_op jit(solution)/shard_map/ppermute | solution.py:30
  11.8 20.6 %collective-permute-start.4 = (bf16[320,768]{1,0:T(8,128)(2,1)S(1)}, bf16[320,768]{1,0:T(8,128)(2,1)S(1)}, u32[]{:S(2)}, u32[]{:S(2)}) collective-permute-start(bf16[320,768]{1,0:T(8,128)(2,1)S(1)} %shard_map.68.refs_0_.refs_4_), channel_id=1, source_target_pairs={{8,0},{10,2},{12,4},{14,6},{16,8},{18,10},{20,12},{22,14},{24,16},... | collective-permute-start | bytes 1474568 | tf_op jit(solution)/shard_map/ppermute | solution.py:30
  13.6 9.5 %collective-permute-start.7 = (bf16[160,768]{1,0:T(8,128)(2,1)S(1)}, bf16[160,768]{1,0:T(8,128)(2,1)S(1)}, u32[]{:S(2)}, u32[]{:S(2)}) collective-permute-start(bf16[160,768]{1,0:T(8,128)(2,1)S(1)} %shard_map.70.refs_8_), channel_id=1, source_target_pairs={{64,0},{66,2},{68,4},{70,6},{72,8},{74,10},{76,12},{78,14},{80,16}... | collective-permute-start | bytes 737288 | tf_op jit(solution)/shard_map/ppermute | solution.py:30
  15.2 19.4 %collective-permute-start.6 = (bf16[320,768]{1,0:T(8,128)(2,1)S(1)}, bf16[320,768]{1,0:T(8,128)(2,1)S(1)}, u32[]{:S(2)}, u32[]{:S(2)}) collective-permute-start(bf16[320,768]{1,0:T(8,128)(2,1)S(1)} %shard_map.68.refs_0_.refs_4_), channel_id=1, source_target_pairs={{24,0},{26,2},{28,4},{30,6},{0,8},{2,10},{4,12},{6,14},{8,16},{10,... | collective-permute-start | bytes 1474568 | tf_op jit(solution)/shard_map/ppermute | solution.py:30
  16.1 16.3 %collective-permute-start.9 = (bf16[160,768]{1,0:T(8,128)(2,1)S(1)}, bf16[160,768]{1,0:T(8,128)(2,1)S(1)}, u32[]{:S(2)}, u32[]{:S(2)}) collective-permute-start(bf16[160,768]{1,0:T(8,128)(2,1)S(1)} %collective-permute-done.8.refs_0_.refs_10_), channel_id=1, source_target_pairs={{64,0},{66,2},{68,4},{70,6},{72,8},{74,10},{76,12},{78,14},{80,16}... | collective-permute-start | bytes 737288 | tf_op jit(solution)/shard_map/ppermute | solution.py:30
  19.1 9.4 %collective-permute-start.10 = (bf16[80,768]{1,0:T(8,128)(2,1)S(1)}, bf16[80,768]{1,0:T(8,128)(2,1)S(1)}, u32[]{:S(2)}, u32[]{:S(2)}) collective-permute-start(bf16[80,768]{1,0:T(8,128)(2,1)S(1)} %shard_map.72), channel_id=1, source_target_pairs={{128,0},{130,2},{132,4},{134,6},{136,8},{138,10},{140,12},{142,14}... | collective-permute-start | bytes 368648 | tf_op jit(solution)/shard_map/ppermute | solution.py:30
  23.1 11.6 %collective-permute-start.5 = (bf16[320,768]{1,0:T(8,128)(2,1)S(1)}, bf16[320,768]{1,0:T(8,128)(2,1)S(1)}, u32[]{:S(2)}, u32[]{:S(2)}) collective-permute-start(bf16[320,768]{1,0:T(8,128)(2,1)S(1)} %shard_map.68.refs_0_.refs_4_), channel_id=1, source_target_pairs={{16,0},{18,2},{20,4},{22,6},{24,8},{26,10},{28,12},{30,14},{0,16},... | collective-permute-start | bytes 1474568 | tf_op jit(solution)/shard_map/ppermute | solution.py:30
  28.4 4.4 %collective-permute-start.11 = (bf16[80,768]{1,0:T(8,128)(2,1)S(1)}, bf16[80,768]{1,0:T(8,128)(2,1)S(1)}, u32[]{:S(2)}, u32[]{:S(2)}) collective-permute-start(bf16[80,768]{1,0:T(8,128)(2,1)S(1)} %collective-permute-done.10.refs_12_), channel_id=1, source_target_pairs={{32,0},{34,2},{36,4},{38,6},{40,8},{42,10},{44,12},{46,14},{48,16}... | collective-permute-start | bytes 368648 | tf_op jit(solution)/shard_map/ppermute | solution.py:30
  31.7 0.6 copy-start.4
  32.4 2.3 %collective-permute-start.13 = (bf16[160,768]{1,0:T(8,128)(2,1)S(1)}, bf16[160,768]{1,0:T(8,128)(2,1)S(1)}, u32[]{:S(2)}, u32[]{:S(2)}) collective-permute-start(bf16[160,768]{1,0:T(8,128)(2,1)S(1)} %collective-permute-done.8.refs_0_.refs_10_), channel_id=1, source_target_pairs={{32,0},{34,2},{36,4},{38,6},{40,8},{42,10},{44,12},{46,14},{48,16}... | collective-permute-start | bytes 737288 | tf_op jit(solution)/shard_map/ppermute | solution.py:30
  32.4 2.3 %collective-permute-start.14 = (bf16[160,768]{1,0:T(8,128)(2,1)S(1)}, bf16[160,768]{1,0:T(8,128)(2,1)S(1)}, u32[]{:S(2)}, u32[]{:S(2)}) collective-permute-start(bf16[160,768]{1,0:T(8,128)(2,1)S(1)} %collective-permute-done.9.refs_11_), channel_id=1, source_target_pairs={{32,0},{34,2},{36,4},{38,6},{40,8},{42,10},{44,12},{46,14},{48,16}... | collective-permute-start | bytes 737288 | tf_op jit(solution)/shard_map/ppermute | solution.py:30
  32.9 0.6 copy-start.6
  33.5 1.6 %collective-permute-start.12 = (bf16[160,768]{1,0:T(8,128)(2,1)S(1)}, bf16[160,768]{1,0:T(8,128)(2,1)}, u32[]{:S(2)}, u32[]{:S(2)}) collective-permute-start(bf16[160,768]{1,0:T(8,128)(2,1)S(1)} %collective-permute-done.7.refs_9_), channel_id=1, source_target_pairs={{32,0},{34,2},{36,4},{38,6},{40,8},{42,10},{44,12},{46,14},{48,16}... | collective-permute-start | bytes 737288 | tf_op jit(solution)/shard_map/ppermute | solution.py:30
  35.2 0.9 copy-start.5
  36.1 0.9 copy-start.7
  57.6 8.5 %collective-permute-start.21 = (bf16[560,768]{1,0:T(8,128)(2,1)S(1)}, bf16[560,768]{1,0:T(8,128)(2,1)S(1)}, u32[]{:S(2)}, u32[]{:S(2)}) collective-permute-start(bf16[560,768]{1,0:T(8,128)(2,1)S(1)} %get-tuple-element.69), channel_id=1, source_target_pairs={{32,0},{34,2},{36,4},{38,6},{40,8},{42,10},{44,12},{46,14},{48,16}... | collective-permute-start | bytes 2580488 | tf_op jit(solution)/shard_map/ppermute | solution.py:30
  64.0 14.1 %collective-permute-start.17 = (bf16[320,768]{1,0:T(8,128)(2,1)S(1)}, bf16[320,768]{1,0:T(8,128)(2,1)S(1)}, u32[]{:S(2)}, u32[]{:S(2)}) collective-permute-start(bf16[320,768]{1,0:T(8,128)(2,1)S(1)} %shard_map.78), channel_id=1, source_target_pairs={{8,0},{10,2},{12,4},{14,6},{16,8},{18,10},{20,12},{22,14},{24,16},... | collective-permute-start | bytes 1474568 | tf_op jit(solution)/shard_map/ppermute | solution.py:30
  65.0 13.2 %collective-permute-start.16 = (bf16[320,768]{1,0:T(8,128)(2,1)S(1)}, bf16[320,768]{1,0:T(8,128)(2,1)S(1)}, u32[]{:S(2)}, u32[]{:S(2)}) collective-permute-start(bf16[320,768]{1,0:T(8,128)(2,1)S(1)} %shard_map.77), channel_id=1, source_target_pairs={{16,0},{18,2},{20,4},{22,6},{24,8},{26,10},{28,12},{30,14},{0,16},... | collective-permute-start | bytes 1474568 | tf_op jit(solution)/shard_map/ppermute | solution.py:30
  66.1 13.5 %collective-permute-start.15 = (bf16[320,768]{1,0:T(8,128)(2,1)S(1)}, bf16[320,768]{1,0:T(8,128)(2,1)S(1)}, u32[]{:S(2)}, u32[]{:S(2)}) collective-permute-start(bf16[320,768]{1,0:T(8,128)(2,1)S(1)} %shard_map.76), channel_id=1, source_target_pairs={{24,0},{26,2},{28,4},{30,6},{0,8},{2,10},{4,12},{6,14},{8,16},{10,... | collective-permute-start | bytes 1474568 | tf_op jit(solution)/shard_map/ppermute | solution.py:30
  66.2 9.4 %collective-permute-start.23 = (bf16[160,768]{1,0:T(8,128)(2,1)S(1)}, bf16[160,768]{1,0:T(8,128)(2,1)S(1)}, u32[]{:S(2)}, u32[]{:S(2)}) collective-permute-start(bf16[160,768]{1,0:T(8,128)(2,1)S(1)} %shard_map.83), channel_id=1, source_target_pairs={{193,0},{195,2},{197,4},{199,6},{201,8},{203,10},{205,12},{207,14}... | collective-permute-start | bytes 737288 | tf_op jit(solution)/shard_map/ppermute | solution.py:30
  67.9 7.8 %collective-permute-start.24 = (bf16[80,768]{1,0:T(8,128)(2,1)S(1)}, bf16[80,768]{1,0:T(8,128)(2,1)S(1)}, u32[]{:S(2)}, u32[]{:S(2)}) collective-permute-start(bf16[80,768]{1,0:T(8,128)(2,1)S(1)} %shard_map.84), channel_id=1, source_target_pairs={{129,0},{131,2},{133,4},{135,6},{137,8},{139,10},{141,12},{143,14}... | collective-permute-start | bytes 368648 | tf_op jit(solution)/shard_map/ppermute | solution.py:30
  75.6 7.9 %collective-permute-start.22 = (bf16[160,768]{1,0:T(8,128)(2,1)S(1)}, bf16[160,768]{1,0:T(8,128)(2,1)S(1)}, u32[]{:S(2)}, u32[]{:S(2)}) collective-permute-start(bf16[160,768]{1,0:T(8,128)(2,1)S(1)} %shard_map.82), channel_id=1, source_target_pairs={{193,0},{195,2},{197,4},{199,6},{201,8},{203,10},{205,12},{207,14}... | collective-permute-start | bytes 737288 | tf_op jit(solution)/shard_map/ppermute | solution.py:30
  75.8 16.1 %copy-start.1 = (bf16[80,768]{1,0:T(8,128)(2,1)S(1)}, bf16[80,768]{1,0:T(8,128)(2,1)}, u32[]{:S(2)}) copy-start(bf16[80,768]{1,0:T(8,128)(2,1)} %src.6) | copy-start | bytes 368644
  75.8 17.1 %copy-start.3 = (bf16[80,768]{1,0:T(8,128)(2,1)S(1)}, bf16[80,768]{1,0:T(8,128)(2,1)}, u32[]{:S(2)}) copy-start(bf16[80,768]{1,0:T(8,128)(2,1)} %src.7) | copy-start | bytes 368644
  75.8 8.3 %collective-permute-start.25 = (bf16[160,768]{1,0:T(8,128)(2,1)S(1)}, bf16[160,768]{1,0:T(8,128)(2,1)S(1)}, u32[]{:S(2)}, u32[]{:S(2)}) collective-permute-start(bf16[160,768]{1,0:T(8,128)(2,1)S(1)} %shard_map.86), channel_id=1, source_target_pairs={{129,0},{131,2},{133,4},{135,6},{137,8},{139,10},{141,12},{143,14}... | collective-permute-start | bytes 737288 | tf_op jit(solution)/shard_map/ppermute | solution.py:30
  79.8 12.1 %collective-permute-start.18 = (bf16[80,768]{1,0:T(8,128)(2,1)S(1)}, bf16[80,768]{1,0:T(8,128)(2,1)S(1)}, u32[]{:S(2)}, u32[]{:S(2)}) collective-permute-start(bf16[80,768]{1,0:T(8,128)(2,1)S(1)} %get-tuple-element.64), channel_id=1, source_target_pairs={{6,0},{0,2},{2,4},{4,6},{14,8},{8,10},{10,12},{12,14},{22,16},{16,... | collective-permute-start | bytes 368648 | tf_op jit(solution)/shard_map/ppermute | solution.py:30
  81.8 10.0 %collective-permute-start.19 = (bf16[80,768]{1,0:T(8,128)(2,1)S(1)}, bf16[80,768]{1,0:T(8,128)(2,1)S(1)}, u32[]{:S(2)}, u32[]{:S(2)}) collective-permute-start(bf16[80,768]{1,0:T(8,128)(2,1)S(1)} %get-tuple-element.65), channel_id=1, source_target_pairs={{4,0},{6,2},{0,4},{2,6},{12,8},{14,10},{8,12},{10,14},{20,16},{22,... | collective-permute-start | bytes 368648 | tf_op jit(solution)/shard_map/ppermute | solution.py:30
  81.9 10.0 %collective-permute-start.20 = (bf16[80,768]{1,0:T(8,128)(2,1)S(1)}, bf16[80,768]{1,0:T(8,128)(2,1)S(1)}, u32[]{:S(2)}, u32[]{:S(2)}) collective-permute-start(bf16[80,768]{1,0:T(8,128)(2,1)S(1)} %get-tuple-element.66), channel_id=1, source_target_pairs={{2,0},{4,2},{6,4},{0,6},{10,8},{12,10},{14,12},{8,14},{18,16},{20,... | collective-permute-start | bytes 368648 | tf_op jit(solution)/shard_map/ppermute | solution.py:30
  84.2 8.7 %collective-permute-start.26 = (bf16[80,768]{1,0:T(8,128)(2,1)S(1)}, bf16[80,768]{1,0:T(8,128)(2,1)S(1)}, u32[]{:S(2)}, u32[]{:S(2)}) collective-permute-start(bf16[80,768]{1,0:T(8,128)(2,1)S(1)} %get-tuple-element.76), channel_id=1, source_target_pairs={{32,0},{34,2},{36,4},{38,6},{40,8},{42,10},{44,12},{46,14},{48,16}... | collective-permute-start | bytes 368648 | tf_op jit(solution)/shard_map/ppermute | solution.py:30

commit v7 on v4

--- a/solution.py
+++ b/solution.py
@@ -84,8 +84,8 @@
 
 
 def logits_kernel(rows, chunk, temp, *refs):
-    q_parts, targets, p_parts = refs[:4], refs[4:8], refs[8:17]
-    p_all, stat, e_outs, row_outs, logits = refs[17], refs[18], refs[19:23], refs[23:27], refs[27]
+    q_parts, targets, p_parts = refs[:4], refs[4:8], refs[8:16]
+    p_all, stat, e_outs, row_outs, logits = refs[16], refs[17], refs[18:22], refs[22:26], refs[26]
     count = p_all.shape[0]
     scale = temp[0]
     at = 0
@@ -266,7 +266,9 @@
     four = along_z(join(rows, relay), 2)
     one_b = swap(after(one, far[0]))
     two_b = swap(two)
-    return [near, *far], [pair, one, two, three, four, swap(four), one_b, two_b, swap(three)]
+    fours = join(2 * rows, four, swap(four))
+    three_b = swap(three)
+    return [near, *far], [pair, one, two, three, fours, one_b, two_b, three_b]
 
 
 def add(sizes, *terms):
@@ -322,7 +324,7 @@
         [shape((count, width), BF16), shape((16, 17 * 128), F32)]
         + [shape((count, part_rows), BF16)] * 4
         + [shape((8, part_rows), F32)] * 4,
-        smem(1) + vmem(17),
+        smem(1) + vmem(16),
         (temp, *q_parts, *targets, *p_parts),
         [pltpu.VMEM((2, count, part_rows), F32)],
     )

time: 94.1 us -> 93.8 us (level)
    pallas_call x22 -> x23, Pallas kernels: 19.6 us -> 19.6 us  [call(): pl.pallas_call(kernel, out_shape=shapes, in_specs=in_specs, out_specs=vme...]
  transfers between devices with their start and end apart: 27 -> 27, of which waited for: 9 -> 8; matrix products, arithmetic and copies ran while one was open for 0% -> 0% of each run, Pallas kernels for 7% -> 7%
where the time goes in v7:
time: 93.8 us; the launch traced here: 93.6 us
  starting transfers between devices  47.4 us (51%)
  Pallas kernels  19.6 us (21%)
  waiting for transfers between devices  11 us (12%)
  blocking collectives  8.82 us (9%)
  local copies, waits for them, and re-layouts  5.16 us (6%)
  between operations  1.52 us (2%)
    ppermute x27, starting transfers between devices, fetch(): return lax.ppermute(array, AXES, pairs)  47.4 us
    pallas_call x23, Pallas kernels, call(): pl.pallas_call(kernel, out_shape=shapes, in_specs=in_specs, out_specs=vme...  19.6 us
    ppermute x27, waiting for transfers between devices, fetch(): return lax.ppermute(array, AXES, pairs)  11 us
    all_to_all x1, blocking collectives, local(): stats = lax.all_to_all(stat, ('y', 'x'), 0, 0, tiled=True)  8.82 us
    unnamed x19, local copies, waits for them, and re-layouts  4.92 us
  transfers between devices with their start and end apart: 27, of which 8 were waited for; matrix products, arithmetic and copies ran while one was open for 0% of the time, Pallas kernels for 7%

profile of v7, /device:TPU:49, one launch (start us, length us, event | category | flops | bytes accessed | tf_op | source)
XLA Modules:
  0.0 93.6 jit_solution(17396950602734887063)
XLA Ops:
  0.6 0.9 copy-done.2
  1.7 0.8 collective-permute-start.3
  2.4 0.9 copy-done
  3.4 1.1 %collective-permute-start.2 = (bf16[80,768]{1,0:T(8,128)(2,1)S(1)}, bf16[80,768]{1,0:T(8,128)(2,1)S(1)}, u32[]{:S(2)}, u32[]{:S(2)}) collective-permute-start(bf16[80,768]{1,0:T(8,128)(2,1)S(1)} %shard_map.67.refs_0_), channel_id=1, source_target_pairs={{6,0},{0,2},{2,4},{4,6},{14,8},{8,10},{10,12},{12,14},{22,16},{16,... | collective-permute-start | bytes 368648 | tf_op jit(solution)/shard_map/ppermute | solution.py:30
  4.5 0.3 collective-permute-start.1
  4.9 0.9 collective-permute-start
  5.8 3.1 %collective-permute-start.8 = (bf16[160,768]{1,0:T(8,128)(2,1)S(1)}, bf16[160,768]{1,0:T(8,128)(2,1)S(1)}, u32[]{:S(2)}, u32[]{:S(2)}) collective-permute-start(bf16[160,768]{1,0:T(8,128)(2,1)S(1)} %shard_map.70.refs_8_), channel_id=1, source_target_pairs={{128,0},{130,2},{132,4},{134,6},{136,8},{138,10},{140,12},{142,14}... | collective-permute-start | bytes 737288 | tf_op jit(solution)/shard_map/ppermute | solution.py:30
  8.9 0.9 collective-permute-done.1.refs_2_
  9.8 0.9 %collective-permute-done.refs_1_ = bf16[80,768]{1,0:T(8,128)(2,1)S(1)} collective-permute-done((bf16[80,768]{1,0:T(8,128)(2,1)S(1)}, bf16[80,768]{1,0:T(8,128)(2,1)S(1)}, u32[]{:S(2)}, u32[]{:S(2)}) %collective-permute-start) | collective-permute-done | bytes 122912 | tf_op jit(solution)/shard_map/ppermute | solution.py:30
  10.7 2.3 %collective-permute-start.4 = (bf16[320,768]{1,0:T(8,128)(2,1)S(1)}, bf16[320,768]{1,0:T(8,128)(2,1)S(1)}, u32[]{:S(2)}, u32[]{:S(2)}) collective-permute-start(bf16[320,768]{1,0:T(8,128)(2,1)S(1)} %shard_map.68.refs_0_.refs_4_), channel_id=1, source_target_pairs={{8,0},{10,2},{12,4},{14,6},{16,8},{18,10},{20,12},{22,14},{24,16},... | collective-permute-start | bytes 1474568 | tf_op jit(solution)/shard_map/ppermute | solution.py:30
  13.0 1.6 %collective-permute-start.7 = (bf16[160,768]{1,0:T(8,128)(2,1)S(1)}, bf16[160,768]{1,0:T(8,128)(2,1)S(1)}, u32[]{:S(2)}, u32[]{:S(2)}) collective-permute-start(bf16[160,768]{1,0:T(8,128)(2,1)S(1)} %shard_map.70.refs_8_), channel_id=1, source_target_pairs={{64,0},{66,2},{68,4},{70,6},{72,8},{74,10},{76,12},{78,14},{80,16}... | collective-permute-start | bytes 737288 | tf_op jit(solution)/shard_map/ppermute | solution.py:30
  14.6 2.7 %collective-permute-done.8.refs_0_.refs_10_ = bf16[160,768]{1,0:T(8,128)(2,1)S(1)} collective-permute-done((bf16[160,768]{1,0:T(8,128)(2,1)S(1)}, bf16[160,768]{1,0:T(8,128)(2,1)S(1)}, u32[]{:S(2)}, u32[]{:S(2)}) %collective-permute-start.8) | collective-permute-done | bytes 245792 | tf_op jit(solution)/shard_map/ppermute | solution.py:30
  17.5 4.0 %collective-permute-start.10 = (bf16[80,768]{1,0:T(8,128)(2,1)S(1)}, bf16[80,768]{1,0:T(8,128)(2,1)S(1)}, u32[]{:S(2)}, u32[]{:S(2)}) collective-permute-start(bf16[80,768]{1,0:T(8,128)(2,1)S(1)} %shard_map.72), channel_id=1, source_target_pairs={{128,0},{130,2},{132,4},{134,6},{136,8},{138,10},{140,12},{142,14}... | collective-permute-start | bytes 368648 | tf_op jit(solution)/shard_map/ppermute | solution.py:30
  21.5 2.8 %collective-permute-start.5 = (bf16[320,768]{1,0:T(8,128)(2,1)S(1)}, bf16[320,768]{1,0:T(8,128)(2,1)S(1)}, u32[]{:S(2)}, u32[]{:S(2)}) collective-permute-start(bf16[320,768]{1,0:T(8,128)(2,1)S(1)} %shard_map.68.refs_0_.refs_4_), channel_id=1, source_target_pairs={{16,0},{18,2},{20,4},{22,6},{24,8},{26,10},{28,12},{30,14},{0,16},... | collective-permute-start | bytes 1474568 | tf_op jit(solution)/shard_map/ppermute | solution.py:30
  24.4 1.8 %collective-permute-done.10.refs_0_ = bf16[80,768]{1,0:T(8,128)(2,1)S(1)} collective-permute-done((bf16[80,768]{1,0:T(8,128)(2,1)S(1)}, bf16[80,768]{1,0:T(8,128)(2,1)S(1)}, u32[]{:S(2)}, u32[]{:S(2)}) %collective-permute-start.10) | collective-permute-done | bytes 122912 | tf_op jit(solution)/shard_map/ppermute | solution.py:30
  26.2 4.8 %collective-permute-start.11 = (bf16[80,768]{1,0:T(8,128)(2,1)S(1)}, bf16[80,768]{1,0:T(8,128)(2,1)S(1)}, u32[]{:S(2)}, u32[]{:S(2)}) collective-permute-start(bf16[80,768]{1,0:T(8,128)(2,1)S(1)} %collective-permute-done.10.refs_0_), channel_id=1, source_target_pairs={{32,0},{34,2},{36,4},{38,6},{40,8},{42,10},{44,12},{46,14},{48,16}... | collective-permute-start | bytes 368648 | tf_op jit(solution)/shard_map/ppermute | solution.py:30
  31.0 0.6 copy-done.4
  31.6 0.5 collective-permute-start.14
  32.1 0.6 copy-done.6
  32.8 0.2 collective-permute-start.12
  33.7 0.2 shard_map.71
  33.9 0.9 copy-done.5
  34.8 0.9 copy-done.7
  35.8 6.9 %shard_map.74 = (bf16[1280,768]{1,0:T(8,128)(2,1)S(1)}, f32[16,2176]{1,0:T(8,128)S(1)}, bf16[1280,320]{1,0:T(8,128)(2,1)S(1)}, bf16[1280,320]{1,0:T(8,128)(2,1)S...) custom-call(f32[1]{0:T(128)} %bitcast.6.temp, ...), custom_call_target="tpu_custom_call" | custom-call | tf_op jit(solution)/shard_map/pallas_call | solution.py:233
  42.7 0.2 copy.7
  42.8 8.8 %all_to_all.11 = f32[16,1,2176]{2,1,0:T(1,128)S(1)} all-to-all(f32[16,1,2176]{2,1,0:T(1,128)S(1)} %copy.7), channel_id=1, replica_groups=mesh['zl'=4,'core'=2,'y'=4,'x'=4,'zh'=2] {'y','x'}, dimensions={0} | all-to-all | bytes 278528 | tf_op jit(solution)/shard_map/all_to_all | solution.py:332
  51.7 2.0 %shard_map.75 = (bf16[1280,320]{1,0:T(8,128)(2,1)S(1)}, bf16[1280,320]{1,0:T(8,128)(2,1)S(1)}, bf16[1280,320]{1,0:T(8,128)(2,1)S(1)}, bf16[1280,320]{1,0:T(8,128)(2,1)S(1)}, f32[1,80]{1,0:T(1,128)}) custom-call(f32[16,2176]{1,0:T(8,128)S(1)} %bitcast.12, bf16[1280,320]{1,0:T(8,128)(2,1)S(1)} %get-tuple-element.48.refs_0_, ...), custom_call_target="tpu_custom_call" | custom-call | tf_op jit(solution)/shard_map/pallas_call | solution.py:233
  53.7 2.9 %shard_map.82 = (bf16[160,768]{1,0:T(8,128)(2,1)S(1)}, bf16[80,768]{1,0:T(8,128)(2,1)S(1)}, bf16[560,768]{1,0:T(8,128)(2,1)S(1)}) custom-call(f32[1]{0:T(128)} %bitcast.11.temp, bf16[1280,320]{1,0:T(8,128)(2,1)S(1)} %get-tuple-element.58.refs_0_, bf16[1280,320]{1,0:T(8,128)(2,1)S(1)} %get-tuple-element.59.refs_1_.delta, ...), custom_call_target="tpu_custom_call" | custom-call | tf_op jit(solution)/shard_map/pallas_call | solution.py:233
  56.6 3.1 %collective-permute-start.21 = (bf16[560,768]{1,0:T(8,128)(2,1)S(1)}, bf16[560,768]{1,0:T(8,128)(2,1)S(1)}, u32[]{:S(2)}, u32[]{:S(2)}) collective-permute-start(bf16[560,768]{1,0:T(8,128)(2,1)S(1)} %get-tuple-element.69), channel_id=1, source_target_pairs={{32,0},{34,2},{36,4},{38,6},{40,8},{42,10},{44,12},{46,14},{48,16}... | collective-permute-start | bytes 2580488 | tf_op jit(solution)/shard_map/ppermute | solution.py:30
  59.6 0.9 shard_map.77
  60.5 0.9 shard_map.78
  61.4 0.9 shard_map.79
  62.3 1.0 %collective-permute-start.17 = (bf16[320,768]{1,0:T(8,128)(2,1)S(1)}, bf16[320,768]{1,0:T(8,128)(2,1)S(1)}, u32[]{:S(2)}, u32[]{:S(2)}) collective-permute-start(bf16[320,768]{1,0:T(8,128)(2,1)S(1)} %shard_map.79), channel_id=1, source_target_pairs={{8,0},{10,2},{12,4},{14,6},{16,8},{18,10},{20,12},{22,14},{24,16},... | collective-permute-start | bytes 1474568 | tf_op jit(solution)/shard_map/ppermute | solution.py:30
  63.3 1.1 %collective-permute-start.16 = (bf16[320,768]{1,0:T(8,128)(2,1)S(1)}, bf16[320,768]{1,0:T(8,128)(2,1)S(1)}, u32[]{:S(2)}, u32[]{:S(2)}) collective-permute-start(bf16[320,768]{1,0:T(8,128)(2,1)S(1)} %shard_map.78), channel_id=1, source_target_pairs={{16,0},{18,2},{20,4},{22,6},{24,8},{26,10},{28,12},{30,14},{0,16},... | collective-permute-start | bytes 1474568 | tf_op jit(solution)/shard_map/ppermute | solution.py:30
  64.6 2.8 %collective-permute-start.24 = (bf16[80,768]{1,0:T(8,128)(2,1)S(1)}, bf16[80,768]{1,0:T(8,128)(2,1)S(1)}, u32[]{:S(2)}, u32[]{:S(2)}) collective-permute-start(bf16[80,768]{1,0:T(8,128)(2,1)S(1)} %shard_map.85), channel_id=1, source_target_pairs={{129,0},{131,2},{133,4},{135,6},{137,8},{139,10},{141,12},{143,14}... | collective-permute-start | bytes 368648 | tf_op jit(solution)/shard_map/ppermute | solution.py:30
  67.4 2.4 %shard_map.76 = (bf16[160,768]{1,0:T(8,128)(2,1)S(1)}, bf16[160,768]{1,0:T(8,128)(2,1)S(1)}, bf16[160,768]{1,0:T(8,128)(2,1)S(1)}, bf16[320,768]{1,0:T(8,128)(2,1)S(1)}) custom-call(f32[1]{0:T(128)} %bitcast.7.temp, bf16[1280,768]{1,0:T(8,128)(2,1)S(1)} %get-tuple-element.57.p_all, bf16[1280,320]{1,0:T(8,128)(2,1)S(1)} %get-tuple-element.58.refs_0_, ...), custom_call_target="tpu_custom_call" | custom-call | tf_op jit(solution)/shard_map/pallas_call | solution.py:233
  69.8 1.6 %collective-permute-done.24.refs_3_ = bf16[80,768]{1,0:T(8,128)(2,1)S(1)} collective-permute-done((bf16[80,768]{1,0:T(8,128)(2,1)S(1)}, bf16[80,768]{1,0:T(8,128)(2,1)S(1)}, u32[]{:S(2)}, u32[]{:S(2)}) %collective-permute-start.24) | collective-permute-done | bytes 122912 | tf_op jit(solution)/shard_map/ppermute | solution.py:30
  71.4 2.4 %collective-permute-start.22 = (bf16[160,768]{1,0:T(8,128)(2,1)S(1)}, bf16[160,768]{1,0:T(8,128)(2,1)S(1)}, u32[]{:S(2)}, u32[]{:S(2)}) collective-permute-start(bf16[160,768]{1,0:T(8,128)(2,1)S(1)} %shard_map.83), channel_id=1, source_target_pairs={{193,0},{195,2},{197,4},{199,6},{201,8},{203,10},{205,12},{207,14}... | collective-permute-start | bytes 737288 | tf_op jit(solution)/shard_map/ppermute | solution.py:30
  74.0 3.5 %collective-permute-start.25 = (bf16[160,768]{1,0:T(8,128)(2,1)S(1)}, bf16[160,768]{1,0:T(8,128)(2,1)S(1)}, u32[]{:S(2)}, u32[]{:S(2)}) collective-permute-start(bf16[160,768]{1,0:T(8,128)(2,1)S(1)} %shard_map.87), channel_id=1, source_target_pairs={{129,0},{131,2},{133,4},{135,6},{137,8},{139,10},{141,12},{143,14}... | collective-permute-start | bytes 737288 | tf_op jit(solution)/shard_map/ppermute | solution.py:30
  77.5 0.2 collective-permute-done.15.refs_1_
  77.7 0.2 shard_map.80
  78.0 1.3 %collective-permute-start.18 = (bf16[80,768]{1,0:T(8,128)(2,1)S(1)}, bf16[80,768]{1,0:T(8,128)(2,1)S(1)}, u32[]{:S(2)}, u32[]{:S(2)}) collective-permute-start(bf16[80,768]{1,0:T(8,128)(2,1)S(1)} %get-tuple-element.64), channel_id=1, source_target_pairs={{6,0},{0,2},{2,4},{4,6},{14,8},{8,10},{10,12},{12,14},{22,16},{16,... | collective-permute-start | bytes 368648 | tf_op jit(solution)/shard_map/ppermute | solution.py:30
  79.3 1.1 %collective-permute-start.19 = (bf16[80,768]{1,0:T(8,128)(2,1)S(1)}, bf16[80,768]{1,0:T(8,128)(2,1)S(1)}, u32[]{:S(2)}, u32[]{:S(2)}) collective-permute-start(bf16[80,768]{1,0:T(8,128)(2,1)S(1)} %get-tuple-element.65), channel_id=1, source_target_pairs={{4,0},{6,2},{0,4},{2,6},{12,8},{14,10},{8,12},{10,14},{20,16},{22,... | collective-permute-start | bytes 368648 | tf_op jit(solution)/shard_map/ppermute | solution.py:30
  80.4 2.0 %collective-permute-start.20 = (bf16[80,768]{1,0:T(8,128)(2,1)S(1)}, bf16[80,768]{1,0:T(8,128)(2,1)S(1)}, u32[]{:S(2)}, u32[]{:S(2)}) collective-permute-start(bf16[80,768]{1,0:T(8,128)(2,1)S(1)} %get-tuple-element.66), channel_id=1, source_target_pairs={{2,0},{4,2},{6,4},{0,6},{10,8},{12,10},{14,12},{8,14},{18,16},{20,... | collective-permute-start | bytes 368648 | tf_op jit(solution)/shard_map/ppermute | solution.py:30
  82.4 2.7 %collective-permute-done.25.refs_2_ = bf16[160,768]{1,0:T(8,128)(2,1)S(1)} collective-permute-done((bf16[160,768]{1,0:T(8,128)(2,1)S(1)}, bf16[160,768]{1,0:T(8,128)(2,1)S(1)}, u32[]{:S(2)}, u32[]{:S(2)}) %collective-permute-start.25) | collective-permute-done | bytes 245792 | tf_op jit(solution)/shard_map/ppermute | solution.py:30
  85.2 6.5 %collective-permute-start.26 = (bf16[80,768]{1,0:T(8,128)(2,1)S(1)}, bf16[80,768]{1,0:T(8,128)(2,1)S(1)}, u32[]{:S(2)}, u32[]{:S(2)}) collective-permute-start(bf16[80,768]{1,0:T(8,128)(2,1)S(1)} %get-tuple-element.76), channel_id=1, source_target_pairs={{32,0},{34,2},{36,4},{38,6},{40,8},{42,10},{44,12},{46,14},{48,16}... | collective-permute-start | bytes 368648 | tf_op jit(solution)/shard_map/ppermute | solution.py:30
  91.7 0.9 shard_map.81
  92.7 0.9 shard_map.89
  (51 shorter events, 1.2 us)
Async XLA Ops:
  0.6 0.9 copy-start.2
  1.5 32.1 %copy-start.8 = (s32[2560]{0:T(1024)S(1)}, s32[2560]{0:T(1024)}, u32[]{:S(2)}) copy-start(s32[2560]{0:T(1024)} %param.6) | copy-start | bytes 30724
  1.7 4.2 %collective-permute-start.3 = (bf16[80,768]{1,0:T(8,128)(2,1)S(1)}, bf16[80,768]{1,0:T(8,128)(2,1)S(1)}, u32[]{:S(2)}, u32[]{:S(2)}) collective-permute-start(bf16[80,768]{1,0:T(8,128)(2,1)S(1)} %shard_map.69.refs_0_), channel_id=1, source_target_pairs={{32,0},{34,2},{36,4},{38,6},{40,8},{42,10},{44,12},{46,14},{48,16}... | collective-permute-start | bytes 368648 | tf_op jit(solution)/shard_map/ppermute | solution.py:30
  2.4 0.9 copy-start
  3.4 5.5 %collective-permute-start.2 = (bf16[80,768]{1,0:T(8,128)(2,1)S(1)}, bf16[80,768]{1,0:T(8,128)(2,1)S(1)}, u32[]{:S(2)}, u32[]{:S(2)}) collective-permute-start(bf16[80,768]{1,0:T(8,128)(2,1)S(1)} %shard_map.67.refs_0_), channel_id=1, source_target_pairs={{6,0},{0,2},{2,4},{4,6},{14,8},{8,10},{10,12},{12,14},{22,16},{16,... | collective-permute-start | bytes 368648 | tf_op jit(solution)/shard_map/ppermute | solution.py:30
  4.5 5.2 %collective-permute-start.1 = (bf16[80,768]{1,0:T(8,128)(2,1)S(1)}, bf16[80,768]{1,0:T(8,128)(2,1)S(1)}, u32[]{:S(2)}, u32[]{:S(2)}) collective-permute-start(bf16[80,768]{1,0:T(8,128)(2,1)S(1)} %shard_map.67.refs_0_), channel_id=1, source_target_pairs={{4,0},{6,2},{0,4},{2,6},{12,8},{14,10},{8,12},{10,14},{20,16},{22,... | collective-permute-start | bytes 368648 | tf_op jit(solution)/shard_map/ppermute | solution.py:30
  4.9 5.8 %collective-permute-start = (bf16[80,768]{1,0:T(8,128)(2,1)S(1)}, bf16[80,768]{1,0:T(8,128)(2,1)S(1)}, u32[]{:S(2)}, u32[]{:S(2)}) collective-permute-start(bf16[80,768]{1,0:T(8,128)(2,1)S(1)} %shard_map.67.refs_0_), channel_id=1, source_target_pairs={{2,0},{4,2},{6,4},{0,6},{10,8},{12,10},{14,12},{8,14},{18,16},{20,... | collective-permute-start | bytes 368648 | tf_op jit(solution)/shard_map/ppermute | solution.py:30
  5.8 11.5 %collective-permute-start.8 = (bf16[160,768]{1,0:T(8,128)(2,1)S(1)}, bf16[160,768]{1,0:T(8,128)(2,1)S(1)}, u32[]{:S(2)}, u32[]{:S(2)}) collective-permute-start(bf16[160,768]{1,0:T(8,128)(2,1)S(1)} %shard_map.70.refs_8_), channel_id=1, source_target_pairs={{128,0},{130,2},{132,4},{134,6},{136,8},{138,10},{140,12},{142,14}... | collective-permute-start | bytes 737288 | tf_op jit(solution)/shard_map/ppermute | solution.py:30
  10.7 20.9 %collective-permute-start.4 = (bf16[320,768]{1,0:T(8,128)(2,1)S(1)}, bf16[320,768]{1,0:T(8,128)(2,1)S(1)}, u32[]{:S(2)}, u32[]{:S(2)}) collective-permute-start(bf16[320,768]{1,0:T(8,128)(2,1)S(1)} %shard_map.68.refs_0_.refs_4_), channel_id=1, source_target_pairs={{8,0},{10,2},{12,4},{14,6},{16,8},{18,10},{20,12},{22,14},{24,16},... | collective-permute-start | bytes 1474568 | tf_op jit(solution)/shard_map/ppermute | solution.py:30
  13.0 8.5 %collective-permute-start.7 = (bf16[160,768]{1,0:T(8,128)(2,1)S(1)}, bf16[160,768]{1,0:T(8,128)(2,1)S(1)}, u32[]{:S(2)}, u32[]{:S(2)}) collective-permute-start(bf16[160,768]{1,0:T(8,128)(2,1)S(1)} %shard_map.70.refs_8_), channel_id=1, source_target_pairs={{64,0},{66,2},{68,4},{70,6},{72,8},{74,10},{76,12},{78,14},{80,16}... | collective-permute-start | bytes 737288 | tf_op jit(solution)/shard_map/ppermute | solution.py:30
  14.6 21.1 %collective-permute-start.6 = (bf16[320,768]{1,0:T(8,128)(2,1)S(1)}, bf16[320,768]{1,0:T(8,128)(2,1)S(1)}, u32[]{:S(2)}, u32[]{:S(2)}) collective-permute-start(bf16[320,768]{1,0:T(8,128)(2,1)S(1)} %shard_map.68.refs_0_.refs_4_), channel_id=1, source_target_pairs={{24,0},{26,2},{28,4},{30,6},{0,8},{2,10},{4,12},{6,14},{8,16},{10,... | collective-permute-start | bytes 1474568 | tf_op jit(solution)/shard_map/ppermute | solution.py:30
  17.4 14.3 %collective-permute-start.9 = (bf16[160,768]{1,0:T(8,128)(2,1)S(1)}, bf16[160,768]{1,0:T(8,128)(2,1)S(1)}, u32[]{:S(2)}, u32[]{:S(2)}) collective-permute-start(bf16[160,768]{1,0:T(8,128)(2,1)S(1)} %collective-permute-done.8.refs_0_.refs_10_), channel_id=1, source_target_pairs={{64,0},{66,2},{68,4},{70,6},{72,8},{74,10},{76,12},{78,14},{80,16}... | collective-permute-start | bytes 737288 | tf_op jit(solution)/shard_map/ppermute | solution.py:30
  17.5 8.7 %collective-permute-start.10 = (bf16[80,768]{1,0:T(8,128)(2,1)S(1)}, bf16[80,768]{1,0:T(8,128)(2,1)S(1)}, u32[]{:S(2)}, u32[]{:S(2)}) collective-permute-start(bf16[80,768]{1,0:T(8,128)(2,1)S(1)} %shard_map.72), channel_id=1, source_target_pairs={{128,0},{130,2},{132,4},{134,6},{136,8},{138,10},{140,12},{142,14}... | collective-permute-start | bytes 368648 | tf_op jit(solution)/shard_map/ppermute | solution.py:30
  21.5 14.2 %collective-permute-start.5 = (bf16[320,768]{1,0:T(8,128)(2,1)S(1)}, bf16[320,768]{1,0:T(8,128)(2,1)S(1)}, u32[]{:S(2)}, u32[]{:S(2)}) collective-permute-start(bf16[320,768]{1,0:T(8,128)(2,1)S(1)} %shard_map.68.refs_0_.refs_4_), channel_id=1, source_target_pairs={{16,0},{18,2},{20,4},{22,6},{24,8},{26,10},{28,12},{30,14},{0,16},... | collective-permute-start | bytes 1474568 | tf_op jit(solution)/shard_map/ppermute | solution.py:30
  26.2 5.9 %collective-permute-start.11 = (bf16[80,768]{1,0:T(8,128)(2,1)S(1)}, bf16[80,768]{1,0:T(8,128)(2,1)S(1)}, u32[]{:S(2)}, u32[]{:S(2)}) collective-permute-start(bf16[80,768]{1,0:T(8,128)(2,1)S(1)} %collective-permute-done.10.refs_0_), channel_id=1, source_target_pairs={{32,0},{34,2},{36,4},{38,6},{40,8},{42,10},{44,12},{46,14},{48,16}... | collective-permute-start | bytes 368648 | tf_op jit(solution)/shard_map/ppermute | solution.py:30
  31.0 0.6 copy-start.4
  31.6 4.1 %collective-permute-start.13 = (bf16[160,768]{1,0:T(8,128)(2,1)S(1)}, bf16[160,768]{1,0:T(8,128)(2,1)S(1)}, u32[]{:S(2)}, u32[]{:S(2)}) collective-permute-start(bf16[160,768]{1,0:T(8,128)(2,1)S(1)} %collective-permute-done.8.refs_0_.refs_10_), channel_id=1, source_target_pairs={{32,0},{34,2},{36,4},{38,6},{40,8},{42,10},{44,12},{46,14},{48,16}... | collective-permute-start | bytes 737288 | tf_op jit(solution)/shard_map/ppermute | solution.py:30
  31.6 4.2 %collective-permute-start.14 = (bf16[160,768]{1,0:T(8,128)(2,1)S(1)}, bf16[160,768]{1,0:T(8,128)(2,1)S(1)}, u32[]{:S(2)}, u32[]{:S(2)}) collective-permute-start(bf16[160,768]{1,0:T(8,128)(2,1)S(1)} %collective-permute-done.9.refs_11_), channel_id=1, source_target_pairs={{32,0},{34,2},{36,4},{38,6},{40,8},{42,10},{44,12},{46,14},{48,16}... | collective-permute-start | bytes 737288 | tf_op jit(solution)/shard_map/ppermute | solution.py:30
  32.1 0.6 copy-start.6
  32.8 3.0 %collective-permute-start.12 = (bf16[160,768]{1,0:T(8,128)(2,1)S(1)}, bf16[160,768]{1,0:T(8,128)(2,1)}, u32[]{:S(2)}, u32[]{:S(2)}) collective-permute-start(bf16[160,768]{1,0:T(8,128)(2,1)S(1)} %collective-permute-done.7.refs_9_), channel_id=1, source_target_pairs={{32,0},{34,2},{36,4},{38,6},{40,8},{42,10},{44,12},{46,14},{48,16}... | collective-permute-start | bytes 737288 | tf_op jit(solution)/shard_map/ppermute | solution.py:30
  33.9 0.9 copy-start.5
  34.8 0.9 copy-start.7
  56.6 7.9 %collective-permute-start.21 = (bf16[560,768]{1,0:T(8,128)(2,1)S(1)}, bf16[560,768]{1,0:T(8,128)(2,1)S(1)}, u32[]{:S(2)}, u32[]{:S(2)}) collective-permute-start(bf16[560,768]{1,0:T(8,128)(2,1)S(1)} %get-tuple-element.69), channel_id=1, source_target_pairs={{32,0},{34,2},{36,4},{38,6},{40,8},{42,10},{44,12},{46,14},{48,16}... | collective-permute-start | bytes 2580488 | tf_op jit(solution)/shard_map/ppermute | solution.py:30
  62.3 15.2 %collective-permute-start.17 = (bf16[320,768]{1,0:T(8,128)(2,1)S(1)}, bf16[320,768]{1,0:T(8,128)(2,1)S(1)}, u32[]{:S(2)}, u32[]{:S(2)}) collective-permute-start(bf16[320,768]{1,0:T(8,128)(2,1)S(1)} %shard_map.79), channel_id=1, source_target_pairs={{8,0},{10,2},{12,4},{14,6},{16,8},{18,10},{20,12},{22,14},{24,16},... | collective-permute-start | bytes 1474568 | tf_op jit(solution)/shard_map/ppermute | solution.py:30
  63.3 14.2 %collective-permute-start.16 = (bf16[320,768]{1,0:T(8,128)(2,1)S(1)}, bf16[320,768]{1,0:T(8,128)(2,1)S(1)}, u32[]{:S(2)}, u32[]{:S(2)}) collective-permute-start(bf16[320,768]{1,0:T(8,128)(2,1)S(1)} %shard_map.78), channel_id=1, source_target_pairs={{16,0},{18,2},{20,4},{22,6},{24,8},{26,10},{28,12},{30,14},{0,16},... | collective-permute-start | bytes 1474568 | tf_op jit(solution)/shard_map/ppermute | solution.py:30
  64.4 13.4 %collective-permute-start.15 = (bf16[320,768]{1,0:T(8,128)(2,1)S(1)}, bf16[320,768]{1,0:T(8,128)(2,1)S(1)}, u32[]{:S(2)}, u32[]{:S(2)}) collective-permute-start(bf16[320,768]{1,0:T(8,128)(2,1)S(1)} %shard_map.77), channel_id=1, source_target_pairs={{24,0},{26,2},{28,4},{30,6},{0,8},{2,10},{4,12},{6,14},{8,16},{10,... | collective-permute-start | bytes 1474568 | tf_op jit(solution)/shard_map/ppermute | solution.py:30
  64.5 9.3 %collective-permute-start.23 = (bf16[160,768]{1,0:T(8,128)(2,1)S(1)}, bf16[160,768]{1,0:T(8,128)(2,1)S(1)}, u32[]{:S(2)}, u32[]{:S(2)}) collective-permute-start(bf16[160,768]{1,0:T(8,128)(2,1)S(1)} %shard_map.84), channel_id=1, source_target_pairs={{193,0},{195,2},{197,4},{199,6},{201,8},{203,10},{205,12},{207,14}... | collective-permute-start | bytes 737288 | tf_op jit(solution)/shard_map/ppermute | solution.py:30
  64.6 6.8 %collective-permute-start.24 = (bf16[80,768]{1,0:T(8,128)(2,1)S(1)}, bf16[80,768]{1,0:T(8,128)(2,1)S(1)}, u32[]{:S(2)}, u32[]{:S(2)}) collective-permute-start(bf16[80,768]{1,0:T(8,128)(2,1)S(1)} %shard_map.85), channel_id=1, source_target_pairs={{129,0},{131,2},{133,4},{135,6},{137,8},{139,10},{141,12},{143,14}... | collective-permute-start | bytes 368648 | tf_op jit(solution)/shard_map/ppermute | solution.py:30
  71.4 11.0 %collective-permute-start.22 = (bf16[160,768]{1,0:T(8,128)(2,1)S(1)}, bf16[160,768]{1,0:T(8,128)(2,1)S(1)}, u32[]{:S(2)}, u32[]{:S(2)}) collective-permute-start(bf16[160,768]{1,0:T(8,128)(2,1)S(1)} %shard_map.83), channel_id=1, source_target_pairs={{193,0},{195,2},{197,4},{199,6},{201,8},{203,10},{205,12},{207,14}... | collective-permute-start | bytes 737288 | tf_op jit(solution)/shard_map/ppermute | solution.py:30
  73.9 17.8 %copy-start.1 = (bf16[80,768]{1,0:T(8,128)(2,1)S(1)}, bf16[80,768]{1,0:T(8,128)(2,1)}, u32[]{:S(2)}) copy-start(bf16[80,768]{1,0:T(8,128)(2,1)} %src.6) | copy-start | bytes 368644
  73.9 18.8 %copy-start.3 = (bf16[80,768]{1,0:T(8,128)(2,1)S(1)}, bf16[80,768]{1,0:T(8,128)(2,1)}, u32[]{:S(2)}) copy-start(bf16[80,768]{1,0:T(8,128)(2,1)} %src.7) | copy-start | bytes 368644
  74.0 11.2 %collective-permute-start.25 = (bf16[160,768]{1,0:T(8,128)(2,1)S(1)}, bf16[160,768]{1,0:T(8,128)(2,1)S(1)}, u32[]{:S(2)}, u32[]{:S(2)}) collective-permute-start(bf16[160,768]{1,0:T(8,128)(2,1)S(1)} %shard_map.87), channel_id=1, source_target_pairs={{129,0},{131,2},{133,4},{135,6},{137,8},{139,10},{141,12},{143,14}... | collective-permute-start | bytes 737288 | tf_op jit(solution)/shard_map/ppermute | solution.py:30
  78.0 13.7 %collective-permute-start.18 = (bf16[80,768]{1,0:T(8,128)(2,1)S(1)}, bf16[80,768]{1,0:T(8,128)(2,1)S(1)}, u32[]{:S(2)}, u32[]{:S(2)}) collective-permute-start(bf16[80,768]{1,0:T(8,128)(2,1)S(1)} %get-tuple-element.64), channel_id=1, source_target_pairs={{6,0},{0,2},{2,4},{4,6},{14,8},{8,10},{10,12},{12,14},{22,16},{16,... | collective-permute-start | bytes 368648 | tf_op jit(solution)/shard_map/ppermute | solution.py:30
  79.3 12.4 %collective-permute-start.19 = (bf16[80,768]{1,0:T(8,128)(2,1)S(1)}, bf16[80,768]{1,0:T(8,128)(2,1)S(1)}, u32[]{:S(2)}, u32[]{:S(2)}) collective-permute-start(bf16[80,768]{1,0:T(8,128)(2,1)S(1)} %get-tuple-element.65), channel_id=1, source_target_pairs={{4,0},{6,2},{0,4},{2,6},{12,8},{14,10},{8,12},{10,14},{20,16},{22,... | collective-permute-start | bytes 368648 | tf_op jit(solution)/shard_map/ppermute | solution.py:30
  80.4 11.3 %collective-permute-start.20 = (bf16[80,768]{1,0:T(8,128)(2,1)S(1)}, bf16[80,768]{1,0:T(8,128)(2,1)S(1)}, u32[]{:S(2)}, u32[]{:S(2)}) collective-permute-start(bf16[80,768]{1,0:T(8,128)(2,1)S(1)} %get-tuple-element.66), channel_id=1, source_target_pairs={{2,0},{4,2},{6,4},{0,6},{10,8},{12,10},{14,12},{8,14},{18,16},{20,... | collective-permute-start | bytes 368648 | tf_op jit(solution)/shard_map/ppermute | solution.py:30
  85.2 7.5 %collective-permute-start.26 = (bf16[80,768]{1,0:T(8,128)(2,1)S(1)}, bf16[80,768]{1,0:T(8,128)(2,1)S(1)}, u32[]{:S(2)}, u32[]{:S(2)}) collective-permute-start(bf16[80,768]{1,0:T(8,128)(2,1)S(1)} %get-tuple-element.76), channel_id=1, source_target_pairs={{32,0},{34,2},{36,4},{38,6},{40,8},{42,10},{44,12},{46,14},{48,16}... | collective-permute-start | bytes 368648 | tf_op jit(solution)/shard_map/ppermute | solution.py:30
